TPU v7x, 32 devices: a whole 2x2x4 slice. The times are simulated.
32 devices in a mesh: fsdp: 16 (over z, y, x), tensor: 2 (over core).
Axes of the slice: x: 2, y: 2, z: 4, core: 2. Of those that a mesh axis runs over, the one named last changes fastest.
Arguments:
- layer_input: bfloat16 [16384, 1024], P(('fsdp', 'tensor')), may hold values from -6 to 6
- doc_ids: int32 [16, 1024], P('fsdp'), may hold values from 0 to 3, never falling along the last dimension, each value on 1 to 768 neighbouring positions
- input_gain: float32 [1024], replicated, may hold values from 0.1 to 1.9
- mixer_weight: float32 [1024, 2, 1536], P('fsdp', None, 'tensor'), may hold values from -0.1875 to 0.1875
- state_weight: float32 [1024, 256], P('fsdp'), may hold values from -0.1875 to 0.1875
- step_weight: float32 [1024, 24], P('fsdp', 'tensor'), may hold values from -0.1875 to 0.1875
- conv_weight: float32 [4, 1536], P(None, 'tensor'), may hold values from -3 to 3
- conv_bias: float32 [1536], P('tensor'), may hold values from -3 to 3
- state_conv: float32 [4, 256], replicated, may hold values from -3 to 3
- state_conv_bias: float32 [256], replicated, may hold values from -3 to 3
- step_bias: float32 [24], P('tensor'), may hold values from -5 to -1
- decay_log: float32 [24], P('tensor'), may hold values from -1 to 2
- skip_gain: float32 [24], P('tensor'), may hold values from 0.5 to 1.5
- mixer_gain: float32 [1536], P('tensor'), may hold values from 0.1 to 1.9
- mixer_proj: float32 [1536, 1024], P('tensor', 'fsdp'), may hold values from -0.15625 to 0.15625
- query_weight: float32 [1024, 512], P('fsdp', 'tensor'), may hold values from -0.1875 to 0.1875
- keyval_projection: float32 [1024, 2, 128], P('fsdp'), may hold values from -0.1875 to 0.1875
- attention_proj: float32 [512, 1024], P('tensor', 'fsdp'), may hold values from -1.5 to 1.5
- second_gain: float32 [1024], replicated, may hold values from 0.1 to 1.9
- gate_up: float32 [1024, 2, 2048], P('fsdp', None, 'tensor'), may hold values from -0.1875 to 0.1875
- down_proj: float32 [2048, 1024], P('tensor', 'fsdp'), may hold values from -0.125 to 0.125
- cotangent: bfloat16 [16384, 1024], P(('fsdp', 'tensor')), may hold values from -6 to 6
Outputs:
- layer_output: bfloat16 [16384, 1024], P(('fsdp', 'tensor'))
- input_grad: float32 [16384, 1024], P(('fsdp', 'tensor'))
- grad_input_gain: float32 [1024], replicated
- grad_mixer_weight: float32 [1024, 2, 1536], P('fsdp', None, 'tensor')
- grad_state_weight: float32 [1024, 256], P('fsdp')
- grad_step_weight: float32 [1024, 24], P('fsdp', 'tensor')
- grad_conv_weight: float32 [4, 1536], P(None, 'tensor')
- grad_conv_bias: float32 [1536], P('tensor')
- grad_state_conv: float32 [4, 256], replicated
- grad_state_conv_bias: float32 [256], replicated
- grad_step_bias: float32 [24], P('tensor')
- grad_decay_log: float32 [24], P('tensor')
- grad_skip_gain: float32 [24], P('tensor')
- grad_mixer_gain: float32 [1536], P('tensor')
- grad_mixer_proj: float32 [1536, 1024], P('tensor', 'fsdp')
- grad_query_weight: float32 [1024, 512], P('fsdp', 'tensor')
- grad_keyval_weight: float32 [1024, 2, 128], P('fsdp')
- grad_attention_proj: float32 [512, 1024], P('tensor', 'fsdp')
- grad_second_gain: float32 [1024], replicated
- grad_gate_up: float32 [1024, 2, 2048], P('fsdp', None, 'tensor')
- grad_down_proj: float32 [2048, 1024], P('tensor', 'fsdp')
Inputs may be any that keep to these rules, and one draw needn't show every extreme that they name: `doc_ids`: in each row the document numbers start at 0, never fall and step by one; no document has more than 768 tokens, and some document has exactly that many.
All inputs are finite; a program needn't handle non-finite values.
Results may differ from a plain program's by a relative error of at most 0.02.
Values may be sent and summed in bfloat16 or wider, within the bound.
A program may use at most 256 MiB of HBM per device.

v0:
```python
import math

import jax
import jax.numpy as jnp
from jax import lax
from jax.sharding import PartitionSpec as P

QUERY_HEADS = 8
KEYVAL_HEADS = 2
HEAD_SIZE = 64
SSD_BLOCK = 128
DSSM = 1536


EPS = 1e-05
THETA = 100000000000.0
MASKED = -1e30


def left_dot(left_side, right_side, precision=None):
    return lax.dot_general(
        left_side,
        right_side,
        (((0,), (0,)), ((), ())),
        precision=precision,
        preferred_element_type=jnp.float32,
    )


def right_dot(left_side, right_side, precision=None):
    return lax.dot_general(
        left_side,
        right_side,
        (((1,), (1,)), ((), ())),
        precision=precision,
        preferred_element_type=jnp.float32,
    )


def plain_dot(left_side, right_side):
    return jnp.dot(left_side, right_side, preferred_element_type=jnp.float32)


def norm_scale(values):
    return lax.rsqrt(jnp.mean(values * values, axis=-1, keepdims=True) + EPS)


def norm_grads(values, scales, gains, upstream):
    weighted = upstream * gains
    through = scales * weighted - values * scales**3 * jnp.mean(
        weighted * values, axis=-1, keepdims=True
    )
    return (through, jnp.sum(upstream * values * scales, axis=0))


def positions(segments):
    length = segments.shape[-1]
    position_table = jnp.arange(length, dtype=jnp.int32)
    change = jnp.concatenate(
        [jnp.ones(segments.shape[:-1] + (1,), jnp.bool_), segments[..., 1:] != segments[..., :-1]],
        axis=-1,
    )
    starts = jnp.where(change, position_table, jnp.zeros_like(position_table))
    begins = lax.cummax(starts, axis=segments.ndim - 1)
    return (position_table - begins).astype(jnp.float32)


def apply_rotation(values, position_table, direction):
    half_width = values.shape[-1] // 2
    frequencies = jnp.exp(
        jnp.arange(half_width, dtype=jnp.float32) * (-2.0 * math.log(THETA) / values.shape[-1])
    )
    angles = position_table[:, None] * frequencies[None, :]
    cosine = jnp.cos(angles)[:, None, :]
    sine_part = direction * jnp.sin(angles)[:, None, :]
    front_half = values[..., :half_width]
    rear_half = values[..., half_width:]
    return jnp.concatenate(
        [front_half * cosine - rear_half * sine_part, rear_half * cosine + front_half * sine_part],
        axis=-1,
    )


def causal_conv(values, segments, kernel, biases):
    kernel_taps = kernel.shape[0]
    result = values * kernel[kernel_taps - 1] + biases
    for offset in range(1, kernel_taps):
        earlier = jnp.concatenate(
            [jnp.zeros((offset, values.shape[1]), jnp.float32), values[:-offset]], axis=0
        )
        same_doc = jnp.concatenate(
            [jnp.zeros((offset,), jnp.bool_), segments[offset:] == segments[:-offset]], axis=0
        )
        result = (
            result + jnp.where(same_doc[:, None], earlier, 0.0) * kernel[kernel_taps - 1 - offset]
        )
    return result


def state_scan(inputs, state_in, state_out, step_sizes, decay_rates, segments, block_len):
    length, head_count, channels = inputs.shape
    states = state_in.shape[1]
    blocks = length // block_len
    highest = lax.Precision.HIGHEST

    def advance(carry, pieces):
        memory, before = carry
        values, keys_in, read_keys, widths, labels = pieces
        log_decay = jnp.cumsum(widths * decay_rates[None, :], axis=0)
        position_table = jnp.arange(block_len, dtype=jnp.int32)
        allowed = (labels[:, None] == labels[None, :]) & (
            position_table[:, None] >= position_table[None, :]
        )
        log_gaps = jnp.where(
            allowed[:, :, None], log_decay[:, None, :] - log_decay[None, :, :], 0.0
        )
        decays = jnp.where(allowed[:, :, None], jnp.exp(log_gaps), 0.0)
        intersection = jnp.dot(
            read_keys, keys_in.T, precision=highest, preferred_element_type=jnp.float32
        )
        scaled = widths[:, :, None] * values
        within = jnp.einsum(
            "tsh,shp->thp", intersection[:, :, None] * decays, scaled, precision=highest
        )
        carried_on = (labels == before).astype(jnp.float32)
        carried = (
            jnp.einsum("tn,hpn->thp", read_keys, memory, precision=highest)
            * (jnp.exp(log_decay) * carried_on[:, None])[:, :, None]
        )
        tail_decay = jnp.where(
            (labels == labels[-1])[:, None], jnp.exp(log_decay[-1][None, :] - log_decay), 0.0
        )
        memory = memory * (jnp.exp(log_decay[-1]) * carried_on[-1])[:, None, None] + jnp.einsum(
            "sh,shp,sn->hpn", tail_decay, scaled, keys_in, precision=highest
        )
        return ((memory, labels[-1]), within + carried)

    initial = (jnp.zeros((head_count, channels, states), jnp.float32), jnp.int32(-1))
    pieces = (
        inputs.reshape(blocks, block_len, head_count, channels),
        state_in.reshape(blocks, block_len, states),
        state_out.reshape(blocks, block_len, states),
        step_sizes.reshape(blocks, block_len, head_count),
        segments.reshape(blocks, block_len),
    )
    outputs = lax.scan(jax.checkpoint(advance), initial, pieces)[1]
    return outputs.reshape(length, head_count, channels)


def mamba_mixer(
    mixed_x,
    state_proj,
    step_raw,
    gate_z,
    segments,
    conv_weight,
    conv_bias,
    state_conv,
    state_conv_bias,
    step_bias,
    decay_log,
    skip_gain,
    block_len,
):
    total_rows = mixed_x.shape[0]
    head_count = step_raw.shape[1]
    conv_values = jax.nn.silu(causal_conv(mixed_x, segments, conv_weight, conv_bias))
    conv_state = jax.nn.silu(causal_conv(state_proj, segments, state_conv, state_conv_bias))
    half_width = conv_state.shape[1] // 2
    step_sizes = jax.nn.softplus(step_raw + step_bias)
    decay_rates = -jnp.exp(decay_log)
    values = conv_values.reshape(total_rows, head_count, -1)
    scanned = state_scan(
        values,
        conv_state[:, :half_width],
        conv_state[:, half_width:],
        step_sizes,
        decay_rates,
        segments,
        block_len,
    )
    scanned = scanned + skip_gain[None, :, None] * values
    return scanned.reshape(total_rows, -1) * jax.nn.silu(gate_z)


def allowed_mask(segments):
    position_table = jnp.arange(segments.shape[0], dtype=jnp.int32)
    return (segments[:, None] == segments[None, :]) & (
        position_table[:, None] >= position_table[None, :]
    )


def attention_rows(pieces):
    query_rot, key_rotated, value_reduced, segments = pieces
    expand_heads = query_rot.shape[1] // key_rotated.shape[1]
    key_complete = jnp.repeat(key_rotated, expand_heads, axis=1)
    value_complete = jnp.repeat(value_reduced, expand_heads, axis=1)
    scores = jnp.einsum(
        "qhd,khd->hqk", query_rot, key_complete, preferred_element_type=jnp.float32
    ) * query_rot.shape[2] ** (-0.5)
    scores = jnp.where(allowed_mask(segments)[None], scores, MASKED)
    maxima = jnp.max(scores, axis=-1, keepdims=True)
    exponent = jnp.exp(scores - maxima)
    totals = jnp.sum(exponent, axis=-1, keepdims=True)
    probabilities = exponent / totals
    attended = jnp.einsum(
        "hqk,khd->qhd",
        probabilities.astype(jnp.bfloat16),
        value_complete,
        preferred_element_type=jnp.float32,
    )
    return (attended.astype(jnp.bfloat16), (maxima + jnp.log(totals))[..., 0])


def attention_grads(pieces):
    query_rot, key_rotated, value_reduced, segments, log_sums, upstream = pieces
    expand_heads = query_rot.shape[1] // key_rotated.shape[1]
    factor = query_rot.shape[2] ** (-0.5)
    key_complete = jnp.repeat(key_rotated, expand_heads, axis=1)
    value_complete = jnp.repeat(value_reduced, expand_heads, axis=1)
    scores = (
        jnp.einsum("qhd,khd->hqk", query_rot, key_complete, preferred_element_type=jnp.float32)
        * factor
    )
    scores = jnp.where(allowed_mask(segments)[None], scores, MASKED)
    probabilities = jnp.exp(scores - log_sums[..., None])
    prob_grads = jnp.einsum(
        "qhd,khd->hqk", upstream, value_complete, preferred_element_type=jnp.float32
    )
    centre = jnp.sum(probabilities * prob_grads, axis=-1, keepdims=True)
    score_grads = (probabilities * (prob_grads - centre)).astype(jnp.bfloat16)
    query_grads = (
        jnp.einsum("hqk,khd->qhd", score_grads, key_complete, preferred_element_type=jnp.float32)
        * factor
    )
    key_grads = (
        jnp.einsum("hqk,qhd->khd", score_grads, query_rot, preferred_element_type=jnp.float32)
        * factor
    )
    value_grads = jnp.einsum(
        "hqk,qhd->khd",
        probabilities.astype(jnp.bfloat16),
        upstream,
        preferred_element_type=jnp.float32,
    )
    length = key_rotated.shape[0]
    kv_heads = key_rotated.shape[1]
    key_grads = jnp.sum(key_grads.reshape(length, kv_heads, expand_heads, -1), axis=2)
    value_grads = jnp.sum(value_grads.reshape(length, kv_heads, expand_heads, -1), axis=2)
    return (query_grads, key_grads, value_grads)


def send_ffn(gate_up_grad, down_grad):
    return (
        lax.psum_scatter(
            gate_up_grad.astype(jnp.bfloat16), "fsdp", scatter_dimension=0, tiled=True
        ).astype(jnp.float32),
        lax.psum_scatter(
            down_grad.astype(jnp.bfloat16), "fsdp", scatter_dimension=1, tiled=True
        ).astype(jnp.float32),
    )


def send_mixer(mixer_grad, step_grad, query_grad, proj_grad, attention_grad):
    return (
        lax.psum_scatter(
            mixer_grad.astype(jnp.bfloat16), "fsdp", scatter_dimension=0, tiled=True
        ).astype(jnp.float32),
        lax.psum_scatter(
            step_grad.astype(jnp.bfloat16), "fsdp", scatter_dimension=0, tiled=True
        ).astype(jnp.float32),
        lax.psum_scatter(
            query_grad.astype(jnp.bfloat16), "fsdp", scatter_dimension=0, tiled=True
        ).astype(jnp.float32),
        lax.psum_scatter(
            proj_grad.astype(jnp.bfloat16), "fsdp", scatter_dimension=1, tiled=True
        ).astype(jnp.float32),
        lax.psum_scatter(
            attention_grad.astype(jnp.bfloat16), "fsdp", scatter_dimension=1, tiled=True
        ).astype(jnp.float32),
    )


def body(
    layer_input,
    doc_ids,
    input_gain,
    mixer_weight,
    state_weight,
    step_weight,
    conv_weight,
    conv_bias,
    state_conv,
    state_conv_bias,
    step_bias,
    decay_log,
    skip_gain,
    mixer_gain,
    mixer_proj,
    query_weight,
    keyval_projection,
    attention_proj,
    second_gain,
    gate_up,
    down_proj,
    cotangent,
):
    tensor_count = lax.axis_size("tensor")
    tensor_index = lax.axis_index("tensor")
    fsdp_index = lax.axis_index("fsdp")
    hidden_width = layer_input.shape[1]
    shard_rows = state_weight.shape[0]
    seq_count, seq_length = doc_ids.shape
    group_rows = seq_count * seq_length
    query_heads = query_weight.shape[1] // HEAD_SIZE
    queries_per_group = QUERY_HEADS // KEYVAL_HEADS
    kv_heads = max(1, query_heads // queries_per_group)
    keyval_leading = tensor_index * query_heads // queries_per_group
    ssm_width = conv_weight.shape[1]
    ffn_width = down_proj.shape[0]
    highest = lax.Precision.HIGHEST
    (
        full_mixer,
        full_state,
        full_step,
        full_query,
        full_keyval,
        full_gate_up,
        full_mixer_proj,
        full_attention_proj,
        full_down,
    ) = (
        lax.all_gather(mixer_weight.astype(jnp.bfloat16), "fsdp", axis=0, tiled=True),
        lax.all_gather(state_weight.astype(jnp.bfloat16), "fsdp", axis=0, tiled=True),
        lax.all_gather(step_weight.astype(jnp.bfloat16), "fsdp", axis=0, tiled=True),
        lax.all_gather(query_weight.astype(jnp.bfloat16), "fsdp", axis=0, tiled=True),
        lax.all_gather(keyval_projection.astype(jnp.bfloat16), "fsdp", axis=0, tiled=True),
        lax.all_gather(gate_up.astype(jnp.bfloat16), "fsdp", axis=0, tiled=True),
        lax.all_gather(mixer_proj.astype(jnp.bfloat16), "fsdp", axis=1, tiled=True),
        lax.all_gather(attention_proj.astype(jnp.bfloat16), "fsdp", axis=1, tiled=True),
        lax.all_gather(down_proj.astype(jnp.bfloat16), "fsdp", axis=1, tiled=True),
    )
    mixer_matrix = full_mixer.reshape(hidden_width, 2 * ssm_width)
    keyval_matrix = lax.dynamic_slice_in_dim(
        full_keyval, keyval_leading * HEAD_SIZE, kv_heads * HEAD_SIZE, 2
    ).reshape(hidden_width, 2 * kv_heads * HEAD_SIZE)
    gate_up_matrix = full_gate_up.reshape(hidden_width, 2 * ffn_width)
    seq_offsets = jnp.arange(seq_count, dtype=jnp.int32)[:, None] * seq_length
    flat_docs = (doc_ids + seq_offsets).reshape(group_rows)
    position_table = positions(doc_ids).reshape(group_rows)
    tokens_float = layer_input.astype(jnp.float32)
    first_scale = norm_scale(tokens_float)
    normalized_input = (tokens_float * first_scale * input_gain).astype(jnp.bfloat16)
    normed_group = lax.all_gather(normalized_input, "tensor", axis=0, tiled=True)
    mixer_in = plain_dot(normed_group, mixer_matrix)
    gate_z = mixer_in[:, :ssm_width]
    mixed_x = mixer_in[:, ssm_width:]
    state_proj = plain_dot(normed_group, full_state)
    step_raw = plain_dot(normed_group, full_step)
    queries = plain_dot(normed_group, full_query)
    keyval_rows = plain_dot(normed_group, keyval_matrix)

    def mixer_local(
        x_part,
        state_part,
        step_part,
        gate_part,
        taps_x,
        bias_x,
        taps_state,
        bias_state,
        bias_step,
        rate_log,
        skip_part,
    ):
        return mamba_mixer(
            x_part,
            state_part,
            step_part,
            gate_part,
            flat_docs,
            taps_x,
            bias_x,
            taps_state,
            bias_state,
            bias_step,
            rate_log,
            skip_part,
            SSD_BLOCK,
        )

    gated_out, mixer_pull = jax.vjp(
        mixer_local,
        mixed_x,
        state_proj,
        step_raw,
        gate_z,
        conv_weight,
        conv_bias,
        state_conv,
        state_conv_bias,
        step_bias,
        decay_log,
        skip_gain,
    )
    squares = lax.psum(jnp.sum(gated_out * gated_out, axis=-1), "tensor")
    gated_scale = lax.rsqrt(squares / DSSM + EPS)[:, None]
    mixed_norm = (gated_out * gated_scale * mixer_gain).astype(jnp.bfloat16)
    query_rot = apply_rotation(
        queries.reshape(group_rows, query_heads, HEAD_SIZE), position_table, 1.0
    ).astype(jnp.bfloat16)
    key_rotated = apply_rotation(
        keyval_rows[:, : kv_heads * HEAD_SIZE].reshape(group_rows, kv_heads, HEAD_SIZE),
        position_table,
        1.0,
    ).astype(jnp.bfloat16)
    value_reduced = (
        keyval_rows[:, kv_heads * HEAD_SIZE :]
        .reshape(group_rows, kv_heads, HEAD_SIZE)
        .astype(jnp.bfloat16)
    )
    query_seq = query_rot.reshape(seq_count, seq_length, query_heads, HEAD_SIZE)
    key_seq = key_rotated.reshape(seq_count, seq_length, kv_heads, HEAD_SIZE)
    value_seq = value_reduced.reshape(seq_count, seq_length, kv_heads, HEAD_SIZE)
    attended_seq, log_sums = lax.map(attention_rows, (query_seq, key_seq, value_seq, doc_ids))
    attended = attended_seq.reshape(group_rows, query_heads * HEAD_SIZE)
    branch_part = plain_dot(mixed_norm, full_mixer_proj) + plain_dot(attended, full_attention_proj)
    branch = lax.psum_scatter(branch_part, "tensor", scatter_dimension=0, tiled=True)
    middle = tokens_float + branch
    second_scale = norm_scale(middle)
    second = (middle * second_scale * second_gain).astype(jnp.bfloat16)
    second_group = lax.all_gather(second, "tensor", axis=0, tiled=True)
    gate_vals = plain_dot(second_group, gate_up_matrix)
    gate_part = gate_vals[:, :ffn_width]
    up_part = gate_vals[:, ffn_width:]
    active = (jax.nn.silu(gate_part) * up_part).astype(jnp.bfloat16)
    ffn_out = lax.psum_scatter(
        plain_dot(active, full_down).astype(jnp.bfloat16), "tensor", scatter_dimension=0, tiled=True
    ).astype(jnp.float32)
    layer_output = (middle + ffn_out).astype(jnp.bfloat16)
    upstream = cotangent.astype(jnp.float32)
    upstream_group = lax.all_gather(cotangent, "tensor", axis=0, tiled=True)
    grad_down = left_dot(active, upstream_group)
    active_grad = right_dot(upstream_group, full_down)
    sigmoid_gate = jax.nn.sigmoid(gate_part)
    gate_grad = active_grad * up_part * sigmoid_gate * (1.0 + gate_part * (1.0 - sigmoid_gate))
    up_grad = active_grad * gate_part * sigmoid_gate
    gate_up_grad = jnp.concatenate([gate_grad, up_grad], axis=-1).astype(jnp.bfloat16)
    grad_gate_up_full = left_dot(second_group, gate_up_grad).reshape(hidden_width, 2, ffn_width)
    second_part = right_dot(gate_up_grad, gate_up_matrix)
    second_grad = lax.psum_scatter(second_part, "tensor", scatter_dimension=0, tiled=True)
    middle_back, second_gain_part = norm_grads(middle, second_scale, second_gain, second_grad)
    middle_grad = upstream + middle_back
    branch_group = lax.all_gather(middle_grad.astype(jnp.bfloat16), "tensor", axis=0, tiled=True)
    grad_mixer_proj_full = left_dot(mixed_norm, branch_group)
    grad_attention_full = left_dot(attended, branch_group)
    norm_grad = right_dot(branch_group, full_mixer_proj)
    attended_grad = right_dot(branch_group, full_attention_proj).astype(jnp.bfloat16)
    mixer_gain_part = jnp.sum(norm_grad * gated_out * gated_scale, axis=0)
    weighted = norm_grad * mixer_gain
    inner_sums = lax.psum(jnp.sum(weighted * gated_out, axis=-1), "tensor")
    gated_grad = gated_scale * weighted - gated_out * gated_scale**3 * (inner_sums / DSSM)[:, None]
    (
        x_grad,
        state_grad,
        step_grad,
        gate_z_grad,
        conv_weight_part,
        conv_bias_part,
        state_conv_part,
        state_bias_part,
        step_bias_part,
        decay_part,
        skip_part,
    ) = mixer_pull(gated_grad)
    upstream_seq = attended_grad.reshape(seq_count, seq_length, query_heads, HEAD_SIZE)
    query_grad_seq, key_grad_seq, value_grad_seq = lax.map(
        attention_grads, (query_seq, key_seq, value_seq, doc_ids, log_sums, upstream_seq)
    )
    query_grad = (
        apply_rotation(
            query_grad_seq.reshape(group_rows, query_heads, HEAD_SIZE), position_table, -1.0
        )
        .reshape(group_rows, query_heads * HEAD_SIZE)
        .astype(jnp.bfloat16)
    )
    key_grad = apply_rotation(
        key_grad_seq.reshape(group_rows, kv_heads, HEAD_SIZE), position_table, -1.0
    ).reshape(group_rows, kv_heads * HEAD_SIZE)
    value_grad = value_grad_seq.reshape(group_rows, kv_heads * HEAD_SIZE)
    mixer_grad = jnp.concatenate([gate_z_grad, x_grad], axis=-1).astype(jnp.bfloat16)
    step_low = step_grad.astype(jnp.bfloat16)
    shared_rows = jnp.concatenate([state_grad, key_grad, value_grad], axis=-1)
    shared_matrix = jnp.concatenate([full_state, keyval_matrix], axis=-1).astype(jnp.float32)
    grad_mixer_full = left_dot(normed_group, mixer_grad).reshape(hidden_width, 2, ssm_width)
    grad_step_full = left_dot(normed_group, step_low)
    grad_query_full = left_dot(normed_group, query_grad)
    grad_shared = left_dot(normed_group.astype(jnp.float32), shared_rows, highest)
    normed_part = (
        right_dot(mixer_grad, mixer_matrix)
        + right_dot(step_low, full_step)
        + right_dot(query_grad, full_query)
        + right_dot(shared_rows, shared_matrix, highest)
    )
    normed_grad = lax.psum_scatter(
        normed_part.astype(jnp.bfloat16), "tensor", scatter_dimension=0, tiled=True
    ).astype(jnp.float32)
    input_back, input_gain_part = norm_grads(tokens_float, first_scale, input_gain, normed_grad)
    input_grad = middle_grad + input_back
    ffn_grads = send_ffn(grad_gate_up_full, grad_down)
    mixer_grads = send_mixer(
        grad_mixer_full, grad_step_full, grad_query_full, grad_mixer_proj_full, grad_attention_full
    )

    def spread(values, along):
        shape = list(values.shape)
        shape[along] = shape[along] * tensor_count
        return lax.dynamic_update_slice_in_dim(
            jnp.zeros(shape, jnp.float32), values, tensor_index * values.shape[along], along
        )

    def own_part(values, size, along):
        return lax.dynamic_slice_in_dim(values, tensor_index * size, size, along)

    state_cols = full_state.shape[1]
    keyval_slice = grad_shared[:, state_cols:].reshape(hidden_width, 2, kv_heads * HEAD_SIZE)
    keyval_full = lax.dynamic_update_slice_in_dim(
        jnp.zeros((hidden_width, 2, KEYVAL_HEADS * HEAD_SIZE), jnp.float32),
        keyval_slice,
        keyval_leading * HEAD_SIZE,
        2,
    )
    (
        state_sum,
        keyval_sum,
        state_conv_sum,
        state_bias_sum,
        input_gain_sum,
        second_gain_sum,
        conv_weight_sum,
        conv_bias_sum,
        step_bias_sum,
        decay_sum,
        skip_sum,
        mixer_gain_sum,
    ) = lax.psum(
        (
            grad_shared[:, :state_cols],
            keyval_full,
            state_conv_part,
            state_bias_part,
            input_gain_part,
            second_gain_part,
            spread(conv_weight_part, 1),
            spread(conv_bias_part, 0),
            spread(step_bias_part, 0),
            spread(decay_part, 0),
            spread(skip_part, 0),
            spread(mixer_gain_part, 0),
        ),
        ("fsdp", "tensor"),
    )
    heads_local = step_bias.shape[0]
    grad_state_weight = lax.dynamic_slice_in_dim(state_sum, fsdp_index * shard_rows, shard_rows, 0)
    grad_keyval_weight = lax.dynamic_slice_in_dim(
        keyval_sum, fsdp_index * shard_rows, shard_rows, 0
    )
    return (
        layer_output,
        input_grad,
        input_gain_sum,
        mixer_grads[0],
        grad_state_weight,
        mixer_grads[1],
        own_part(conv_weight_sum, ssm_width, 1),
        own_part(conv_bias_sum, ssm_width, 0),
        state_conv_sum,
        state_bias_sum,
        own_part(step_bias_sum, heads_local, 0),
        own_part(decay_sum, heads_local, 0),
        own_part(skip_sum, heads_local, 0),
        own_part(mixer_gain_sum, ssm_width, 0),
        mixer_grads[3],
        mixer_grads[2],
        grad_keyval_weight,
        mixer_grads[4],
        second_gain_sum,
        ffn_grads[0],
        ffn_grads[1],
    )


def solution(mesh):
    placed = (
        P(("fsdp", "tensor"), None),
        P("fsdp", None),
        P(),
        P("fsdp", None, "tensor"),
        P("fsdp", None),
        P("fsdp", "tensor"),
        P(None, "tensor"),
        P("tensor"),
        P(),
        P(),
        P("tensor"),
        P("tensor"),
        P("tensor"),
        P("tensor"),
        P("tensor", "fsdp"),
        P("fsdp", "tensor"),
        P("fsdp", None, None),
        P("tensor", "fsdp"),
        P(),
        P("fsdp", None, "tensor"),
        P("tensor", "fsdp"),
        P(("fsdp", "tensor"), None),
    )
    return jax.shard_map(
        body,
        mesh=mesh,
        in_specs=placed,
        out_specs=(
            P(("fsdp", "tensor"), None),
            P(("fsdp", "tensor"), None),
            P(),
            P("fsdp", None, "tensor"),
            P("fsdp", None),
            P("fsdp", "tensor"),
            P(None, "tensor"),
            P("tensor"),
            P(),
            P(),
            P("tensor"),
            P("tensor"),
            P("tensor"),
            P("tensor"),
            P("tensor", "fsdp"),
            P("fsdp", "tensor"),
            P("fsdp", None, None),
            P("tensor", "fsdp"),
            P(),
            P("fsdp", None, "tensor"),
            P("tensor", "fsdp"),
        ),
        check_vma=False,
    )
```

profile of v0, /device:TPU:0, one launch (start us, length us, event | category | flops | bytes accessed | tf_op | source)
XLA Modules:
  0.0 2071.9 jit_solution(13056220638379729504)
XLA Ops:
  16.5 46.5 %all_gather.44 = bf16[1024,2,128]{2,1,0:T(2,128)(2,1)S(1)} all-gather(bf16[64,2,128]{2,1,0:T(2,128)(2,1)S(1)} %convert_element_type.190), channel_id=1, replica_groups=mesh['fsdp'=16,'tensor'=2] {'fsdp'}, dimensions={0}, use_global_device_ids=true | all-gather | bytes 557056 | tf_op jit(solution)/shard_map/all_gather | solution.py:337
  64.9 40.6 %all_gather.45 = bf16[1024,256]{1,0:T(8,128)(2,1)S(1)} all-gather(bf16[64,256]{1,0:T(8,128)(2,1)S(1)} %convert_element_type.191), channel_id=1, replica_groups=mesh['fsdp'=16,'tensor'=2] {'fsdp'}, dimensions={0}, use_global_device_ids=true | all-gather | bytes 557056 | tf_op jit(solution)/shard_map/all_gather | solution.py:336
  109.8 43.6 %all_gather.42 = bf16[1024,256]{1,0:T(8,128)(2,1)} all-gather(bf16[64,256]{1,0:T(8,128)(2,1)S(1)} %convert_element_type.187), channel_id=1, replica_groups=mesh['fsdp'=16,'tensor'=2] {'fsdp'}, dimensions={0}, use_global_device_ids=true | all-gather | bytes 557056 | tf_op jit(solution)/shard_map/all_gather | solution.py:334
  153.9 36.6 %all-gather = bf16[16,64,12]{1,2,0:T(8,128)(2,1)S(1)} all-gather(bf16[1,64,12]{1,2,0:T(8,128)(2,1)S(1)} %convert_bitcast_fusion), channel_id=1, replica_groups=mesh['fsdp'=16,'tensor'=2] {'fsdp'}, dimensions={0}, use_global_device_ids=true | all-gather | bytes 26112 | tf_op jit(solution)/shard_map/all_gather | solution.py:335
  192.6 41.9 %all_gather.46 = bf16[256,1024]{0,1:T(8,128)(2,1)} all-gather(bf16[256,64]{0,1:T(8,128)(2,1)S(1)} %convert_element_type.196), channel_id=1, replica_groups=mesh['fsdp'=16,'tensor'=2] {'fsdp'}, dimensions={1}, use_global_device_ids=true | all-gather | bytes 557056 | tf_op jit(solution)/shard_map/all_gather | solution.py:340
  301.2 297.3 %while.57 = (s32[]{:T(128)}, f32[12,64,128]{2,1,0:T(8,128)S(1)}, s32[]{:T(128)}, f32[8,128,12,64]{1,0,3,2:T(8,128)}, f32[8,12,64,128]{3,2,1,0:T(8,128)}, /*index...) while((s32[]{:T(128)}, f32[12,64,128]{2,1,0:T(8,128)S(1)}, ...), condition=%wide.region_3.4_spmd.clone, body=%wide.region_1.3_spmd.clone.sunk | while | flops 480170880 | bytes 5297505 | solution.py:146
  319.6 11.0 dynamic_update_slice.122
  356.8 11.0 dynamic_update_slice.122
  393.9 11.0 dynamic_update_slice.122
  431.1 11.0 dynamic_update_slice.122
  468.3 11.0 dynamic_update_slice.122
  505.4 11.0 dynamic_update_slice.122
  542.6 11.0 dynamic_update_slice.122
  579.8 11.0 dynamic_update_slice.122
  636.4 74.4 %all-gather.18.cloned.1.call-done = bf16[1024,2,1024]{2,1,0:T(2,128)(2,1)} async-done(((bf16[64,2,1024]{2,1,0:T(2,128)(2,1)}), bf16[1024,2,1024]{2,1,0:T(2,128)(2,1)}) %all-gather.18.cloned.1.call-update) | async-done | bytes 4194320 | tf_op jit(solution)/shard_map/all_gather | solution.py:338
  735.4 65.6 %all-gather.20.cloned.1.call-done = bf16[1024,1024]{0,1:T(8,128)(2,1)} async-done(((bf16[1024,64]{0,1:T(8,128)(2,1)}), bf16[1024,1024]{0,1:T(8,128)(2,1)}) %all-gather.20.cloned.1.call-update) | async-done | bytes 2097168 | tf_op jit(solution)/shard_map/all_gather | solution.py:341
  887.7 268.3 %while.58 = (s32[]{:T(128)}, f32[12]{0:T(128)S(1)}, f32[12,64,128]{2,1,0:T(8,128)S(1)}, f32[8,128,12,64]{1,0,3,2:T(8,128)}, f32[8,128,128]{2,1,0:T(8,128)}, /*in...) while((s32[]{:T(128)}, f32[12]{0:T(128)S(1)}, ...), condition=%wide.region_28.29_spmd.clone, body=%wide.region_17.28_spmd.clone.sunk | while | flops 1137862528 | bytes 13380840 | solution.py:146
  909.3 11.0 dynamic_update_slice.127
  976.3 10.9 dynamic_update_slice.127
  1009.8 10.9 dynamic_update_slice.127
  1043.3 10.9 dynamic_update_slice.127
  1076.8 10.9 dynamic_update_slice.127
  1110.3 10.9 dynamic_update_slice.127
  1143.9 10.9 dynamic_update_slice.127
  1158.4 15.4 multiply_reduce_fusion.5
  1223.2 32.9 %dynamic_update_slice.100 = f32[1024,2,128]{2,1,0:T(2,128)} dynamic-update-slice(f32[1024,2,128]{2,1,0:T(2,128)} %broadcast_in_dim.425, f32[1024,2,64]{2,1,0:T(2,128)S(1)} %copy.230, s32[]{:T(128)} %constant.232.clone.1, s32[]{:T(128)} %constant.232.clone.1, s32[]{:T(128)S(6)} %select_n.187) | dynamic-update-slice | bytes 1048580 | tf_op jit(solution)/shard_map/dynamic_update_slice | solution.py:527
  1345.8 183.2 %all-reduce.34.cloned.1.call-done = (f32[1024,256]{0,1:T(8,128)}, f32[1024,2,128]{2,1,0:T(2,128)}) async-done(((f32[1024,256]{0,1:T(8,128)}, f32[1024,2,128]{2,1,0:T(2,128)}), (f32[1024,256]{0,1:T(8,128)}, f32[1024,2,128]{2,1,0:T(2,128)})) %all-reduce.34.cloned.1.call-update) | async-done | bytes 2097168 | tf_op jit(solution)/shard_map/psum | solution.py:546
  1532.2 74.6 %reduce-scatter.24.cloned.1.call-done = bf16[256,64]{0,1:T(8,128)(2,1)} async-done(((bf16[256,1024]{0,1:T(8,128)(2,1)}), bf16[256,64]{0,1:T(8,128)(2,1)}) %reduce-scatter.24.cloned.1.call-update) | async-done | bytes 32784 | tf_op jit(solution)/shard_map/reduce_scatter | solution.py:278
  1608.2 73.8 %reduce-scatter.22.cloned.1.call-done = bf16[64,256]{1,0:T(8,128)(2,1)} async-done(((bf16[1024,256]{1,0:T(8,128)(2,1)}), bf16[64,256]{1,0:T(8,128)(2,1)}) %reduce-scatter.22.cloned.1.call-update) | async-done | bytes 32784 | tf_op jit(solution)/shard_map/reduce_scatter | solution.py:272
  1683.3 124.9 %reduce-scatter.20.cloned.1.call-done = bf16[768,64]{0,1:T(8,128)(2,1)} async-done(((bf16[768,1024]{0,1:T(8,128)(2,1)}), bf16[768,64]{0,1:T(8,128)(2,1)}) %reduce-scatter.20.cloned.1.call-update) | async-done | bytes 98320 | tf_op jit(solution)/shard_map/reduce_scatter | solution.py:275
  1821.7 44.5 %all-reduce.28 = (f32[1024]{0:T(1024)}, f32[4,1536]{1,0:T(4,128)S(1)}, f32[1536]{0:T(1024)S(1)}, f32[4,256]{1,0:T(4,128)}, f32[256]{0:T(256)}, /*index=5*/f32[24...) all-reduce(f32[1024]{0:T(1024)S(1)} %get-tuple-element.920, ...), channel_id=1, replica_groups=mesh['fsdp'=16,'tensor'=2] {'fsdp','tensor'}, use_global_device_ids=true, to_apply=%region_34.35 | all-reduce | flops 12616 | bytes 100928 | tf_op jit(solution)/shard_map/psum | solution.py:546
  1873.0 188.3 %all-reduce.36.cloned.1.call-done = (bf16[1024,2,768]{2,1,0:T(2,128)(2,1)}, bf16[1024,2,1024]{2,1,0:T(2,128)(2,1)}) async-done(((bf16[1024,2,768]{2,1,0:T(2,128)(2,1)}, bf16[1024,2,1024]{2,1,0:T(2,128)(2,1)}), (bf16[1024,2,768]{2,1,0:T(2,128)(2,1)}, bf16[1024,2,1024]{2,1,0:T(2,128)(2,1)})) %all-reduce.36.cloned.1.call-update) | async-done | bytes 7340048
  (1066 shorter events, 797.4 us)
Async XLA Ops:
  7.2 229.1 %all-gather.10.cloned.1.call-start = ((), (), s32[]{:S(2)}) async-start(), calls=%async_computation.9 | async-start | bytes 3145728 | tf_op jit(solution)/shard_map/all_gather | solution.py:354
  12.0 179.2 %copy-start.133 = (f32[12]{0:T(128)S(1)}, f32[12]{0:T(128)}, u32[]{:S(2)}) copy-start(f32[12]{0:T(128)} %param.37) | copy-start | bytes 148
  12.0 179.8 %copy-start.132 = (f32[12]{0:T(128)S(1)}, f32[12]{0:T(128)}, u32[]{:S(2)}) copy-start(f32[12]{0:T(128)} %param.38) | copy-start | bytes 148
  12.0 180.6 %copy-start.68 = (f32[256,64]{0,1:T(8,128)S(1)}, f32[256,64]{0,1:T(8,128)}, u32[]{:S(2)}) copy-start(f32[256,64]{0,1:T(8,128)} %param.43) | copy-start | bytes 196612
  12.1 261.2 %all-gather.12.cloned.1.call-start = ((), (), s32[]{:S(2)}) async-start(), calls=%async_computation.10 | async-start | bytes 3342336 | tf_op jit(solution)/shard_map/all_gather | solution.py:333
  13.0 601.0 %all-gather.14.cloned.1.call-start = ((), (), s32[]{:S(2)}) async-start(), calls=%async_computation.11 | async-start | bytes 1671168 | tf_op jit(solution)/shard_map/all_gather | solution.py:339
  13.7 616.1 %reduce-scatter.12.cloned.1.call-start = ((), (), s32[]{:S(2)}) async-start(), calls=%async_computation.12 | async-start | bytes 6291456 | tf_op jit(solution)/shard_map/reduce_scatter | solution.py:428
  13.8 222.0 %copy-start.121 = (f32[32]{0:T(128)}, f32[32]{0:T(128)S(1)}, u32[]{:S(2)}) copy-start(f32[32]{0:T(128)S(1)} %multiply_exponential_fusion) | copy-start | bytes 388
  289.8 580.4 %copy-start.3 = (f32[1024,768]{1,0:T(8,128)}, f32[1024,768]{1,0:T(8,128)S(1)}, u32[]{:S(2)}) copy-start(f32[1024,768]{1,0:T(8,128)S(1)} %get-tuple-element.1020) | copy-start | bytes 9437188
  614.0 256.2 %copy-start.100 = (f32[1024]{0:T(1024)}, f32[1024]{0:T(1024)S(1)}, u32[]{:S(2)}) copy-start(f32[1024]{0:T(1024)S(1)} %get-tuple-element.1051) | copy-start | bytes 12292
  621.2 89.6 %all-gather.18.cloned.1.call-start = ((), (), s32[]{:S(2)}) async-start(), calls=%async_computation.14 | async-start | bytes 4456448 | tf_op jit(solution)/shard_map/all_gather | solution.py:338
  623.2 98.9 %all-gather.16.cloned.1.call-start = ((), (), s32[]{:S(2)}) async-start(), calls=%async_computation.13 | async-start | bytes 3145728 | tf_op jit(solution)/shard_map/all_gather | solution.py:432
  634.6 100.8 %all-gather.22.cloned.1.call-start = ((), (), s32[]{:S(2)}) async-start(), calls=%async_computation.17 | async-start | bytes 3145728 | tf_op jit(solution)/shard_map/all_gather | solution.py:442
  635.4 165.7 %all-gather.20.cloned.1.call-start = ((), (), s32[]{:S(2)}) async-start(), calls=%async_computation.15 | async-start | bytes 2228224 | tf_op jit(solution)/shard_map/all_gather | solution.py:341
  636.1 193.9 %reduce-scatter.16.cloned.1.call-start = ((), (), s32[]{:S(2)}) async-start(), calls=%async_computation.18 | async-start | bytes 6291456 | tf_op jit(solution)/shard_map/reduce_scatter | solution.py:451
  819.2 23.8 %reduce-scatter.14.cloned.1.call-start = ((), (), s32[]{:S(2)}) async-start(), calls=%async_computation.16 | async-start | bytes 3145728 | tf_op jit(solution)/shard_map/reduce_scatter | solution.py:437
  825.2 35.4 %all-gather.24.cloned.1.call-start = ((), (), s32[]{:S(2)}) async-start(), calls=%async_computation.19 | async-start | bytes 3145728 | tf_op jit(solution)/shard_map/all_gather | solution.py:454
  848.7 492.6 %reduce-scatter.26.cloned.1.call-start = ((), (), s32[]{:S(2)}) async-start(), calls=%async_computation.24 | async-start | bytes 2228224 | tf_op jit(solution)/shard_map/reduce_scatter | solution.py:258
  856.5 487.8 %reduce-scatter.28.cloned.1.call-start = ((), (), s32[]{:S(2)}) async-start(), calls=%async_computation.25 | async-start | bytes 278528
  887.7 268.3 %copy-start.36 = (bf16[256,1024]{0,1:T(8,128)(2,1)S(1)}, bf16[256,1024]{0,1:T(8,128)(2,1)}, u32[]{:S(2)}) copy-start(bf16[256,1024]{0,1:T(8,128)(2,1)} %all_gather.46) | copy-start | bytes 1572868
  1213.0 316.0 %all-reduce.34.cloned.1.call-start = ((), (), s32[]{:S(2)}) async-start(), calls=%async_computation.26 | async-start | bytes 4194304 | tf_op jit(solution)/shard_map/psum | solution.py:546
  1256.1 350.7 %reduce-scatter.24.cloned.1.call-start = ((), (), s32[]{:S(2)}) async-start(), calls=%async_computation.23 | async-start | bytes 557056 | tf_op jit(solution)/shard_map/reduce_scatter | solution.py:278
  1268.3 413.7 %reduce-scatter.22.cloned.1.call-start = ((), (), s32[]{:S(2)}) async-start(), calls=%async_computation.22 | async-start | bytes 557056 | tf_op jit(solution)/shard_map/reduce_scatter | solution.py:272
  1276.0 532.3 %reduce-scatter.20.cloned.1.call-start = ((), (), s32[]{:S(2)}) async-start(), calls=%async_computation.21 | async-start | bytes 1671168 | tf_op jit(solution)/shard_map/reduce_scatter | solution.py:275
  1292.0 527.6 %reduce-scatter.18.cloned.1.call-start = ((), (), s32[]{:S(2)}) async-start(), calls=%async_computation.20 | async-start | bytes 3145728 | tf_op jit(solution)/shard_map/reduce_scatter | solution.py:505
  1308.5 752.9 %all-reduce.36.cloned.1.call-start = ((), (), s32[]{:S(2)}) async-start(), calls=%async_computation.27 | async-start | bytes 14680064
  1339.4 480.2 %copy-start.11 = (bf16[512,1024]{1,0:T(8,128)(2,1)S(1)}, bf16[512,1024]{1,0:T(8,128)(2,1)}, u32[]{:S(2)}) copy-start(bf16[512,1024]{1,0:T(8,128)(2,1)} %param.26) | copy-start | bytes 3145732
  1339.4 480.2 %copy-start.87 = (f32[1024]{0:T(1024)S(1)}, f32[1024]{0:T(1024)}, u32[]{:S(2)}) copy-start(f32[1024]{0:T(1024)} %param.28) | copy-start | bytes 12292
  1339.4 480.2 %copy-start.91 = (f32[512]{0:T(512)S(1)}, f32[512]{0:T(512)}, u32[]{:S(2)}) copy-start(f32[512]{0:T(512)} %copy-done.90) | copy-start | bytes 6148
  1339.5 482.3 %copy-start.99 = (f32[1024]{0:T(1024)S(1)}, f32[1024]{0:T(1024)}, u32[]{:S(2)}) copy-start(f32[1024]{0:T(1024)} %get-tuple-element.913) | copy-start | bytes 12292
  1339.5 530.4 %copy-start.17 = (f32[512,1024]{1,0:T(8,128)S(1)}, f32[512,1024]{1,0:T(8,128)}, u32[]{:S(2)}) copy-start(f32[512,1024]{1,0:T(8,128)} %get-tuple-element.1012) | copy-start | bytes 6291460
  1339.5 530.4 %copy-start.119 = (f32[512]{0:T(512)S(1)}, f32[512]{0:T(512)}, u32[]{:S(2)}) copy-start(f32[512]{0:T(512)} %get-tuple-element.1058) | copy-start | bytes 6148
  (146 other events, 2584.6 us)
Sparse Core Ops, SparseCore 0:
  12.1 13.2 all-gather.9
  28.8 73.8 all-gather.11
  106.0 58.7 all-gather.13
  621.3 8.4 reduce-scatter.11
  633.4 77.3 all-gather.17
  712.8 9.1 all-gather.15
  723.6 11.7 all-gather.21
  739.1 61.8 all-gather.19
  819.3 10.6 reduce-scatter.15
  832.1 10.8 reduce-scatter.13
  848.8 11.7 all-gather.23
  862.8 81.8 reduce-scatter.25
  1213.2 77.3 reduce-scatter.27
  1296.0 233.0 all-reduce.33
  1531.2 75.5 reduce-scatter.23
  1608.9 73.0 reduce-scatter.21
  1687.3 120.9 reduce-scatter.19
  1811.0 8.5 reduce-scatter.17
  1826.1 235.2 all-reduce.35
where the time goes:
time: 2090 us; the launch traced here: 2070 us
  waiting for transfers between devices  828 us (40%)
  local copies, waits for them, and re-layouts  447 us (21%)
  matrix products  284 us (14%)
  blocking collectives  259 us (12%)
  other arithmetic  229 us (11%)
    unnamed x21, waiting for transfers between devices  189 us
    dynamic_update_slice x24, local copies, waits for them, and re-layouts, state_scan(): outputs = lax.scan(jax.checkpoint(advance), initial, pieces)[1]  185 us
    psum x1, waiting for transfers between devices, body(): lax.psum((grad_shared[:, :state_cols], keyval_full, state_conv_part, stat...  183 us
    reduce_scatter x1, waiting for transfers between devices, send_mixer(): lax.psum_scatter(proj_grad.astype(jnp.bfloat16), 'fsdp', scatter_dimensio...  125 us
    reduce_scatter x1, waiting for transfers between devices, send_mixer(): lax.psum_scatter(attention_grad.astype(jnp.bfloat16), 'fsdp', scatter_dim...  74.6 us
    all_gather x1, waiting for transfers between devices, body(): lax.all_gather(gate_up.astype(jnp.bfloat16), 'fsdp', axis=0, tiled=True)  74.4 us
    reduce_scatter x1, waiting for transfers between devices, send_mixer(): lax.psum_scatter(query_grad.astype(jnp.bfloat16), 'fsdp', scatter_dimensi...  73.8 us
    all_gather x1, waiting for transfers between devices, body(): lax.all_gather(down_proj.astype(jnp.bfloat16), 'fsdp', axis=1, tiled=True)  65.6 us
  transfers between devices with their start and end apart: 19, of which 14 were waited for; matrix products, arithmetic and copies ran while one was open for 44% of the time, Pallas kernels for 0%

commit v1 on v0

v1 whole, which is shorter than its diff:
```python
import functools
import math

import jax
import jax.numpy as jnp
from jax import lax
from jax.experimental import pallas as pl
from jax.experimental.pallas import tpu as pltpu
from jax.sharding import PartitionSpec as P

QUERY_HEADS = 8
KEYVAL_HEADS = 2
HEAD_SIZE = 64
DSSM = 1536
EPS = 1e-05
THETA = 100000000000.0

LANES = 128
CHUNK = 128
MASKED = -1e30
BF, F32 = jnp.bfloat16, jnp.float32


def left_dot(left_side, right_side):
    return lax.dot_general(left_side, right_side, (((0,), (0,)), ((), ())), preferred_element_type=F32)


def right_dot(left_side, right_side):
    return lax.dot_general(left_side, right_side, (((1,), (1,)), ((), ())), preferred_element_type=F32)


def plain_dot(left_side, right_side):
    return jnp.dot(left_side, right_side, preferred_element_type=F32)


def mm(a, b):
    return jnp.dot(a.astype(BF), b.astype(BF), preferred_element_type=F32)


def mm_nt(a, b):
    return lax.dot_general(a.astype(BF), b.astype(BF), (((1,), (1,)), ((), ())), preferred_element_type=F32)


def mm_tn(a, b):
    return lax.dot_general(a.astype(BF), b.astype(BF), (((0,), (0,)), ((), ())), preferred_element_type=F32)


def exact_mm(a, b):
    return jnp.dot(a, b, precision=lax.Precision.HIGHEST, preferred_element_type=F32)


def sigmoid(v):
    return 1.0 / (1.0 + jnp.exp(-v))


def softplus(v):
    return jnp.maximum(v, 0.0) + jnp.log1p(jnp.exp(-jnp.abs(v)))


def split_lanes(values, axis):
    high = values.astype(BF)
    low = (values - high.astype(F32)).astype(BF)
    return jnp.concatenate([high, low], axis=axis)


def iota2(shape, axis):
    return lax.broadcasted_iota(jnp.int32, shape, axis)


def conv_taps(buffer, feats, taps, bias, rows):
    total = buffer[8 : 8 + rows, :] * taps[3:4, :] + bias
    for k in range(1, 4):
        total = total + buffer[8 - k : 8 - k + rows, :] * feats[:, k : k + 1] * taps[3 - k : 4 - k, :]
    return total


def step_parts(step_ref, heads_ref, feats, rows):
    raw = step_ref[...] + heads_ref[0:1, :]
    step = softplus(raw)
    lower = (iota2((rows, rows), 0) >= iota2((rows, rows), 1)).astype(F32)
    log_decay = exact_mm(lower, step * heads_ref[1:2, :])
    last = log_decay[rows - 1 : rows, :]
    enter = jnp.exp(log_decay) * feats[:, 4:5]
    leave = jnp.exp(last - log_decay) * feats[:, 5:6]
    return raw, step, log_decay, enter, leave


def mamba_fwd_kernel(
    feats_ref, docs_ref, x_ref, bc_ref, step_ref, z_ref, taps_ref, staps_ref, heads_ref, expand_ref,
    gain_ref, scan_ref, low_ref, square_ref, states_ref, xbuf, bcbuf, memory,
):
    rows, width = x_ref.shape
    states = bc_ref.shape[1] // 2

    @pl.when(pl.program_id(0) == 0)
    def _():
        xbuf[0:8, :] = jnp.zeros((8, width), F32)
        bcbuf[0:8, :] = jnp.zeros((8, 2 * states), F32)
        memory[...] = jnp.zeros_like(memory)

    feats = feats_ref[...]
    xbuf[8 : 8 + rows, :] = x_ref[...]
    bcbuf[8 : 8 + rows, :] = bc_ref[...]
    pre = conv_taps(xbuf, feats, taps_ref, taps_ref[4:5, :], rows)
    values = pre * sigmoid(pre)
    pre_bc = conv_taps(bcbuf, feats, staps_ref, staps_ref[4:5, :], rows)
    both = pre_bc * sigmoid(pre_bc)
    xbuf[0:8, :] = xbuf[rows : rows + 8, :]
    bcbuf[0:8, :] = bcbuf[rows : rows + 8, :]
    key_in = both[:, :states].astype(BF)
    key_out = both[:, states:].astype(BF)
    _, step, log_decay, enter, leave = step_parts(step_ref, heads_ref, feats, rows)
    expanded = jnp.dot(
        split_lanes(jnp.concatenate([step, enter, leave], axis=0), 1), expand_ref[...], preferred_element_type=F32
    )
    step_w, enter_w, leave_w = expanded[:rows], expanded[rows : 2 * rows], expanded[2 * rows :]
    scaled = values * step_w
    gram = mm_nt(key_out, key_in)
    allowed = (feats[:, 0:1] == docs_ref[...]) & (iota2((rows, rows), 0) >= iota2((rows, rows), 1))
    bias = jnp.where(allowed, 0.0, MASKED)
    log_rows = log_decay.T
    front = iota2((rows, LANES), 1) < LANES // 2
    held = memory[...]
    states_ref[0] = held.astype(BF)
    carried = mm(key_out, held) * enter_w
    fresh = mm_tn(key_in, leave_w * scaled)
    memory[...] = held * enter_w[rows - 1 : rows, :] + fresh
    squares = jnp.zeros((rows, 1), F32)
    for pair in range(width // LANES):
        lanes = slice(pair * LANES, (pair + 1) * LANES)
        mixes = []
        for h in (2 * pair, 2 * pair + 1):
            decay = jnp.exp(log_decay[:, h : h + 1] - log_rows[h : h + 1, :] + bias)
            mixes.append((gram * decay).astype(BF))
        part = scaled[:, lanes]
        stacked = jnp.concatenate([jnp.where(front, part, 0.0), jnp.where(front, 0.0, part)], axis=0)
        inside = mm(jnp.concatenate(mixes, axis=1), stacked)
        scan = inside + carried[:, lanes] + values[:, lanes] * taps_ref[5:6, lanes]
        scan_ref[:, lanes] = scan
        z = z_ref[:, lanes]
        gated = scan * (z * sigmoid(z))
        low_ref[:, lanes] = (gated * gain_ref[:, lanes]).astype(BF)
        squares = squares + jnp.sum(gated * gated, axis=1, keepdims=True)
    square_ref[...] = squares


def mamba_bwd_kernel(
    feats_ref, docs_col_ref, docs_ref, x_ref, x_before_ref, bc_ref, bc_before_ref, step_ref, z_ref, scan_ref, states_ref, norm_grad_ref,
    taps_ref, staps_ref, heads_ref, expand_ref, reduce_ref, gain_ref,
    dz_ref, grads_ref, sums_ref, ssums_ref, hsums_ref,
    xbuf, bcbuf, dxbuf, dbcbuf, dmemory,
):
    rows, width = x_ref.shape
    states = bc_ref.shape[1] // 2

    @pl.when(pl.program_id(0) == 0)
    def _():
        dxbuf[rows : rows + 8, :] = jnp.zeros((8, width), F32)
        dbcbuf[rows : rows + 8, :] = jnp.zeros((8, 2 * states), F32)
        dmemory[...] = jnp.zeros_like(dmemory)
        sums_ref[...] = jnp.zeros_like(sums_ref)
        ssums_ref[...] = jnp.zeros_like(ssums_ref)
        hsums_ref[...] = jnp.zeros_like(hsums_ref)

    feats = feats_ref[...]
    xbuf[0:8, :] = x_before_ref[...]
    bcbuf[0:8, :] = bc_before_ref[...]
    xbuf[8 : 8 + rows, :] = x_ref[...]
    bcbuf[8 : 8 + rows, :] = bc_ref[...]
    pre = conv_taps(xbuf, feats, taps_ref, taps_ref[4:5, :], rows)
    pre_gate = sigmoid(pre)
    values = pre * pre_gate
    pre_bc = conv_taps(bcbuf, feats, staps_ref, staps_ref[4:5, :], rows)
    bc_gate = sigmoid(pre_bc)
    both = pre_bc * bc_gate
    key_in = both[:, :states].astype(BF)
    key_out = both[:, states:].astype(BF)
    raw, step, log_decay, enter, leave = step_parts(step_ref, heads_ref, feats, rows)
    expanded = jnp.dot(
        split_lanes(jnp.concatenate([step, enter, leave], axis=0), 1), expand_ref[...], preferred_element_type=F32
    )
    step_w, enter_w, leave_w = expanded[:rows], expanded[rows : 2 * rows], expanded[2 * rows :]
    scaled = values * step_w
    z = z_ref[...]
    z_gate = sigmoid(z)
    z_silu = z * z_gate
    scan = scan_ref[...]
    gated = scan * z_silu
    norm_grad = norm_grad_ref[...].astype(F32)
    weighted = norm_grad * feats[:, 9:10]
    gated_grad = weighted * gain_ref[...] - gated * feats[:, 10:11]
    dscan = gated_grad * z_silu
    dz_ref[...] = (gated_grad * scan * (z_gate * (1.0 + z * (1.0 - z_gate)))).astype(BF)
    sums_ref[6:7, :] += jnp.sum(weighted * gated, axis=0, keepdims=True)
    sums_ref[5:6, :] += jnp.sum(dscan * values, axis=0, keepdims=True)
    held = states_ref[0]
    dheld = dmemory[...]
    dheld_low = dheld.astype(BF)
    enter_grad = (dscan * enter_w).astype(BF)
    left = leave_w * scaled
    passed = mm(key_in, dheld_low)
    arrived = mm(key_out, held)
    dkey_out = mm_nt(enter_grad, held)
    dkey_in = mm_nt(left, dheld_low)
    carry = enter_w[rows - 1 : rows, :]
    dmemory[...] = dheld * carry + mm_tn(key_out, enter_grad)
    enter_terms = dscan * enter_w * arrived
    leave_terms = left * passed
    carry_terms = jnp.sum(dheld * held.astype(F32), axis=0, keepdims=True) * carry
    gram = mm_nt(key_in, key_out)
    allowed = (docs_col_ref[...] == docs_ref[...]) & (iota2((rows, rows), 0) <= iota2((rows, rows), 1))
    bias = jnp.where(allowed, 0.0, MASKED)
    log_rows = log_decay.T
    front = iota2((rows, LANES), 1) < LANES // 2
    gram_grad = jnp.zeros((rows, rows), F32)
    lane_of = iota2((rows, LANES), 1)
    row_of = iota2((LANES, rows), 0)
    sent = jnp.zeros((rows, LANES), F32)
    received = jnp.zeros((LANES, rows), F32)
    inside_grads = []
    for pair in range(width // LANES):
        lanes = slice(pair * LANES, (pair + 1) * LANES)
        dy = dscan[:, lanes].astype(BF)
        part = scaled[:, lanes]
        stacked = jnp.concatenate([jnp.where(front, part, 0.0), jnp.where(front, 0.0, part)], axis=0)
        cross = mm_nt(stacked, dy)
        mixes = []
        for j, h in enumerate((2 * pair, 2 * pair + 1)):
            decay = jnp.exp(log_rows[h : h + 1, :] - log_decay[:, h : h + 1] + bias)
            mix = gram * decay
            mixes.append(mix.astype(BF))
            dmix = cross[j * rows : (j + 1) * rows, :]
            gram_grad = gram_grad + dmix * decay
            flow = dmix * mix
            sent = jnp.where(lane_of == h, jnp.sum(flow, axis=1, keepdims=True), sent)
            received = jnp.where(row_of == h, jnp.sum(flow, axis=0, keepdims=True), received)
        grads = mm(jnp.concatenate(mixes, axis=0), dy)
        inside_grads.append(jnp.where(front, grads[:rows], grads[rows:]))
    dscaled = jnp.concatenate(inside_grads, axis=1) + leave_w * passed
    dkey_in = dkey_in + mm(gram_grad, key_out)
    dkey_out = dkey_out + mm_tn(gram_grad, key_in)
    reduced = jnp.dot(
        split_lanes(
            jnp.concatenate([enter_terms, leave_terms, dscaled * values, jnp.broadcast_to(carry_terms, (8, width))], axis=0), 1
        ),
        reduce_ref[...],
        preferred_element_type=F32,
    )
    after = reduced[:rows] + received.T - sent
    upper = (iota2((rows, rows), 0) <= iota2((rows, rows), 1)).astype(F32)
    strict = (iota2((rows, rows), 0) > iota2((rows, rows), 1)).astype(F32)
    decay_grad = exact_mm(upper, after) + exact_mm(strict, reduced[rows : 2 * rows]) + reduced[3 * rows : 3 * rows + 1]
    dstep = decay_grad * heads_ref[1:2, :] + reduced[2 * rows : 3 * rows]
    draw = dstep * sigmoid(raw)
    grads_ref[:, width + 2 * states :] = draw.astype(BF)
    hsums_ref[0:1, :] += jnp.sum(draw, axis=0, keepdims=True)
    hsums_ref[1:2, :] += jnp.sum(decay_grad * step, axis=0, keepdims=True) * heads_ref[1:2, :]
    dvalues = dscaled * step_w + dscan * taps_ref[5:6, :]
    dpre = dvalues * (pre_gate * (1.0 + pre * (1.0 - pre_gate)))
    dboth = jnp.concatenate([dkey_in, dkey_out], axis=1)
    dpre_bc = dboth * (bc_gate * (1.0 + pre_bc * (1.0 - bc_gate)))
    for dpre_now, buffer, dbuffer, taps, totals, lanes in (
        (dpre, xbuf, dxbuf, taps_ref, sums_ref, slice(0, width)),
        (dpre_bc, bcbuf, dbcbuf, staps_ref, ssums_ref, slice(width, width + 2 * states)),
    ):
        dbuffer[0:rows, :] = dpre_now
        grad = dpre_now * taps[3:4, :]
        totals[3:4, :] += jnp.sum(dpre_now * buffer[8 : 8 + rows, :], axis=0, keepdims=True)
        totals[4:5, :] += jnp.sum(dpre_now, axis=0, keepdims=True)
        for k in range(1, 4):
            grad = grad + dbuffer[k : k + rows, :] * feats[:, 5 + k : 6 + k] * taps[3 - k : 4 - k, :]
            totals[3 - k : 4 - k, :] += jnp.sum(
                dpre_now * buffer[8 - k : 8 - k + rows, :] * feats[:, k : k + 1], axis=0, keepdims=True
            )
        grads_ref[:, lanes] = grad.astype(BF)
        dbuffer[rows : rows + 8, :] = dbuffer[0:8, :]


def expand_matrix(width):
    head_of = jnp.arange(width, dtype=jnp.int32) // (LANES // 2)
    one = (jnp.arange(LANES, dtype=jnp.int32)[:, None] == head_of[None, :]).astype(BF)
    return jnp.concatenate([one, one], axis=0)


def token_features(docs, chunk):
    total = docs.shape[0]
    doc = docs.astype(F32)
    back = [jnp.concatenate([jnp.zeros((k,), F32), (docs[k:] == docs[:-k]).astype(F32)]) for k in (1, 2, 3)]
    ahead = [jnp.concatenate([(docs[k:] == docs[:-k]).astype(F32), jnp.zeros((k,), F32)]) for k in (1, 2, 3)]
    blocks = docs.reshape(-1, chunk)
    before = jnp.concatenate([jnp.full((1,), -1, jnp.int32), blocks[:-1, -1]])
    entered = (blocks == before[:, None]).astype(F32).reshape(total)
    leaving = (blocks == blocks[:, -1:]).astype(F32).reshape(total)
    return jnp.stack([doc] + back + [entered, leaving] + ahead, axis=1)


def spec(block, index):
    return pl.BlockSpec(block, index)


def mamba_forward(feats, doc_row, ssm_in, z, taps, staps, heads, gain, width, states2):
    total = z.shape[0]
    rows = CHUNK
    count = total // rows
    block = lambda w, place=0: spec((rows, w), lambda i: (i, place))
    whole = lambda a: spec(a.shape, lambda i: (0,) * a.ndim)
    expand = expand_matrix(width)
    return pl.pallas_call(
        mamba_fwd_kernel,
        grid=(count,),
        in_specs=[
            block(feats.shape[1]), spec((1, rows), lambda i: (0, i)), block(width), block(states2, width // states2),
            block(LANES, (width + states2) // LANES), block(width), whole(taps), whole(staps), whole(heads), whole(expand), whole(gain),
        ],
        out_specs=[block(width), block(width), block(1), spec((1, states2 // 2, width), lambda i: (i, 0, 0))],
        out_shape=[
            jax.ShapeDtypeStruct((total, width), F32),
            jax.ShapeDtypeStruct((total, width), BF),
            jax.ShapeDtypeStruct((total, 1), F32),
            jax.ShapeDtypeStruct((count, states2 // 2, width), BF),
        ],
        scratch_shapes=[
            pltpu.VMEM((rows + 8, width), F32), pltpu.VMEM((rows + 8, states2), F32), pltpu.VMEM((states2 // 2, width), F32),
        ],
        compiler_params=pltpu.CompilerParams(vmem_limit_bytes=32 * 2**20),
        cost_estimate=pl.CostEstimate(flops=20 * 10**9, bytes_accessed=total * width * 20, transcendentals=total * width * 4),
        name="mamba_fwd",
    )(feats, doc_row, ssm_in, ssm_in, ssm_in, z, taps, staps, heads, expand, gain)


def mamba_backward(feats, doc_col, doc_row, ssm_in, z, scan, states, norm_grad, taps, staps, heads, gain, width, states2):
    total = z.shape[0]
    rows = CHUNK
    count = total // rows
    back = lambda i: count - 1 - i
    block = lambda w, place=0: spec((rows, w), lambda i: (back(i), place))
    before = lambda w, place=0: spec((8, w), lambda i: (jnp.maximum(back(i) * (rows // 8) - 1, 0), place))
    whole = lambda a: spec(a.shape, lambda i: (0,) * a.ndim)
    expand = expand_matrix(width)
    reduce = expand[:LANES].T
    reduce = jnp.concatenate([reduce, reduce], axis=0)
    totals = lambda w: spec((8, w), lambda i: (0, 0))
    return pl.pallas_call(
        mamba_bwd_kernel,
        grid=(count,),
        in_specs=[
            block(feats.shape[1]), block(1), spec((1, rows), lambda i: (0, back(i))), block(width), before(width),
            block(states2, width // states2), before(states2, width // states2), block(LANES, (width + states2) // LANES),
            block(width), block(width), spec((1, states2 // 2, width), lambda i: (back(i), 0, 0)), block(width),
            whole(taps), whole(staps), whole(heads), whole(expand), whole(reduce), whole(gain),
        ],
        out_specs=[block(width), block(width + states2 + LANES), totals(width), totals(states2), totals(LANES)],
        out_shape=[
            jax.ShapeDtypeStruct((total, width), BF),
            jax.ShapeDtypeStruct((total, width + states2 + LANES), BF),
            jax.ShapeDtypeStruct((8, width), F32),
            jax.ShapeDtypeStruct((8, states2), F32),
            jax.ShapeDtypeStruct((8, LANES), F32),
        ],
        scratch_shapes=[
            pltpu.VMEM((rows + 8, width), F32), pltpu.VMEM((rows + 8, states2), F32),
            pltpu.VMEM((rows + 8, width), F32), pltpu.VMEM((rows + 8, states2), F32), pltpu.VMEM((states2 // 2, width), F32),
        ],
        compiler_params=pltpu.CompilerParams(vmem_limit_bytes=32 * 2**20),
        cost_estimate=pl.CostEstimate(flops=35 * 10**9, bytes_accessed=total * width * 24, transcendentals=total * width * 5),
        name="mamba_bwd",
    )(feats, doc_col, doc_row, ssm_in, ssm_in, ssm_in, ssm_in, ssm_in, z, scan, states, norm_grad, taps, staps, heads, expand, reduce, gain)


QBLOCK = 256


def swap_halves(values):
    lane = iota2(values.shape, 1) % (LANES // 2)
    return jnp.where(lane < LANES // 4, pltpu.roll(values, LANES - LANES // 4, 1), pltpu.roll(values, LANES // 4, 1))


def stack_heads(part):
    front = iota2(part.shape, 1) < LANES // 2
    zero = jnp.zeros_like(part)
    return jnp.concatenate([jnp.where(front, part, zero), jnp.where(front, zero, part)], axis=0)


def attention_fwd_kernel(groups, docs_col_ref, docs_ref, q_ref, kv_ref, cos_ref, sin_ref, out_ref, lse_ref, qrot_ref, keys_ref, values_ref):
    total = q_ref.shape[0]
    pairs = q_ref.shape[1] // LANES
    block = min(QBLOCK, total)
    cos, sin = cos_ref[...], sin_ref[...]
    front = iota2((total, LANES), 1) < LANES // 2
    for g in range(groups):
        lanes = slice(g * LANES, (g + 1) * LANES)
        raw = kv_ref[:, lanes]
        turned = raw * cos + swap_halves(raw) * sin
        keys_ref[:, lanes] = jnp.where(front, turned, pltpu.roll(turned, LANES // 2, 1)).astype(BF)
        values_ref[:, lanes] = jnp.where(front, pltpu.roll(raw, LANES // 2, 1), raw).astype(BF)
    for p in range(pairs):
        lanes = slice(p * LANES, (p + 1) * LANES)
        raw = q_ref[:, lanes]
        qrot_ref[:, lanes] = ((raw * cos + swap_halves(raw) * sin).astype(BF).astype(F32) * (LANES // 2) ** -0.5).astype(BF)
    front = iota2((block, LANES), 1) < LANES // 2
    lane_of = iota2((block, LANES), 1)
    for start in range(0, total, block):
        rows, end = slice(start, start + block), start + block
        allowed = (docs_col_ref[rows, :] == docs_ref[:, :end]) & (
            iota2((block, end), 0) + start >= iota2((block, end), 1)
        )
        bias = jnp.where(allowed, 0.0, MASKED)
        bias = jnp.concatenate([bias, bias], axis=0)
        sums = jnp.zeros((block, LANES), F32)
        for p in range(pairs):
            lanes = slice(p * LANES, (p + 1) * LANES)
            g = p * groups // pairs
            kv = slice(g * LANES, (g + 1) * LANES)
            scores = mm_nt(stack_heads(qrot_ref[rows, lanes]), keys_ref[:end, kv]) + bias
            top = jnp.max(scores, axis=1, keepdims=True)
            raised = jnp.exp(scores - top)
            whole = jnp.sum(raised, axis=1, keepdims=True)
            mixed = mm(raised, values_ref[:end, kv]) / whole
            out_ref[rows, lanes] = jnp.where(front, mixed[:block], mixed[block:]).astype(BF)
            logs = top + jnp.log(whole)
            sums = jnp.where(lane_of == 2 * p, logs[:block], sums)
            sums = jnp.where(lane_of == 2 * p + 1, logs[block:], sums)
        lse_ref[rows, :] = sums


def attention_bwd_kernel(groups, docs_col_ref, docs_ref, qrot_ref, keys_ref, values_ref, lse_ref, up_ref, cos_ref, sin_ref, grads_ref, dk_acc, dv_acc):
    total = qrot_ref.shape[0]
    pairs = qrot_ref.shape[1] // LANES
    block = min(QBLOCK, total)
    dk_acc[...] = jnp.zeros_like(dk_acc)
    dv_acc[...] = jnp.zeros_like(dv_acc)
    front = iota2((block, LANES), 1) < LANES // 2
    for start in range(0, total, block):
        rows, end = slice(start, start + block), start + block
        allowed = (docs_col_ref[:end, :] == docs_ref[:, rows]) & (
            iota2((end, block), 0) <= iota2((end, block), 1) + start
        )
        bias = jnp.where(allowed, 0.0, MASKED)
        logs = lse_ref[rows, :].T
        cos, sin = cos_ref[rows, :], sin_ref[rows, :]
        for p in range(pairs):
            lanes = slice(p * LANES, (p + 1) * LANES)
            g = p * groups // pairs
            kv = slice(g * LANES, (g + 1) * LANES)
            keys, values = keys_ref[:end, kv], values_ref[:end, kv]
            queries = stack_heads(qrot_ref[rows, lanes])
            ups = stack_heads(up_ref[rows, lanes])
            shift = jnp.concatenate([bias - logs[2 * p : 2 * p + 1], bias - logs[2 * p + 1 : 2 * p + 2]], axis=1)
            probs = jnp.exp(mm_nt(keys, queries) + shift)
            grads = mm_nt(values, ups)
            centre = jnp.sum(probs * grads, axis=0, keepdims=True)
            score_grads = (probs * (grads - centre)).astype(BF)
            dk_acc[:end, kv] += mm(score_grads, queries)
            dv_acc[:end, kv] += mm(probs, ups)
            dq = mm_tn(score_grads, keys)
            dq = jnp.where(front, dq[:block], dq[block:]) * (LANES // 2) ** -0.5
            grads_ref[rows, lanes] = (dq * cos - swap_halves(dq) * sin).astype(BF)
    front = iota2((total, LANES), 1) < LANES // 2
    for g in range(groups):
        kv = slice(g * LANES, (g + 1) * LANES)
        dk, dv = dk_acc[:, kv], dv_acc[:, kv]
        dk = dk + pltpu.roll(dk, LANES // 2, 1)
        dk = dk * cos_ref[...] - swap_halves(dk) * sin_ref[...]
        dv = dv + pltpu.roll(dv, LANES // 2, 1)
        out = slice((pairs + g) * LANES, (pairs + g + 1) * LANES)
        grads_ref[:, out] = jnp.where(front, dk, dv).astype(BF)


def attention_forward(groups, doc_col, doc_row, qkv, cos, sin, query_width):
    total = qkv.shape[0]
    kv_width = qkv.shape[1] - query_width
    whole = lambda a: spec(a.shape, lambda i: (0,) * a.ndim)
    columns = lambda w, place=0: spec((total, w), lambda i: (0, place))
    return pl.pallas_call(
        functools.partial(attention_fwd_kernel, groups),
        grid=(1,),
        in_specs=[whole(doc_col), whole(doc_row), columns(query_width), columns(kv_width, query_width // kv_width), whole(cos), whole(sin)],
        out_specs=[columns(query_width), columns(LANES), columns(query_width), columns(kv_width), columns(kv_width)],
        out_shape=[
            jax.ShapeDtypeStruct((total, query_width), BF), jax.ShapeDtypeStruct((total, LANES), F32),
            jax.ShapeDtypeStruct((total, query_width), BF), jax.ShapeDtypeStruct((total, kv_width), BF),
            jax.ShapeDtypeStruct((total, kv_width), BF),
        ],
        compiler_params=pltpu.CompilerParams(vmem_limit_bytes=32 * 2**20),
        cost_estimate=pl.CostEstimate(flops=12 * 10**9, bytes_accessed=total * query_width * 10, transcendentals=total * total * 2),
        name="attention_fwd",
    )(doc_col, doc_row, qkv, qkv, cos, sin)


def attention_backward(groups, doc_col, doc_row, qrot, keys, values, lse, up, cos, sin):
    total = qrot.shape[0]
    return pl.pallas_call(
        functools.partial(attention_bwd_kernel, groups),
        out_shape=jax.ShapeDtypeStruct((total, qrot.shape[1] + keys.shape[1]), BF),
        scratch_shapes=[pltpu.VMEM(keys.shape, F32), pltpu.VMEM(keys.shape, F32)],
        compiler_params=pltpu.CompilerParams(vmem_limit_bytes=32 * 2**20),
        cost_estimate=pl.CostEstimate(flops=16 * 10**9, bytes_accessed=total * qrot.shape[1] * 10, transcendentals=total * total * 2),
        name="attention_bwd",
    )(doc_col, doc_row, qrot, keys, values, lse, up, cos, sin)


def swap(values, mask):
    count = lax.axis_size("fsdp")
    return lax.ppermute(values, "fsdp", [(i, i ^ mask) for i in range(count)])


def high_bits():
    count = lax.axis_size("fsdp")
    bits = []
    while 4 << len(bits) < count:
        bits.append(4 << len(bits))
    return bits


def block_masks(count):
    quarter = count // 4
    places = jnp.arange(count, dtype=jnp.int32)
    return places // quarter + 4 * (places % quarter)


def gather_rows(shard, order):
    block = shard
    for bit in high_bits():
        block = jnp.concatenate([block, swap(block, bit)], axis=0)
    size = block.shape[0]
    near = swap(block, 2 if order else 1)
    far = swap(jnp.concatenate([block, near], axis=0), 1 if order else 2)
    if order:
        return jnp.concatenate([block, far[:size], near, far[size:]], axis=0)
    return jnp.concatenate([block, near, far], axis=0)


def scatter_rows(grads, order):
    size = grads.shape[0] // 4
    if order:
        sent = jnp.concatenate([grads[size : 2 * size], grads[3 * size :]], axis=0)
        kept = jnp.concatenate([grads[:size], grads[2 * size : 3 * size]], axis=0)
    else:
        sent, kept = grads[2 * size :], grads[: 2 * size]
    total = kept.astype(F32) + swap(sent, 1 if order else 2).astype(F32)
    total = total[:size] + swap(total[size:].astype(BF), 2 if order else 1).astype(F32)
    for bit in reversed(high_bits()):
        half = total.shape[0] // 2
        total = total[:half] + swap(total[half:].astype(BF), bit).astype(F32)
    return total


def sum_everywhere(values, names):
    if "fsdp" in names:
        for bit in [1, 2] + high_bits():
            values = values + swap(values, bit)
    if "tensor" in names:
        values = tensor_sum(values)
    return values


def tensor_swap(values):
    return lax.ppermute(values, "tensor", [(0, 1), (1, 0)])


def tensor_sum(values):
    if lax.axis_size("tensor") == 2:
        return values + tensor_swap(values)
    return lax.psum(values, "tensor")


def tensor_sum_low(values):
    if lax.axis_size("tensor") == 2:
        return values + tensor_swap(values.astype(BF)).astype(F32)
    return lax.psum(values, "tensor")


def tensor_gather(values):
    if lax.axis_size("tensor") == 2:
        other = tensor_swap(values)
        first = lax.axis_index("tensor") == 0
        return jnp.concatenate([jnp.where(first, values, other), jnp.where(first, other, values)], axis=0)
    return lax.all_gather(values, "tensor", axis=0, tiled=True)


def tensor_scatter(values):
    if lax.axis_size("tensor") == 2:
        half = values.shape[0] // 2
        first = lax.axis_index("tensor") == 0
        mine = jnp.where(first, values[:half], values[half:])
        other = jnp.where(first, values[half:], values[:half])
        return mine.astype(F32) + tensor_swap(other.astype(BF)).astype(F32)
    return lax.psum_scatter(values.astype(BF), "tensor", scatter_dimension=0, tiled=True).astype(F32)


def pad_to(values, size, axis=-1):
    pads = [(0, 0)] * values.ndim
    pads[axis] = (0, size - values.shape[axis])
    return jnp.pad(values, pads) if size > values.shape[axis] else values


def norm_scale(values):
    return lax.rsqrt(jnp.mean(values * values, axis=-1, keepdims=True) + EPS)


def rotation_tables(place):
    half = HEAD_SIZE // 2
    rates = jnp.exp(jnp.arange(half, dtype=F32) * (-2.0 * math.log(THETA) / HEAD_SIZE))
    angles = place[:, None] * rates[None, :]
    cos, sin = jnp.cos(angles), jnp.sin(angles)
    return jnp.concatenate([cos] * 4, axis=1), jnp.concatenate([-sin, sin, -sin, sin], axis=1)


def body(
    layer_input, doc_ids, input_gain, mixer_weight, state_weight, step_weight, conv_weight, conv_bias, state_conv,
    state_conv_bias, step_bias, decay_log, skip_gain, mixer_gain, mixer_proj, query_weight, keyval_projection,
    attention_proj, second_gain, gate_up, down_proj, cotangent,
):
    tensor_count = lax.axis_size("tensor")
    tensor_index = lax.axis_index("tensor")
    fsdp_count = lax.axis_size("fsdp")
    fsdp_index = lax.axis_index("fsdp")
    own_rows, hidden = layer_input.shape
    unit = state_weight.shape[0]
    seq_count, seq_length = doc_ids.shape
    total = seq_count * seq_length
    heads = step_bias.shape[0]
    width = conv_weight.shape[1]
    wide = -(-width // LANES) * LANES
    query_width = query_weight.shape[1]
    query_wide = -(-query_width // LANES) * LANES
    per_group = QUERY_HEADS // KEYVAL_HEADS
    query_heads = query_width // HEAD_SIZE
    kv_heads = max(1, query_heads // per_group)
    kv_leading = tensor_index * query_heads // per_group
    states2 = state_weight.shape[1]
    ffn = down_proj.shape[0]

    own_keyval = lax.dynamic_slice_in_dim(keyval_projection, kv_leading * HEAD_SIZE, kv_heads * HEAD_SIZE, 2)
    own_keyval = own_keyval.reshape(unit, 2, kv_heads, HEAD_SIZE).transpose(0, 2, 1, 3).reshape(unit, 2 * kv_heads * HEAD_SIZE)
    kv_wide = 2 * kv_heads * HEAD_SIZE
    low = lambda v: v.astype(BF)
    pack = lambda parts: jnp.concatenate([low(v) for v in parts], axis=1)
    ssm_wide, qkv_wide = wide + states2 + LANES, query_wide + kv_wide
    first = gather_rows(
        pack([
            pad_to(mixer_weight[:, 1, :], wide), state_weight, pad_to(step_weight, LANES),
            pad_to(query_weight, query_wide), own_keyval,
        ]),
        0,
    )
    full_ssm, full_qkv = first[:, :ssm_wide], first[:, ssm_wide:]
    after = gather_rows(
        pack([pad_to(mixer_weight[:, 0, :], wide), pad_to(mixer_proj.T, wide), pad_to(attention_proj.T, query_wide)]), 1
    )
    full_z, full_proj, full_attention = after[:, :wide], after[:, wide : 2 * wide], after[:, 2 * wide :]
    full_gate_up = gather_rows(low(gate_up).reshape(unit, 2 * ffn), 0)
    full_down = gather_rows(low(down_proj).T, 1)

    masks = block_masks(fsdp_count)
    features = jnp.arange(hidden, dtype=jnp.int32)
    source = (masks[features // unit] ^ fsdp_index) * unit + features % unit
    turn = (features[:, None] == source[None, :]).astype(BF)
    turn_back = (source[:, None] == features[None, :]).astype(BF)
    tokens = tensor_gather(low(plain_dot(layer_input, turn))).astype(F32)
    upstream = tensor_gather(low(plain_dot(cotangent, turn)))
    gains = jnp.dot(
        jnp.stack([input_gain, second_gain]), turn.astype(F32), precision=lax.Precision.HIGHEST, preferred_element_type=F32
    )
    first_gain, second_gain_turned = gains[0:1], gains[1:2]

    docs = (doc_ids + jnp.arange(seq_count, dtype=jnp.int32)[:, None] * seq_length).reshape(total)
    place = (jnp.arange(total, dtype=jnp.int32) - jnp.sum((docs[None, :] < docs[:, None]).astype(jnp.int32), axis=1)).astype(F32)
    cos, sin = rotation_tables(place)
    feats = token_features(docs, CHUNK)
    doc_col, doc_row = docs.astype(F32)[:, None], docs.astype(F32)[None, :]
    taps = jnp.concatenate(
        [conv_weight, conv_bias[None], jnp.repeat(skip_gain, width // heads)[None], jnp.zeros((2, width), F32)], axis=0
    )
    taps = pad_to(taps, wide)
    state_taps = jnp.concatenate([state_conv, state_conv_bias[None], jnp.zeros((3, states2), F32)], axis=0)
    head_rows = pad_to(pad_to(jnp.stack([step_bias, -jnp.exp(decay_log)]), 8, 0), LANES)
    gain_row = pad_to(mixer_gain[None], wide)

    first_scale = norm_scale(tokens)
    normed = low(tokens * first_scale * first_gain)
    ssm_in = plain_dot(normed, full_ssm)
    qkv_in = plain_dot(normed, full_qkv)
    gate_z = plain_dot(normed, full_z)
    scan, gated_low, squares, states = mamba_forward(feats, doc_row, ssm_in, gate_z, taps, state_taps, head_rows, gain_row, wide, states2)
    attended, log_sums, query_rot, keys, values = attention_forward(kv_heads, doc_col, doc_row, qkv_in, cos, sin, query_wide)
    squares = tensor_sum(squares.reshape(-1, LANES)).reshape(total, 1)
    gated_scale = lax.rsqrt(squares / DSSM + EPS)
    branch = gated_scale * right_dot(gated_low, full_proj) + right_dot(attended, full_attention)
    middle = tokens + tensor_sum_low(branch)
    second_scale = norm_scale(middle)
    second = low(middle * second_scale * second_gain_turned)
    gate_vals = plain_dot(second, full_gate_up)
    gate_part, up_part = gate_vals[:, :ffn], gate_vals[:, ffn:]
    gate_sigmoid = jax.nn.sigmoid(gate_part)
    active = low(gate_part * gate_sigmoid * up_part)
    ffn_out = tensor_scatter(low(right_dot(active, full_down)))
    own = lambda v: lax.dynamic_slice_in_dim(v, tensor_index * own_rows, own_rows, 0)
    layer_output = low(plain_dot(low(own(middle) + ffn_out), turn_back))

    grad_down = low(left_dot(upstream, active))
    active_grad = plain_dot(upstream, full_down)
    gate_grad = active_grad * up_part * gate_sigmoid * (1.0 + gate_part * (1.0 - gate_sigmoid))
    up_grad = active_grad * gate_part * gate_sigmoid
    gu_grad = jnp.concatenate([low(gate_grad), low(up_grad)], axis=-1)
    grad_gate_up = low(left_dot(second, gu_grad))
    second_grad = tensor_sum_low(right_dot(gu_grad, full_gate_up))
    weighted = second_grad * second_gain_turned
    inner = jnp.mean(weighted * middle, axis=-1, keepdims=True)
    middle_grad = upstream.astype(F32) + second_scale * weighted - middle * second_scale**3 * inner
    second_gain_part = jnp.sum(second_grad * middle * second_scale, axis=0) * (1.0 / tensor_count)
    branch_low = low(middle_grad)

    norm_grad = low(plain_dot(branch_low, full_proj))
    attended_grad = low(plain_dot(branch_low, full_attention))
    inner_sums = tensor_sum(jnp.sum(norm_grad.astype(F32) * gated_low.astype(F32), axis=-1).reshape(-1, LANES)).reshape(total, 1)
    back_feats = jnp.concatenate([feats, gated_scale, gated_scale**3 * (inner_sums / DSSM)], axis=1)
    grad_proj = low(left_dot(low(gated_scale * branch_low), gated_low))
    grad_attention = low(left_dot(branch_low, attended))
    gate_z_grad, ssm_grad, sums, state_sums, head_sums = mamba_backward(
        back_feats, doc_col, doc_row, ssm_in, gate_z, scan, states, norm_grad, taps, state_taps, head_rows, gain_row, wide, states2
    )
    qkv_grad = attention_backward(kv_heads, doc_col, doc_row, query_rot, keys, values, log_sums, attended_grad, cos, sin)
    grad_z = low(left_dot(normed, gate_z_grad))
    grad_ssm = low(left_dot(normed, ssm_grad))
    grad_qkv = low(left_dot(normed, qkv_grad))
    normed_part = right_dot(gate_z_grad, full_z) + right_dot(ssm_grad, full_ssm) + right_dot(qkv_grad, full_qkv)
    input_gain_part = jnp.sum(normed_part * tokens * first_scale, axis=0)
    normed_grad = tensor_scatter(low(normed_part))
    own_tokens, own_scale = own(tokens), own(first_scale)
    weighted = normed_grad * first_gain
    inner = jnp.mean(weighted * own_tokens, axis=-1, keepdims=True)
    input_grad = own(middle_grad) + own_scale * weighted - own_tokens * own_scale**3 * inner
    turned = plain_dot(split_lanes(input_grad, 0), turn_back)
    input_grad = turned[:own_rows] + turned[own_rows:]

    sum_gate_up = scatter_rows(grad_gate_up, 0).reshape(unit, 2, ffn)
    sum_down = scatter_rows(grad_down, 1).T
    sum_out = scatter_rows(jnp.concatenate([grad_proj, grad_attention], axis=1), 0)
    sum_z = scatter_rows(grad_z, 1)[:, :width]
    sum_ssm = scatter_rows(grad_ssm, 0)
    sum_qkv = scatter_rows(grad_qkv, 1)
    keyval_sum = sum_qkv[:, query_wide:].reshape(unit, kv_heads, 2, HEAD_SIZE).transpose(0, 2, 1, 3).reshape(unit, 2, kv_heads * HEAD_SIZE)
    keyval_sum = lax.dynamic_update_slice_in_dim(
        jnp.zeros((unit, 2, KEYVAL_HEADS * HEAD_SIZE), F32), keyval_sum, kv_leading * HEAD_SIZE, 2
    ).reshape(unit, 2 * KEYVAL_HEADS * HEAD_SIZE)
    shared = tensor_sum(jnp.concatenate([sum_ssm[:, wide : wide + states2], keyval_sum], axis=1))

    def turn_row(row):
        blocks = (jnp.arange(fsdp_count, dtype=jnp.int32)[:, None] == (masks ^ fsdp_index)[None, :]).astype(F32)
        return exact_mm(blocks, row.reshape(fsdp_count, unit)).reshape(1, hidden)

    split_sums = sum_everywhere(jnp.concatenate([sums, head_sums], axis=1), ("fsdp",))
    sums, head_sums = split_sums[:, :wide], split_sums[:, wide:]
    state_sums = sum_everywhere(
        jnp.concatenate([state_sums, pad_to(turn_row(second_gain_part).reshape(-1, states2), 8, 0)], axis=0), ("fsdp", "tensor")
    )
    second_gain_sum = state_sums[8 : 8 + hidden // states2].reshape(hidden)
    input_gain_sum = sum_everywhere(turn_row(input_gain_part).reshape(-1, LANES), ("fsdp", "tensor")).reshape(hidden)
    return (
        layer_output,
        input_grad,
        input_gain_sum,
        jnp.stack([sum_z, sum_ssm[:, :width]], axis=1),
        shared[:, :states2],
        sum_ssm[:, wide + states2 : wide + states2 + heads],
        sums[0:4, :width],
        sums[4, :width],
        state_sums[0:4],
        state_sums[4],
        head_sums[0, :heads],
        head_sums[1, :heads],
        jnp.sum(sums[5, :width].reshape(heads, -1), axis=1),
        sums[6, :width],
        sum_out[:, :width].T,
        sum_qkv[:, :query_width],
        shared[:, states2:].reshape(unit, 2, KEYVAL_HEADS * HEAD_SIZE),
        sum_out[:, wide : wide + query_width].T,
        second_gain_sum,
        sum_gate_up,
        sum_down,
    )


def solution(mesh):
    placed = (
        P(("fsdp", "tensor"), None),
        P("fsdp", None),
        P(),
        P("fsdp", None, "tensor"),
        P("fsdp", None),
        P("fsdp", "tensor"),
        P(None, "tensor"),
        P("tensor"),
        P(),
        P(),
        P("tensor"),
        P("tensor"),
        P("tensor"),
        P("tensor"),
        P("tensor", "fsdp"),
        P("fsdp", "tensor"),
        P("fsdp", None, None),
        P("tensor", "fsdp"),
        P(),
        P("fsdp", None, "tensor"),
        P("tensor", "fsdp"),
        P(("fsdp", "tensor"), None),
    )
    return jax.shard_map(
        body,
        mesh=mesh,
        in_specs=placed,
        out_specs=(
            P(("fsdp", "tensor"), None),
            P(("fsdp", "tensor"), None),
            P(),
            P("fsdp", None, "tensor"),
            P("fsdp", None),
            P("fsdp", "tensor"),
            P(None, "tensor"),
            P("tensor"),
            P(),
            P(),
            P("tensor"),
            P("tensor"),
            P("tensor"),
            P("tensor"),
            P("tensor", "fsdp"),
            P("fsdp", "tensor"),
            P("fsdp", None, None),
            P("tensor", "fsdp"),
            P(),
            P("fsdp", None, "tensor"),
            P("tensor", "fsdp"),
        ),
        check_vma=False,
    )
```

time: 2090 us -> 656 us (0.31)
  waiting for transfers between devices: 828 us -> 267 us
  local copies, waits for them, and re-layouts: 447 us -> 82.5 us
  blocking collectives: 259 us -> 0 us
  matrix products: 284 us -> 87.9 us
  other arithmetic: 229 us -> 90.9 us
  starting transfers between devices: 1.79 us -> 59.2 us
  Pallas kernels: 0 us -> 56.2 us
    reduce_scatter x8 -> x0, waiting for transfers between devices: 304 us -> none  [the longest x1 125 us: send_mixer(): lax.psum_scatter(proj_grad.astype(jnp.bfloat16), 'fsdp', scatter_dimensio...]
    ppermute x0 -> x63, waiting for transfers between devices: none -> 267 us  [the longest x52 266 us: swap(): return lax.ppermute(values, 'fsdp', [(i, i ^ mask) for i in range(count)])]
    dynamic_update_slice x29 -> x1, local copies, waits for them, and re-layouts: 219 us -> 1.21 us  [body(): lax.dynamic_update_slice_in_dim(jnp.zeros((unit, 2, KEYVAL_HEADS * HEAD_S...]
    all_gather x5 -> x0, blocking collectives: 209 us -> none  [the longest x1 46.5 us: body(): lax.all_gather(keyval_projection.astype(jnp.bfloat16), 'fsdp', axis=0, ti...]
    dot_general x143 -> x28, matrix products: 284 us -> 87.9 us  [the longest x11 36.9 us: plain_dot(): return jnp.dot(left_side, right_side, preferred_element_type=F32)]
    unnamed x21 -> x0, waiting for transfers between devices: 189 us -> none
    psum x1 -> x0, waiting for transfers between devices: 183 us -> none  [body(): lax.psum((grad_shared[:, :state_cols], keyval_full, state_conv_part, stat...]
    all_gather x8 -> x0, waiting for transfers between devices: 152 us -> none  [the longest x1 74.4 us: body(): lax.all_gather(gate_up.astype(jnp.bfloat16), 'fsdp', axis=0, tiled=True)]
  transfers between devices with their start and end apart: 19 -> 63, of which waited for: 14 -> 30; matrix products, arithmetic and copies ran while one was open for 44% -> 29% of each run, Pallas kernels for 0% -> 9%
where the time goes in v1:
time: 656 us; the launch traced here: 647 us
  waiting for transfers between devices  267 us (41%)
  other arithmetic  90.9 us (14%)
  matrix products  87.9 us (13%)
  local copies, waits for them, and re-layouts  82.5 us (13%)
  starting transfers between devices  59.2 us (9%)
  Pallas kernels  56.2 us (9%)
    ppermute x52, waiting for transfers between devices, swap(): return lax.ppermute(values, 'fsdp', [(i, i ^ mask) for i in range(count)])  266 us
    ppermute x52, starting transfers between devices, swap(): return lax.ppermute(values, 'fsdp', [(i, i ^ mask) for i in range(count)])  57.2 us
    unnamed x262, local copies, waits for them, and re-layouts  43 us
    dot_general x11, matrix products, plain_dot(): return jnp.dot(left_side, right_side, preferred_element_type=F32)  36.9 us
    pallas_call x1, Pallas kernels, mamba_backward(): pl.pallas_call(mamba_bwd_kernel, grid=(count,), in_specs=[block(feats.sha...  28.8 us
    dot_general x7, matrix products, right_dot(): lax.dot_general(left_side, right_side, (((1,), (1,)), ((), ())), preferre...  27.4 us
    dot_general x7, matrix products, left_dot(): lax.dot_general(left_side, right_side, (((0,), (0,)), ((), ())), preferre...  22 us
  transfers between devices with their start and end apart: 63, of which 30 were waited for; matrix products, arithmetic and copies ran while one was open for 29% of the time, Pallas kernels for 9%

profile of v1, /device:TPU:0, one launch (start us, length us, event | category | flops | bytes accessed | tf_op | source)
XLA Modules:
  0.0 647.0 jit_solution(5617692035354918129)
XLA Ops:
  1.6 4.5 compare_select_fusion.1
  6.2 5.8 fusion.59
  48.2 4.9 stack.55.feats_ref
  72.7 20.5 %collective-permute-done.16 = bf16[128,1024]{1,0:T(8,128)(2,1)S(1)} collective-permute-done((bf16[128,1024]{1,0:T(8,128)(2,1)S(1)}, bf16[128,1024]{1,0:T(8,128)(2,1)S(1)}, u32[]{:S(2)}, u32[]{:S(2)}) %collective-permute-start.16) | collective-permute-done | bytes 262176 | tf_op jit(solution)/shard_map/ppermute | solution.py:504
  95.0 17.9 %collective-permute-done.2 = bf16[128,1536]{1,0:T(8,128)(2,1)S(1)} collective-permute-done((bf16[128,1536]{1,0:T(8,128)(2,1)S(1)}, bf16[128,1536]{1,0:T(8,128)(2,1)S(1)}, u32[]{:S(2)}, u32[]{:S(2)}) %collective-permute-start.2) | collective-permute-done | bytes 393248 | tf_op jit(solution)/shard_map/ppermute | solution.py:504
  115.8 6.9 %collective-permute-done.6 = bf16[128,1792]{1,0:T(8,128)(2,1)S(1)} collective-permute-done((bf16[128,1792]{1,0:T(8,128)(2,1)S(1)}, bf16[128,1792]{1,0:T(8,128)(2,1)S(1)}, u32[]{:S(2)}, u32[]{:S(2)}) %collective-permute-start.6) | collective-permute-done | bytes 458784 | tf_op jit(solution)/shard_map/ppermute | solution.py:504
  125.5 8.2 %collective-permute-done.12 = bf16[128,2048]{1,0:T(8,128)(2,1)S(1)} collective-permute-done((bf16[128,2048]{1,0:T(8,128)(2,1)S(1)}, bf16[128,2048]{1,0:T(8,128)(2,1)S(1)}, u32[]{:S(2)}, u32[]{:S(2)}) %collective-permute-start.12) | collective-permute-done | bytes 524320 | tf_op jit(solution)/shard_map/ppermute | solution.py:504
  144.4 12.6 %collective-permute-done.7 = bf16[256,1792]{1,0:T(8,128)(2,1)S(1)} collective-permute-done((bf16[256,1792]{1,0:T(8,128)(2,1)S(1)}, bf16[256,1792]{1,0:T(8,128)(2,1)S(1)}, u32[]{:S(2)}, u32[]{:S(2)}) %collective-permute-start.7) | collective-permute-done | bytes 917536 | tf_op jit(solution)/shard_map/ppermute | solution.py:504
  165.6 25.1 %collective-permute-done.4 = bf16[512,1536]{1,0:T(8,128)(2,1)S(1)} collective-permute-done((bf16[512,1536]{1,0:T(8,128)(2,1)S(1)}, bf16[512,1536]{1,0:T(8,128)(2,1)S(1)}, u32[]{:S(2)}, u32[]{:S(2)}) %collective-permute-start.4) | collective-permute-done | bytes 1572896 | tf_op jit(solution)/shard_map/ppermute | solution.py:504
  195.5 7.2 %attention_fwd.1 = (bf16[1024,256]{1,0:T(8,128)(2,1)S(1)}, f32[1024,128]{1,0:T(8,128)S(1)}, bf16[1024,256]{1,0:T(8,128)(2,1)S(1)}, bf16[1024,128]{1,0:T(8,128)(2,1)S(1)}, bf16[1024,128]{1,0:T(8,128)(2,1)S(1)}) custom-call(f32[1024,1]{1,0:T(8,128)S(1)} %convert_element_type.352.docs_col_ref, f32[1,1024]{1,0:T(1,128)S(1)} %convert_element_type.361.docs_ref, ...), custom_call_target="tpu_custom_call" | custom-call | flops 12000000000 | bytes 2621440 | tf_op jit(solution)/shard_map/attention_fwd/pallas_call | solution.py:474
  202.7 20.0 %collective-permute-done.8 = bf16[512,1792]{1,0:T(8,128)(2,1)S(1)} collective-permute-done((bf16[512,1792]{1,0:T(8,128)(2,1)S(1)}, bf16[512,1792]{1,0:T(8,128)(2,1)S(1)}, u32[]{:S(2)}, u32[]{:S(2)}) %collective-permute-start.8) | collective-permute-done | bytes 1835040 | tf_op jit(solution)/shard_map/ppermute | solution.py:504
  226.8 10.9 %mamba_fwd.1 = (f32[1024,768]{1,0:T(8,128)S(1)}, bf16[1024,768]{1,0:T(8,128)(2,1)S(1)}, f32[1024,1]{1,0:T(8,128)S(1)}, bf16[8,128,768]{2,1,0:T(8,128)(2,1)S(1)}) custom-call(f32[1024,9]{1,0:T(8,128)S(1)} %stack.55.feats_ref, f32[1,1024]{1,0:T(1,128)S(1)} %convert_element_type.361.docs_ref, ...), custom_call_target="tpu_custom_call" | custom-call | flops 20000000000 | bytes 15728640 | tf_op jit(solution)/shard_map/mamba_fwd/pallas_call | solution.py:308
  267.4 8.0 %fusion.80 = f32[1024,2048]{1,0:T(8,128)S(1)} fusion(bf16[1024,2048]{1,0:T(8,128)(2,1)} %copy-done.89, f32[1024,1024]{1,0:T(8,128)S(1)} %get-tuple-element.166, f32[1024]{0:T(1024)S(1)} %bitcast.148, f32[1024]{0:T(1024)S(1)} %get-tuple-element.212), kind=kOutput, calls=%fused_computation.305 | convolution fusion | flops 4298113024 | bytes 16785408 | tf_op jit(solution)/shard_map/dot_general | solution.py:33
  275.4 6.8 %multiply_convert_fusion.2 = (bf16[1024,1024]{1,0:T(8,128)(2,1)}, bf16[1024,1024]{1,0:T(8,128)(2,1)}, bf16[1024,1024]{1,0:T(8,128)(2,1)S(1)}) fusion(f32[1024,2048]{1,0:T(8,128)S(1)} %fusion.80, bf16[1024,1024]{1,0:T(8,128)(2,1)S(1)} %copy-done.96, bf16[512,1024]{1,0:T(8,128)(2,1)S(1)} %copy-done.50, bf16[512,1024]{1,0:T(8,128)(2,1)S(1)} %copy-done.48), kind=kOutput, calls=%fused_computation.10 | convolution fusion | flops 2168455168 | bytes 18874368 | tf_op jit(solution)/shard_map/dot_general | solution.py:33
  290.4 9.4 %fusion.91 = (bf16[1024,1024]{1,0:T(8,128)(2,1)}, f32[1024,1024]{1,0:T(8,128)S(1)}) fusion(bf16[1024,2048]{1,0:T(8,128)(2,1)} %copy-done.89, bf16[1024,1024]{1,0:T(8,128)(2,1)} %get-tuple-element.168, bf16[1024,1024]{1,0:T(8,128)(2,1)} %get-tuple-element.167), kind=kOutput, calls=%fused_computation.316 | convolution fusion | flops 4304404480 | bytes 14680064 | tf_op jit(solution)/shard_map/dot_general | solution.py:29
  299.8 12.9 %collective-permute-done.59 = bf16[512,1024]{1,0:T(8,128)(2,1)} collective-permute-done((bf16[512,1024]{1,0:T(8,128)(2,1)}, bf16[512,1024]{1,0:T(8,128)(2,1)}, u32[]{:S(2)}, u32[]{:S(2)}) %collective-permute-start.59) | collective-permute-done | bytes 1048608 | tf_op jit(solution)/shard_map/ppermute | solution.py:504
  318.3 9.7 %collective-permute-done.60 = bf16[256,1024]{1,0:T(8,128)(2,1)S(1)} collective-permute-done((bf16[256,1024]{1,0:T(8,128)(2,1)S(1)}, bf16[256,1024]{1,0:T(8,128)(2,1)S(1)}, u32[]{:S(2)}, u32[]{:S(2)}) %collective-permute-start.60) | collective-permute-done | bytes 524320 | tf_op jit(solution)/shard_map/ppermute | solution.py:504
  328.4 5.4 convolution_convert_fusion.1
  334.7 7.1 %collective-permute-done.61 = bf16[128,1024]{1,0:T(8,128)(2,1)S(1)} collective-permute-done((bf16[128,1024]{1,0:T(8,128)(2,1)S(1)}, bf16[128,1024]{1,0:T(8,128)(2,1)S(1)}, u32[]{:S(2)}, u32[]{:S(2)}) %collective-permute-start.61) | collective-permute-done | bytes 262176 | tf_op jit(solution)/shard_map/ppermute | solution.py:504
  342.1 4.0 fusion.23
  349.3 3.9 fusion.82
  362.9 17.5 %collective-permute-done.55 = bf16[512,2048]{1,0:T(8,128)(2,1)S(1)} collective-permute-done((bf16[512,2048]{1,0:T(8,128)(2,1)S(1)}, bf16[512,2048]{1,0:T(8,128)(2,1)S(1)}, u32[]{:S(2)}, u32[]{:S(2)}) %collective-permute-start.55) | collective-permute-done | bytes 2097184 | tf_op jit(solution)/shard_map/ppermute | solution.py:504
  390.4 9.3 %attention_bwd.1 = bf16[1024,384]{1,0:T(8,128)(2,1)S(1)} custom-call(f32[1024,1]{1,0:T(8,128)S(1)} %convert_element_type.352.docs_col_ref, f32[1,1024]{1,0:T(1,128)S(1)} %convert_element_type.361.docs_ref, bf16[1024,256]{1,0:T(8,128)(2,1)S(1)} %copy-done.19, bf16[1024,128]{1,0:T(8,128)(2,1)S(1)} %copy-done.21, bf16[1024,128]{1,0:T(8,128)(2,1)S(1)} %copy-done.23, ...), custom_call_target="tpu_custom_call" | custom-call | flops 16000000000 | bytes 2621440 | tf_op jit(solution)/shard_map/attention_bwd/pallas_call | solution.py:492
  407.0 4.0 concatenate.190.feats_ref
  420.0 28.8 %mamba_bwd.1 = (bf16[1024,768]{1,0:T(8,128)(2,1)S(1)}, bf16[1024,1152]{1,0:T(8,128)(2,1)S(1)}, f32[8,768]{1,0:T(8,128)S(1)}, f32[8,256]{1,0:T(8,128)S(1)}, f32[8,128]{1,0:T(8,128)S(1)}) custom-call(f32[1024,11]{1,0:T(8,128)S(1)} %concatenate.190.feats_ref, f32[1024,1]{1,0:T(8,128)S(1)} %convert_element_type.352.docs_col_ref, ...), custom_call_target="tpu_custom_call" | custom-call | flops 35000000512 | bytes 18874368 | tf_op jit(solution)/shard_map/mamba_bwd/pallas_call | solution.py:343
  448.9 4.7 convolution_convert_fusion
  475.9 4.1 collective-permute-start.26
  503.9 43.3 %collective-permute-done.38 = bf16[256,384]{1,0:T(8,128)(2,1)S(1)} collective-permute-done((bf16[256,384]{1,0:T(8,128)(2,1)S(1)}, bf16[256,384]{1,0:T(8,128)(2,1)S(1)}, u32[]{:S(2)}, u32[]{:S(2)}) %collective-permute-start.38) | collective-permute-done | bytes 196640 | tf_op jit(solution)/shard_map/ppermute | solution.py:504
  549.8 4.6 collective-permute-done.39
  579.4 20.6 %collective-permute-done.31 = bf16[128,768]{1,0:T(8,128)(2,1)S(1)} collective-permute-done((bf16[128,768]{1,0:T(8,128)(2,1)S(1)}, bf16[128,768]{1,0:T(8,128)(2,1)S(1)}, u32[]{:S(2)}, u32[]{:S(2)}) %collective-permute-start.31) | collective-permute-done | bytes 196640 | tf_op jit(solution)/shard_map/ppermute | solution.py:504
  607.3 9.3 %collective-permute-done.34 = bf16[256,1152]{1,0:T(8,128)(2,1)S(1)} collective-permute-done((bf16[256,1152]{1,0:T(8,128)(2,1)S(1)}, bf16[256,1152]{1,0:T(8,128)(2,1)S(1)}, u32[]{:S(2)}, u32[]{:S(2)}) %collective-permute-start.34) | collective-permute-done | bytes 589856 | tf_op jit(solution)/shard_map/ppermute | solution.py:504
  622.2 10.6 %collective-permute-done.54 = bf16[64,1024]{0,1:T(8,128)(2,1)S(1)} collective-permute-done((bf16[64,1024]{0,1:T(8,128)(2,1)S(1)}, bf16[64,1024]{0,1:T(8,128)(2,1)S(1)}, u32[]{:S(2)}, u32[]{:S(2)}) %collective-permute-start.54) | collective-permute-done | bytes 131104 | tf_op jit(solution)/shard_map/ppermute | solution.py:504
  (601 shorter events, 275.0 us)
Async XLA Ops:
  14.5 127.2 %collective-permute-start = (bf16[512,1024]{1,0:T(8,128)(2,1)}, bf16[512,1024]{1,0:T(8,128)(2,1)}, u32[]{:S(2)}, u32[]{:S(2)}) collective-permute-start(bf16[512,1024]{1,0:T(8,128)(2,1)} %fusion.32), channel_id=1, source_target_pairs={{0,1},{1,0},{2,3},{3,2},{4,5},{5,4},{6,7},{7,6},{8,9},{9,8},{10,11... | collective-permute-start | bytes 3145736 | tf_op jit(solution)/shard_map/ppermute | solution.py:558
  16.5 47.7 %collective-permute-start.5 = (bf16[64,1792]{1,0:T(8,128)(2,1)}, bf16[64,1792]{1,0:T(8,128)(2,1)}, u32[]{:S(2)}, u32[]{:S(2)}) collective-permute-start(bf16[64,1792]{1,0:T(8,128)(2,1)} %get-tuple-element.188), channel_id=1, source_target_pairs={{0,8},{2,10},{4,12},{6,14},{8,0},{10,2},{12,4},{14,6},{16,24},{18,... | collective-permute-start | bytes 688136 | tf_op jit(solution)/shard_map/ppermute | solution.py:504
  22.7 36.4 %collective-permute-start.1 = (bf16[64,1536]{1,0:T(8,128)(2,1)}, bf16[64,1536]{1,0:T(8,128)(2,1)}, u32[]{:S(2)}, u32[]{:S(2)}) collective-permute-start(bf16[64,1536]{1,0:T(8,128)(2,1)} %get-tuple-element.202), channel_id=1, source_target_pairs={{0,8},{2,10},{4,12},{6,14},{8,0},{10,2},{12,4},{14,6},{16,24},{18,... | collective-permute-start | bytes 589832 | tf_op jit(solution)/shard_map/ppermute | solution.py:504
  22.9 44.1 %collective-permute-start.11 = (bf16[64,2048]{1,0:T(8,128)(2,1)S(1)}, bf16[64,2048]{1,0:T(8,128)(2,1)}, u32[]{:S(2)}, u32[]{:S(2)}) collective-permute-start(bf16[64,2048]{1,0:T(8,128)(2,1)S(1)} %bitcast.123), channel_id=1, source_target_pairs={{0,8},{2,10},{4,12},{6,14},{8,0},{10,2},{12,4},{14,6},{16,24},{18,... | collective-permute-start | bytes 786440 | tf_op jit(solution)/shard_map/ppermute | solution.py:504
  25.8 30.7 %collective-permute-start.15 = (bf16[64,1024]{1,0:T(8,128)(2,1)}, bf16[64,1024]{1,0:T(8,128)(2,1)}, u32[]{:S(2)}, u32[]{:S(2)}) collective-permute-start(bf16[64,1024]{1,0:T(8,128)(2,1)} %get-tuple-element.164), channel_id=1, source_target_pairs={{0,8},{2,10},{4,12},{6,14},{8,0},{10,2},{12,4},{14,6},{16,24},{18,... | collective-permute-start | bytes 393224 | tf_op jit(solution)/shard_map/ppermute | solution.py:504
  56.5 195.6 %collective-permute-start.20 = (bf16[512,1024]{1,0:T(8,128)(2,1)}, bf16[512,1024]{1,0:T(8,128)(2,1)}, u32[]{:S(2)}, u32[]{:S(2)}) collective-permute-start(bf16[512,1024]{1,0:T(8,128)(2,1)} %fusion.31), channel_id=1, source_target_pairs={{0,1},{1,0},{2,3},{3,2},{4,5},{5,4},{6,7},{7,6},{8,9},{9,8},{10,11... | collective-permute-start | bytes 3145736 | tf_op jit(solution)/shard_map/ppermute | solution.py:558
  59.1 34.1 %collective-permute-start.16 = (bf16[128,1024]{1,0:T(8,128)(2,1)S(1)}, bf16[128,1024]{1,0:T(8,128)(2,1)S(1)}, u32[]{:S(2)}, u32[]{:S(2)}) collective-permute-start(bf16[128,1024]{1,0:T(8,128)(2,1)S(1)} %pad_maximum_fusion.25), channel_id=1, source_target_pairs={{0,16},{2,18},{4,20},{6,22},{8,24},{10,26},{12,28},{14,30},{16,0},... | collective-permute-start | bytes 786440 | tf_op jit(solution)/shard_map/ppermute | solution.py:504
  64.2 48.7 %collective-permute-start.2 = (bf16[128,1536]{1,0:T(8,128)(2,1)S(1)}, bf16[128,1536]{1,0:T(8,128)(2,1)S(1)}, u32[]{:S(2)}, u32[]{:S(2)}) collective-permute-start(bf16[128,1536]{1,0:T(8,128)(2,1)S(1)} %pad_maximum_fusion.22), channel_id=1, source_target_pairs={{0,16},{2,18},{4,20},{6,22},{8,24},{10,26},{12,28},{14,30},{16,0},... | collective-permute-start | bytes 1179656 | tf_op jit(solution)/shard_map/ppermute | solution.py:504
  67.1 55.6 %collective-permute-start.6 = (bf16[128,1792]{1,0:T(8,128)(2,1)S(1)}, bf16[128,1792]{1,0:T(8,128)(2,1)S(1)}, u32[]{:S(2)}, u32[]{:S(2)}) collective-permute-start(bf16[128,1792]{1,0:T(8,128)(2,1)S(1)} %pad_maximum_fusion.21), channel_id=1, source_target_pairs={{0,16},{2,18},{4,20},{6,22},{8,24},{10,26},{12,28},{14,30},{16,0},... | collective-permute-start | bytes 1376264 | tf_op jit(solution)/shard_map/ppermute | solution.py:504
  93.2 40.5 %collective-permute-start.12 = (bf16[128,2048]{1,0:T(8,128)(2,1)S(1)}, bf16[128,2048]{1,0:T(8,128)(2,1)S(1)}, u32[]{:S(2)}, u32[]{:S(2)}) collective-permute-start(bf16[128,2048]{1,0:T(8,128)(2,1)S(1)} %pad_maximum_fusion.19), channel_id=1, source_target_pairs={{0,16},{2,18},{4,20},{6,22},{8,24},{10,26},{12,28},{14,30},{16,0},... | collective-permute-start | bytes 1572872 | tf_op jit(solution)/shard_map/ppermute | solution.py:504
  114.0 22.4 %collective-permute-start.3 = (bf16[256,1536]{1,0:T(8,128)(2,1)S(1)}, bf16[256,1536]{1,0:T(8,128)(2,1)S(1)}, u32[]{:S(2)}, u32[]{:S(2)}) collective-permute-start(bf16[256,1536]{1,0:T(8,128)(2,1)S(1)} %pad_maximum_fusion.13), channel_id=1, source_target_pairs={{0,2},{2,0},{4,6},{6,4},{8,10},{10,8},{12,14},{14,12},{16,18},{18,... | collective-permute-start | bytes 2359304 | tf_op jit(solution)/shard_map/ppermute | solution.py:504
  133.8 23.2 %collective-permute-start.7 = (bf16[256,1792]{1,0:T(8,128)(2,1)S(1)}, bf16[256,1792]{1,0:T(8,128)(2,1)S(1)}, u32[]{:S(2)}, u32[]{:S(2)}) collective-permute-start(bf16[256,1792]{1,0:T(8,128)(2,1)S(1)} %pad_maximum_fusion.12), channel_id=1, source_target_pairs={{0,4},{2,6},{4,0},{6,2},{8,12},{10,14},{12,8},{14,10},{16,20},{18,... | collective-permute-start | bytes 2752520 | tf_op jit(solution)/shard_map/ppermute | solution.py:504
  136.4 26.2 %collective-permute-start.13 = (bf16[256,2048]{1,0:T(8,128)(2,1)S(1)}, bf16[256,2048]{1,0:T(8,128)(2,1)S(1)}, u32[]{:S(2)}, u32[]{:S(2)}) collective-permute-start(bf16[256,2048]{1,0:T(8,128)(2,1)S(1)} %pad_maximum_fusion.9), channel_id=1, source_target_pairs={{0,2},{2,0},{4,6},{6,4},{8,10},{10,8},{12,14},{14,12},{16,18},{18,... | collective-permute-start | bytes 3145736 | tf_op jit(solution)/shard_map/ppermute | solution.py:504
  139.1 51.6 %collective-permute-start.4 = (bf16[512,1536]{1,0:T(8,128)(2,1)S(1)}, bf16[512,1536]{1,0:T(8,128)(2,1)S(1)}, u32[]{:S(2)}, u32[]{:S(2)}) collective-permute-start(bf16[512,1536]{1,0:T(8,128)(2,1)S(1)} %pad_maximum_fusion.7), channel_id=1, source_target_pairs={{0,4},{2,6},{4,0},{6,2},{8,12},{10,14},{12,8},{14,10},{16,20},{18,... | collective-permute-start | bytes 4718600 | tf_op jit(solution)/shard_map/ppermute | solution.py:504
  141.7 113.3 %collective-permute-start.18 = (bf16[512,1024]{1,0:T(8,128)(2,1)}, bf16[512,1024]{1,0:T(8,128)(2,1)}, u32[]{:S(2)}, u32[]{:S(2)}) collective-permute-start(bf16[512,1024]{1,0:T(8,128)(2,1)} %pad_maximum_fusion.10), channel_id=1, source_target_pairs={{0,2},{2,0},{4,6},{6,4},{8,10},{10,8},{12,14},{14,12},{16,18},{18,... | collective-permute-start | bytes 3145736 | tf_op jit(solution)/shard_map/ppermute | solution.py:504
  159.2 63.6 %collective-permute-start.8 = (bf16[512,1792]{1,0:T(8,128)(2,1)S(1)}, bf16[512,1792]{1,0:T(8,128)(2,1)S(1)}, u32[]{:S(2)}, u32[]{:S(2)}) collective-permute-start(bf16[512,1792]{1,0:T(8,128)(2,1)S(1)} %pad_maximum_fusion.6), channel_id=1, source_target_pairs={{0,2},{2,0},{4,6},{6,4},{8,10},{10,8},{12,14},{14,12},{16,18},{18,... | collective-permute-start | bytes 5505032 | tf_op jit(solution)/shard_map/ppermute | solution.py:504
  165.1 93.4 %collective-permute-start.14 = (bf16[512,2048]{1,0:T(8,128)(2,1)}, bf16[512,2048]{1,0:T(8,128)(2,1)}, u32[]{:S(2)}, u32[]{:S(2)}) collective-permute-start(bf16[512,2048]{1,0:T(8,128)(2,1)} %pad_maximum_fusion.4), channel_id=1, source_target_pairs={{0,4},{2,6},{4,0},{6,2},{8,12},{10,14},{12,8},{14,10},{16,20},{18,... | collective-permute-start | bytes 6291464 | tf_op jit(solution)/shard_map/ppermute | solution.py:504
  286.8 25.9 %collective-permute-start.59 = (bf16[512,1024]{1,0:T(8,128)(2,1)}, bf16[512,1024]{1,0:T(8,128)(2,1)}, u32[]{:S(2)}, u32[]{:S(2)}) collective-permute-start(bf16[512,1024]{1,0:T(8,128)(2,1)} %pad_maximum_fusion.11), channel_id=1, source_target_pairs={{0,2},{2,0},{4,6},{6,4},{8,10},{10,8},{12,14},{14,12},{16,18},{18,... | collective-permute-start | bytes 3145736 | tf_op jit(solution)/shard_map/ppermute | solution.py:504
  317.5 30.2 %collective-permute-start.21 = (bf16[1024,1024]{1,0:T(8,128)(2,1)}, bf16[1024,1024]{1,0:T(8,128)(2,1)S(1)}, u32[]{:S(2)}, u32[]{:S(2)}) collective-permute-start(bf16[1024,1024]{1,0:T(8,128)(2,1)} %get-tuple-element.239), channel_id=1, source_target_pairs={{0,1},{1,0},{2,3},{3,2},{4,5},{5,4},{6,7},{7,6},{8,9},{9,8},{10,11... | collective-permute-start | bytes 6291464 | tf_op jit(solution)/shard_map/ppermute | solution.py:558
  317.7 24.3 %collective-permute-start.19 = (bf16[512,1024]{1,0:T(8,128)(2,1)S(1)}, bf16[512,1024]{1,0:T(8,128)(2,1)}, u32[]{:S(2)}, u32[]{:S(2)}) collective-permute-start(bf16[512,1024]{1,0:T(8,128)(2,1)S(1)} %broadcast_select_fusion.4), channel_id=1, source_target_pairs={{0,1},{1,0},{2,3},{3,2},{4,5},{5,4},{6,7},{7,6},{8,9},{9,8},{10,11... | collective-permute-start | bytes 3145736 | tf_op jit(solution)/shard_map/ppermute | solution.py:558
  334.0 46.4 %collective-permute-start.55 = (bf16[512,2048]{1,0:T(8,128)(2,1)S(1)}, bf16[512,2048]{1,0:T(8,128)(2,1)S(1)}, u32[]{:S(2)}, u32[]{:S(2)}) collective-permute-start(bf16[512,2048]{1,0:T(8,128)(2,1)S(1)} %slice.541), channel_id=1, source_target_pairs={{0,4},{2,6},{4,0},{6,2},{8,12},{10,14},{12,8},{14,10},{16,20},{18,... | collective-permute-start | bytes 6291464 | tf_op jit(solution)/shard_map/ppermute | solution.py:504
  385.9 179.1 %collective-permute-start.56 = (bf16[256,2048]{1,0:T(8,128)(2,1)}, bf16[256,2048]{1,0:T(8,128)(2,1)}, u32[]{:S(2)}, u32[]{:S(2)}) collective-permute-start(bf16[256,2048]{1,0:T(8,128)(2,1)} %slice.684), channel_id=1, source_target_pairs={{0,2},{2,0},{4,6},{6,4},{8,10},{10,8},{12,14},{14,12},{16,18},{18,... | collective-permute-start | bytes 3145736 | tf_op jit(solution)/shard_map/ppermute | solution.py:504
  387.4 17.3 %collective-permute-start.22 = (f32[8,128]{1,0:T(8,128)S(1)}, f32[8,128]{1,0:T(8,128)S(1)}, u32[]{:S(2)}, u32[]{:S(2)}) collective-permute-start(f32[8,128]{1,0:T(8,128)S(1)} %bitcast.167), channel_id=1, source_target_pairs={{0,1},{1,0},{2,3},{3,2},{4,5},{5,4},{6,7},{7,6},{8,9},{9,8},{10,11... | collective-permute-start | bytes 12296 | tf_op jit(solution)/shard_map/ppermute | solution.py:558
  404.1 95.0 %collective-permute-start.37 = (bf16[512,384]{1,0:T(8,128)(2,1)}, bf16[512,384]{1,0:T(8,128)(2,1)}, u32[]{:S(2)}, u32[]{:S(2)}) collective-permute-start(bf16[512,384]{1,0:T(8,128)(2,1)} %pad_maximum_fusion.24), channel_id=1, source_target_pairs={{0,2},{2,0},{4,6},{6,4},{8,10},{10,8},{12,14},{14,12},{16,18},{18,... | collective-permute-start | bytes 1179656 | tf_op jit(solution)/shard_map/ppermute | solution.py:504
  463.0 16.9 %collective-permute-start.46 = (f32[16,256]{1,0:T(8,128)S(1)}, f32[16,256]{1,0:T(8,128)S(1)}, u32[]{:S(2)}, u32[]{:S(2)}) collective-permute-start(f32[16,256]{1,0:T(8,128)S(1)} %select_maximum_fusion), channel_id=1, source_target_pairs={{0,2},{2,0},{4,6},{6,4},{8,10},{10,8},{12,14},{14,12},{16,18},{18,... | collective-permute-start | bytes 49160 | tf_op jit(solution)/shard_map/ppermute | solution.py:504
  492.6 75.3 %collective-permute-start.51 = (bf16[512,1024]{0,1:T(8,128)(2,1)}, bf16[512,1024]{0,1:T(8,128)(2,1)}, u32[]{:S(2)}, u32[]{:S(2)}) collective-permute-start(bf16[512,1024]{0,1:T(8,128)(2,1)} %pad_maximum_fusion.8), channel_id=1, source_target_pairs={{0,4},{2,6},{4,0},{6,2},{8,12},{10,14},{12,8},{14,10},{16,20},{18,... | collective-permute-start | bytes 3145736 | tf_op jit(solution)/shard_map/ppermute | solution.py:504
  496.3 103.9 %collective-permute-start.33 = (bf16[512,1152]{1,0:T(8,128)(2,1)}, bf16[512,1152]{1,0:T(8,128)(2,1)}, u32[]{:S(2)}, u32[]{:S(2)}) collective-permute-start(bf16[512,1152]{1,0:T(8,128)(2,1)} %slice.497), channel_id=1, source_target_pairs={{0,4},{2,6},{4,0},{6,2},{8,12},{10,14},{12,8},{14,10},{16,20},{18,... | collective-permute-start | bytes 3538952 | tf_op jit(solution)/shard_map/ppermute | solution.py:504
  500.1 47.1 %collective-permute-start.38 = (bf16[256,384]{1,0:T(8,128)(2,1)S(1)}, bf16[256,384]{1,0:T(8,128)(2,1)S(1)}, u32[]{:S(2)}, u32[]{:S(2)}) collective-permute-start(bf16[256,384]{1,0:T(8,128)(2,1)S(1)} %slice.695), channel_id=1, source_target_pairs={{0,4},{2,6},{4,0},{6,2},{8,12},{10,14},{12,8},{14,10},{16,20},{18,... | collective-permute-start | bytes 589832 | tf_op jit(solution)/shard_map/ppermute | solution.py:504
  503.4 59.5 %collective-permute-start.29 = (bf16[512,768]{1,0:T(8,128)(2,1)}, bf16[512,768]{1,0:T(8,128)(2,1)}, u32[]{:S(2)}, u32[]{:S(2)}) collective-permute-start(bf16[512,768]{1,0:T(8,128)(2,1)} %pad_maximum_fusion.14), channel_id=1, source_target_pairs={{0,2},{2,0},{4,6},{6,4},{8,10},{10,8},{12,14},{14,12},{16,18},{18,... | collective-permute-start | bytes 2359304 | tf_op jit(solution)/shard_map/ppermute | solution.py:504
  567.3 37.5 %collective-permute-start.57 = (bf16[128,2048]{1,0:T(8,128)(2,1)S(1)}, bf16[128,2048]{1,0:T(8,128)(2,1)S(1)}, u32[]{:S(2)}, u32[]{:S(2)}) collective-permute-start(bf16[128,2048]{1,0:T(8,128)(2,1)S(1)} %slice.687), channel_id=1, source_target_pairs={{0,16},{2,18},{4,20},{6,22},{8,24},{10,26},{12,28},{14,30},{16,0},... | collective-permute-start | bytes 1572872 | tf_op jit(solution)/shard_map/ppermute | solution.py:504
  569.8 35.3 %collective-permute-start.52 = (bf16[256,1024]{0,1:T(8,128)(2,1)S(1)}, bf16[256,1024]{0,1:T(8,128)(2,1)S(1)}, u32[]{:S(2)}, u32[]{:S(2)}) collective-permute-start(bf16[256,1024]{0,1:T(8,128)(2,1)S(1)} %slice.688), channel_id=1, source_target_pairs={{0,2},{2,0},{4,6},{6,4},{8,10},{10,8},{12,14},{14,12},{16,18},{18,... | collective-permute-start | bytes 1572872 | tf_op jit(solution)/shard_map/ppermute | solution.py:504
  575.6 24.4 %collective-permute-start.31 = (bf16[128,768]{1,0:T(8,128)(2,1)S(1)}, bf16[128,768]{1,0:T(8,128)(2,1)S(1)}, u32[]{:S(2)}, u32[]{:S(2)}) collective-permute-start(bf16[128,768]{1,0:T(8,128)(2,1)S(1)} %slice.696), channel_id=1, source_target_pairs={{0,16},{2,18},{4,20},{6,22},{8,24},{10,26},{12,28},{14,30},{16,0},... | collective-permute-start | bytes 589832 | tf_op jit(solution)/shard_map/ppermute | solution.py:504
  (147 other events, 1477.3 us)

commit v2 on v1

--- a/solution.py
+++ b/solution.py
@@ -3,6 +3,8 @@
 
 import jax
 import jax.numpy as jnp
+import ml_dtypes
+import numpy as np
 from jax import lax
 from jax.experimental import pallas as pl
 from jax.experimental.pallas import tpu as pltpu
@@ -145,9 +147,9 @@
 
 
 def mamba_bwd_kernel(
-    feats_ref, docs_col_ref, docs_ref, x_ref, x_before_ref, bc_ref, bc_before_ref, step_ref, z_ref, scan_ref, states_ref, norm_grad_ref,
+    feats_ref, scale_ref, coefficient_ref, docs_ref, x_ref, x_before_ref, bc_ref, bc_before_ref, step_ref, z_ref, scan_ref, states_ref, norm_grad_ref,
     taps_ref, staps_ref, heads_ref, expand_ref, reduce_ref, gain_ref,
-    dz_ref, grads_ref, sums_ref, ssums_ref, hsums_ref,
+    grads_ref, sums_ref, ssums_ref, hsums_ref,
     xbuf, bcbuf, dxbuf, dbcbuf, dmemory,
 ):
     rows, width = x_ref.shape
@@ -187,10 +189,10 @@
     scan = scan_ref[...]
     gated = scan * z_silu
     norm_grad = norm_grad_ref[...].astype(F32)
-    weighted = norm_grad * feats[:, 9:10]
-    gated_grad = weighted * gain_ref[...] - gated * feats[:, 10:11]
+    weighted = norm_grad * scale_ref[...]
+    gated_grad = weighted * gain_ref[...] - gated * coefficient_ref[...]
     dscan = gated_grad * z_silu
-    dz_ref[...] = (gated_grad * scan * (z_gate * (1.0 + z * (1.0 - z_gate)))).astype(BF)
+    grads_ref[:, 0:width] = (gated_grad * scan * (z_gate * (1.0 + z * (1.0 - z_gate)))).astype(BF)
     sums_ref[6:7, :] += jnp.sum(weighted * gated, axis=0, keepdims=True)
     sums_ref[5:6, :] += jnp.sum(dscan * values, axis=0, keepdims=True)
     held = states_ref[0]
@@ -208,7 +210,7 @@
     leave_terms = left * passed
     carry_terms = jnp.sum(dheld * held.astype(F32), axis=0, keepdims=True) * carry
     gram = mm_nt(key_in, key_out)
-    allowed = (docs_col_ref[...] == docs_ref[...]) & (iota2((rows, rows), 0) <= iota2((rows, rows), 1))
+    allowed = (feats[:, 0:1] == docs_ref[...]) & (iota2((rows, rows), 0) <= iota2((rows, rows), 1))
     bias = jnp.where(allowed, 0.0, MASKED)
     log_rows = log_decay.T
     front = iota2((rows, LANES), 1) < LANES // 2
@@ -252,7 +254,7 @@
     decay_grad = exact_mm(upper, after) + exact_mm(strict, reduced[rows : 2 * rows]) + reduced[3 * rows : 3 * rows + 1]
     dstep = decay_grad * heads_ref[1:2, :] + reduced[2 * rows : 3 * rows]
     draw = dstep * sigmoid(raw)
-    grads_ref[:, width + 2 * states :] = draw.astype(BF)
+    grads_ref[:, 2 * width + 2 * states :] = draw.astype(BF)
     hsums_ref[0:1, :] += jnp.sum(draw, axis=0, keepdims=True)
     hsums_ref[1:2, :] += jnp.sum(decay_grad * step, axis=0, keepdims=True) * heads_ref[1:2, :]
     dvalues = dscaled * step_w + dscan * taps_ref[5:6, :]
@@ -260,8 +262,8 @@
     dboth = jnp.concatenate([dkey_in, dkey_out], axis=1)
     dpre_bc = dboth * (bc_gate * (1.0 + pre_bc * (1.0 - bc_gate)))
     for dpre_now, buffer, dbuffer, taps, totals, lanes in (
-        (dpre, xbuf, dxbuf, taps_ref, sums_ref, slice(0, width)),
-        (dpre_bc, bcbuf, dbcbuf, staps_ref, ssums_ref, slice(width, width + 2 * states)),
+        (dpre, xbuf, dxbuf, taps_ref, sums_ref, slice(width, 2 * width)),
+        (dpre_bc, bcbuf, dbcbuf, staps_ref, ssums_ref, slice(2 * width, 2 * width + 2 * states)),
     ):
         dbuffer[0:rows, :] = dpre_now
         grad = dpre_now * taps[3:4, :]
@@ -277,29 +279,16 @@
 
 
 def expand_matrix(width):
-    head_of = jnp.arange(width, dtype=jnp.int32) // (LANES // 2)
-    one = (jnp.arange(LANES, dtype=jnp.int32)[:, None] == head_of[None, :]).astype(BF)
-    return jnp.concatenate([one, one], axis=0)
-
-
-def token_features(docs, chunk):
-    total = docs.shape[0]
-    doc = docs.astype(F32)
-    back = [jnp.concatenate([jnp.zeros((k,), F32), (docs[k:] == docs[:-k]).astype(F32)]) for k in (1, 2, 3)]
-    ahead = [jnp.concatenate([(docs[k:] == docs[:-k]).astype(F32), jnp.zeros((k,), F32)]) for k in (1, 2, 3)]
-    blocks = docs.reshape(-1, chunk)
-    before = jnp.concatenate([jnp.full((1,), -1, jnp.int32), blocks[:-1, -1]])
-    entered = (blocks == before[:, None]).astype(F32).reshape(total)
-    leaving = (blocks == blocks[:, -1:]).astype(F32).reshape(total)
-    return jnp.stack([doc] + back + [entered, leaving] + ahead, axis=1)
+    one = np.arange(LANES)[:, None] == np.arange(width)[None, :] // (LANES // 2)
+    return np.concatenate([one, one], axis=0).astype(ml_dtypes.bfloat16)
 
 
 def spec(block, index):
     return pl.BlockSpec(block, index)
 
 
-def mamba_forward(feats, doc_row, ssm_in, z, taps, staps, heads, gain, width, states2):
-    total = z.shape[0]
+def mamba_forward(feats, doc_row, ssm_in, taps, staps, heads, gain, width, states2):
+    total = ssm_in.shape[0]
     rows = CHUNK
     count = total // rows
     block = lambda w, place=0: spec((rows, w), lambda i: (i, place))
@@ -309,8 +298,8 @@
         mamba_fwd_kernel,
         grid=(count,),
         in_specs=[
-            block(feats.shape[1]), spec((1, rows), lambda i: (0, i)), block(width), block(states2, width // states2),
-            block(LANES, (width + states2) // LANES), block(width), whole(taps), whole(staps), whole(heads), whole(expand), whole(gain),
+            block(LANES), spec((1, rows), lambda i: (0, i)), block(width, 1), block(states2, 2 * width // states2),
+            block(LANES, (2 * width + states2) // LANES), block(width), whole(taps), whole(staps), whole(heads), whole(expand), whole(gain),
         ],
         out_specs=[block(width), block(width), block(1), spec((1, states2 // 2, width), lambda i: (i, 0, 0))],
         out_shape=[
@@ -325,11 +314,11 @@
         compiler_params=pltpu.CompilerParams(vmem_limit_bytes=32 * 2**20),
         cost_estimate=pl.CostEstimate(flops=20 * 10**9, bytes_accessed=total * width * 20, transcendentals=total * width * 4),
         name="mamba_fwd",
-    )(feats, doc_row, ssm_in, ssm_in, ssm_in, z, taps, staps, heads, expand, gain)
-
-
-def mamba_backward(feats, doc_col, doc_row, ssm_in, z, scan, states, norm_grad, taps, staps, heads, gain, width, states2):
-    total = z.shape[0]
+    )(feats, doc_row, ssm_in, ssm_in, ssm_in, ssm_in, taps, staps, heads, expand, gain)
+
+
+def mamba_backward(feats, doc_row, scale, coefficient, ssm_in, scan, states, norm_grad, taps, staps, heads, gain, width, states2):
+    total = ssm_in.shape[0]
     rows = CHUNK
     count = total // rows
     back = lambda i: count - 1 - i
@@ -337,22 +326,20 @@
     before = lambda w, place=0: spec((8, w), lambda i: (jnp.maximum(back(i) * (rows // 8) - 1, 0), place))
     whole = lambda a: spec(a.shape, lambda i: (0,) * a.ndim)
     expand = expand_matrix(width)
-    reduce = expand[:LANES].T
-    reduce = jnp.concatenate([reduce, reduce], axis=0)
+    reduce = np.concatenate([expand[:LANES].T] * 2, axis=0)
     totals = lambda w: spec((8, w), lambda i: (0, 0))
     return pl.pallas_call(
         mamba_bwd_kernel,
         grid=(count,),
         in_specs=[
-            block(feats.shape[1]), block(1), spec((1, rows), lambda i: (0, back(i))), block(width), before(width),
-            block(states2, width // states2), before(states2, width // states2), block(LANES, (width + states2) // LANES),
+            block(LANES), block(1), block(1), spec((1, rows), lambda i: (0, back(i))), block(width, 1), before(width, 1),
+            block(states2, 2 * width // states2), before(states2, 2 * width // states2), block(LANES, (2 * width + states2) // LANES),
             block(width), block(width), spec((1, states2 // 2, width), lambda i: (back(i), 0, 0)), block(width),
             whole(taps), whole(staps), whole(heads), whole(expand), whole(reduce), whole(gain),
         ],
-        out_specs=[block(width), block(width + states2 + LANES), totals(width), totals(states2), totals(LANES)],
+        out_specs=[block(2 * width + states2 + LANES), totals(width), totals(states2), totals(LANES)],
         out_shape=[
-            jax.ShapeDtypeStruct((total, width), BF),
-            jax.ShapeDtypeStruct((total, width + states2 + LANES), BF),
+            jax.ShapeDtypeStruct((total, 2 * width + states2 + LANES), BF),
             jax.ShapeDtypeStruct((8, width), F32),
             jax.ShapeDtypeStruct((8, states2), F32),
             jax.ShapeDtypeStruct((8, LANES), F32),
@@ -364,7 +351,7 @@
         compiler_params=pltpu.CompilerParams(vmem_limit_bytes=32 * 2**20),
         cost_estimate=pl.CostEstimate(flops=35 * 10**9, bytes_accessed=total * width * 24, transcendentals=total * width * 5),
         name="mamba_bwd",
-    )(feats, doc_col, doc_row, ssm_in, ssm_in, ssm_in, ssm_in, ssm_in, z, scan, states, norm_grad, taps, staps, heads, expand, reduce, gain)
+    )(feats, scale, coefficient, doc_row, ssm_in, ssm_in, ssm_in, ssm_in, ssm_in, ssm_in, scan, states, norm_grad, taps, staps, heads, expand, reduce, gain)
 
 
 QBLOCK = 256
@@ -401,7 +388,7 @@
     lane_of = iota2((block, LANES), 1)
     for start in range(0, total, block):
         rows, end = slice(start, start + block), start + block
-        allowed = (docs_col_ref[rows, :] == docs_ref[:, :end]) & (
+        allowed = (docs_col_ref[rows, 0:1] == docs_ref[:, :end]) & (
             iota2((block, end), 0) + start >= iota2((block, end), 1)
         )
         bias = jnp.where(allowed, 0.0, MASKED)
@@ -432,7 +419,7 @@
     front = iota2((block, LANES), 1) < LANES // 2
     for start in range(0, total, block):
         rows, end = slice(start, start + block), start + block
-        allowed = (docs_col_ref[:end, :] == docs_ref[:, rows]) & (
+        allowed = (docs_col_ref[:end, 0:1] == docs_ref[:, rows]) & (
             iota2((end, block), 0) <= iota2((end, block), 1) + start
         )
         bias = jnp.where(allowed, 0.0, MASKED)
@@ -499,59 +486,214 @@
     )(doc_col, doc_row, qrot, keys, values, lse, up, cos, sin)
 
 
-def swap(values, mask):
-    count = lax.axis_size("fsdp")
-    return lax.ppermute(values, "fsdp", [(i, i ^ mask) for i in range(count)])
-
-
-def high_bits():
-    count = lax.axis_size("fsdp")
-    bits = []
-    while 4 << len(bits) < count:
-        bits.append(4 << len(bits))
-    return bits
-
-
-def block_masks(count):
-    quarter = count // 4
-    places = jnp.arange(count, dtype=jnp.int32)
-    return places // quarter + 4 * (places % quarter)
-
-
-def gather_rows(shard, order):
-    block = shard
-    for bit in high_bits():
-        block = jnp.concatenate([block, swap(block, bit)], axis=0)
-    size = block.shape[0]
-    near = swap(block, 2 if order else 1)
-    far = swap(jnp.concatenate([block, near], axis=0), 1 if order else 2)
-    if order:
-        return jnp.concatenate([block, far[:size], near, far[size:]], axis=0)
-    return jnp.concatenate([block, near, far], axis=0)
-
-
-def scatter_rows(grads, order):
-    size = grads.shape[0] // 4
-    if order:
-        sent = jnp.concatenate([grads[size : 2 * size], grads[3 * size :]], axis=0)
-        kept = jnp.concatenate([grads[:size], grads[2 * size : 3 * size]], axis=0)
-    else:
-        sent, kept = grads[2 * size :], grads[: 2 * size]
-    total = kept.astype(F32) + swap(sent, 1 if order else 2).astype(F32)
-    total = total[:size] + swap(total[size:].astype(BF), 2 if order else 1).astype(F32)
-    for bit in reversed(high_bits()):
-        half = total.shape[0] // 2
-        total = total[:half] + swap(total[half:].astype(BF), bit).astype(F32)
-    return total
-
-
-def sum_everywhere(values, names):
-    if "fsdp" in names:
-        for bit in [1, 2] + high_bits():
-            values = values + swap(values, bit)
-    if "tensor" in names:
-        values = tensor_sum(values)
-    return values
+def flipped(index, mask):
+    bit = 1
+    while bit <= mask:
+        if mask & bit:
+            index = index + bit * (1 - 2 * ((index // bit) % 2))
+        bit *= 2
+    return index
+
+
+def greet(partners):
+    barrier = pltpu.get_barrier_semaphore()
+    for axis, place in partners:
+        pl.semaphore_signal(barrier, inc=1, device_id={axis: place}, device_id_type=pl.DeviceIdType.MESH)
+    pl.semaphore_wait(barrier, len(partners))
+
+
+def remote(source, target, send, recv, axis, place):
+    return pltpu.make_async_remote_copy(
+        src_ref=source, dst_ref=target, send_sem=send, recv_sem=recv,
+        device_id={axis: place}, device_id_type=pl.DeviceIdType.MESH,
+    )
+
+
+def gather_kernel(count, shard_ref, full_ref, own_sem, send_sems, recv_sems):
+    unit, columns = shard_ref.shape
+    levels = count // 4
+    me = lax.axis_index("fsdp")
+    half = columns // 2 // LANES * LANES
+    parts = (slice(0, half), slice(half, columns))
+    neighbours = (flipped(me, 1), flipped(me, 2))
+    far = [flipped(me, 4 * d) for d in range(1, levels)]
+    greet([("fsdp", p) for p in neighbours] + [("fsdp", p) for p in far])
+
+    def rows(owner):
+        return pl.ds(pl.multiple_of(owner * unit, unit), unit)
+
+    started = []
+
+    def send(source, owner, lanes, slot, place):
+        copy = remote(source, full_ref.at[rows(owner), lanes], send_sems.at[slot], recv_sems.at[slot], "fsdp", place)
+        copy.start()
+        started.append(copy)
+        return copy
+
+    def arrival(owner, lanes, slot):
+        piece = full_ref.at[rows(owner), lanes]
+        return remote(piece, piece, send_sems.at[slot], recv_sems.at[slot], "fsdp", neighbours[0])
+
+    everything = slice(0, columns)
+    own = pltpu.make_async_copy(shard_ref, full_ref.at[rows(me), :], own_sem)
+    own.start()
+    for d in range(1, levels):
+        send(shard_ref, me, everything, d, far[d - 1])
+    base = levels
+    for axis in range(2):
+        send(shard_ref, me, everything, base + axis * levels, neighbours[axis])
+    cross = base + 2 * levels
+
+    def pass_on(d):
+        for axis in range(2):
+            owner = flipped(neighbours[axis], 4 * d)
+            arrival(owner, everything, base + axis * levels + d).wait_recv()
+            piece = full_ref.at[rows(owner), parts[axis]]
+            send(piece, owner, parts[axis], cross + axis * levels + d, neighbours[1 - axis])
+
+    for d in range(1, levels):
+        arrival(far[d - 1], everything, d).wait_recv()
+        for axis in range(2):
+            send(full_ref.at[rows(far[d - 1]), :], far[d - 1], everything, base + axis * levels + d, neighbours[axis])
+        pass_on(d - 1)
+    pass_on(levels - 1)
+    for d in range(levels):
+        for axis in range(2):
+            owner = flipped(me, 4 * d + 3)
+            arrival(owner, parts[axis], cross + axis * levels + d).wait_recv()
+    for copy in started:
+        copy.wait_send()
+    own.wait()
+
+
+def gather_weights(shard, count, collective_id):
+    unit, columns = shard.shape
+    slots = 5 * (count // 4)
+    return pl.pallas_call(
+        functools.partial(gather_kernel, count),
+        in_specs=[pl.BlockSpec(memory_space=pl.ANY)],
+        out_specs=pl.BlockSpec(memory_space=pl.ANY),
+        out_shape=jax.ShapeDtypeStruct((count * unit, columns), shard.dtype),
+        scratch_shapes=[pltpu.SemaphoreType.DMA, pltpu.SemaphoreType.DMA((slots,)), pltpu.SemaphoreType.DMA((slots,))],
+        compiler_params=pltpu.CompilerParams(collective_id=collective_id, has_side_effects=True),
+        cost_estimate=pl.CostEstimate(flops=0, bytes_accessed=2 * count * unit * columns * 2, transcendentals=0),
+        name="gather_weights",
+    )(shard)
+
+
+def scatter_kernel(count, tensors, paths, split_rows, *refs):
+    number = len(paths)
+    grads, small_ref = refs[:number], refs[number]
+    outs, small_out = refs[number + 1 : 2 * number + 1], refs[2 * number + 1]
+    scratch = refs[2 * number + 2 :]
+    cross, along_x, along_y, far_in, staged, far_out = (scratch[k * number : (k + 1) * number] for k in range(6))
+    sums, arrived, send_sems, recv_sems, sum_send, sum_recv = scratch[6 * number :]
+    levels = count // 4
+    unit = grads[0].shape[0] // count
+    me = lax.axis_index("fsdp")
+    core = lax.axis_index("tensor")
+    near = (flipped(me, 1), flipped(me, 2))
+    far = [None] + [flipped(me, 4 * d) for d in range(1, levels)]
+    bits = [1 << k for k in range((count - 1).bit_length())]
+    stages = [("fsdp", flipped(me, bit)) for bit in bits]
+    cores = [("tensor", flipped(core, 1 << k)) for k in range((tensors - 1).bit_length())]
+    greet([("fsdp", p) for p in near] + [("fsdp", p) for p in far[1:]] + cores)
+    stages = stages + cores
+    started = []
+
+    def rows(owner):
+        return pl.ds(pl.multiple_of(owner * unit, unit), unit)
+
+    def link(source, target, slot, place):
+        return remote(source, target, send_sems.at[slot], recv_sems.at[slot], "fsdp", place)
+
+    def send(source, target, slot, place):
+        copy = link(source, target, slot, place)
+        copy.start()
+        started.append(copy)
+
+    def slot(i, kind, d):
+        return (i * 4 + kind) * levels + d
+
+    pending = []
+
+    def next_stage():
+        done = len(pending)
+        if done:
+            pending[-1].wait()
+            sums[done] = sums[done - 1] + arrived[done - 1]
+        if done < len(stages):
+            axis, place = stages[done]
+            copy = remote(sums.at[done], arrived.at[done], sum_send.at[done], sum_recv.at[done], axis, place)
+            copy.start()
+            pending.append(copy)
+
+    sums[0] = small_ref[...]
+    next_stage()
+    order = list(range(levels - 1, -1, -1))
+    inbound = lambda path, d: (along_x, along_y)[path]
+    for d in order:
+        for i, path in enumerate(paths):
+            send(grads[i].at[rows(flipped(me, 4 * d + 3)), :], cross[i].at[d], slot(i, 0, d), near[1 - path])
+        for i, path in enumerate(paths):
+            raw = 1 - path
+            target = (along_x, along_y)[raw][i]
+            send(grads[i].at[rows(flipped(near[raw], 4 * d)), :], target.at[d], slot(i, 1 + raw, d), near[raw])
+    for d in order:
+        for i, path in enumerate(paths):
+            link(cross[i].at[d], cross[i].at[d], slot(i, 0, d), near[0]).wait_recv()
+            staged[i][d] = (grads[i][rows(flipped(near[path], 4 * d)), :].astype(F32) + cross[i][d].astype(F32)).astype(BF)
+            target = (along_x, along_y)[path][i]
+            send(staged[i].at[d], target.at[d], slot(i, 1 + path, d), near[path])
+        if d == order[0] or d == 0:
+            next_stage()
+    for d in order:
+        for i, path in enumerate(paths):
+            link(along_x[i].at[d], along_x[i].at[d], slot(i, 1, d), near[0]).wait_recv()
+            link(along_y[i].at[d], along_y[i].at[d], slot(i, 2, d), near[0]).wait_recv()
+            total = grads[i][rows(flipped(me, 4 * d)), :].astype(F32) + along_x[i][d].astype(F32) + along_y[i][d].astype(F32)
+            if d:
+                far_out[i][d - 1] = total.astype(BF)
+                send(far_out[i].at[d - 1], far_in[i].at[d - 1], slot(i, 3, d), far[d])
+            else:
+                outs[i][...] = total
+        if d == order[0] or d == 0:
+            next_stage()
+    while len(pending) < len(stages):
+        next_stage()
+    next_stage()
+    for d in order[:-1]:
+        for i in range(number):
+            link(far_in[i].at[d - 1], far_in[i].at[d - 1], slot(i, 3, d), near[0]).wait_recv()
+            outs[i][...] += far_in[i][d - 1].astype(F32)
+    small_out[:split_rows, :] = sums[len(bits), :split_rows, :]
+    small_out[split_rows:, :] = sums[len(stages), split_rows:, :]
+    for copy in started:
+        copy.wait_send()
+
+
+def scatter_grads(grads, paths, small, split_rows, count, tensors, collective_id):
+    unit = grads[0].shape[0] // count
+    levels = count // 4
+    stages = (count - 1).bit_length() + (tensors - 1).bit_length()
+    vmem = pl.BlockSpec(memory_space=pltpu.VMEM)
+    buffers = []
+    for slots in (levels, levels, levels, levels - 1, levels, levels - 1):
+        buffers += [pltpu.VMEM((slots, unit, g.shape[1]), BF) for g in grads]
+    buffers += [pltpu.VMEM((stages + 1,) + small.shape, F32), pltpu.VMEM((stages,) + small.shape, F32)]
+    links = 4 * levels * len(grads)
+    buffers += [pltpu.SemaphoreType.DMA((links,))] * 2 + [pltpu.SemaphoreType.DMA((stages,))] * 2
+    size = sum(g.shape[1] for g in grads)
+    return pl.pallas_call(
+        functools.partial(scatter_kernel, count, tensors, tuple(paths), split_rows),
+        in_specs=[vmem] * (len(grads) + 1),
+        out_specs=[vmem] * (len(grads) + 1),
+        out_shape=[jax.ShapeDtypeStruct((unit, g.shape[1]), F32) for g in grads] + [jax.ShapeDtypeStruct(small.shape, F32)],
+        scratch_shapes=buffers,
+        compiler_params=pltpu.CompilerParams(collective_id=collective_id, has_side_effects=True, vmem_limit_bytes=48 * 2**20),
+        cost_estimate=pl.CostEstimate(flops=0, bytes_accessed=2 * count * unit * size * 2, transcendentals=0),
+        name="scatter_grads",
+    )(*grads, small)
 
 
 def tensor_swap(values):
@@ -598,12 +740,102 @@
     return lax.rsqrt(jnp.mean(values * values, axis=-1, keepdims=True) + EPS)
 
 
-def rotation_tables(place):
-    half = HEAD_SIZE // 2
-    rates = jnp.exp(jnp.arange(half, dtype=F32) * (-2.0 * math.log(THETA) / HEAD_SIZE))
-    angles = place[:, None] * rates[None, :]
-    cos, sin = jnp.cos(angles), jnp.sin(angles)
-    return jnp.concatenate([cos] * 4, axis=1), jnp.concatenate([-sin, sin, -sin, sin], axis=1)
+def pack_kernel(
+    mixer_ref, state_ref, step_ref, query_ref, keyval_ref, proj_ref, attention_ref, gate_up_ref, down_ref,
+    first_ref, second_ref,
+):
+    unit = state_ref.shape[0]
+    width, wide = mixer_ref.shape[2], -(-mixer_ref.shape[2] // LANES) * LANES
+    same = (iota2((unit, unit), 0) == iota2((unit, unit), 1)).astype(BF)
+    place = 0
+
+    def put(out_ref, value, size):
+        nonlocal place
+        value = value.astype(BF)
+        if size > value.shape[1]:
+            value = jnp.concatenate([value, jnp.zeros((unit, size - value.shape[1]), BF)], axis=1)
+        out_ref[:, place : place + size] = value
+        place += size
+
+    put(first_ref, mixer_ref[:, 0, :], wide)
+    put(first_ref, mixer_ref[:, 1, :], wide)
+    put(first_ref, state_ref[...], state_ref.shape[1])
+    put(first_ref, step_ref[...], LANES)
+    query_wide = -(-query_ref.shape[1] // LANES) * LANES
+    put(first_ref, query_ref[...], query_wide)
+    put(first_ref, keyval_ref[...], keyval_ref.shape[1])
+    put(first_ref, mm_nt(same, proj_ref[...]), wide)
+    put(first_ref, mm_nt(same, attention_ref[...]), query_wide)
+    place = 0
+    put(second_ref, gate_up_ref[:, 0, :], gate_up_ref.shape[2])
+    put(second_ref, gate_up_ref[:, 1, :], gate_up_ref.shape[2])
+    put(second_ref, mm_nt(same, down_ref[...]), down_ref.shape[0])
+
+
+def pack_weights(mixer, state, step, query, keyval, proj, attention, gate_up, down):
+    unit = state.shape[0]
+    lanes = lambda size: -(-size // LANES) * LANES
+    first = 3 * lanes(mixer.shape[2]) + state.shape[1] + LANES + 2 * lanes(query.shape[1]) + keyval.shape[1]
+    second = 2 * gate_up.shape[2] + down.shape[0]
+    return pl.pallas_call(
+        pack_kernel,
+        out_shape=[jax.ShapeDtypeStruct((unit, first), BF), jax.ShapeDtypeStruct((unit, second), BF)],
+        compiler_params=pltpu.CompilerParams(vmem_limit_bytes=32 * 2**20),
+        name="pack_weights",
+    )(mixer, state, step, query, keyval, proj, attention, gate_up, down)
+
+
+def table_kernel(
+    docs_ref, conv_ref, conv_bias_ref, state_conv_ref, state_bias_ref, step_bias_ref, decay_ref, skip_ref,
+    feats_ref, cos_ref, sin_ref, taps_ref, state_taps_ref, heads_ref,
+):
+    total = docs_ref.shape[1]
+    docs = docs_ref[...]
+    tall = jnp.broadcast_to(docs, (LANES, total)).T
+    spot = iota2((1, total), 1)
+    begin = jnp.sum((tall[:, 0:1] < docs).astype(F32), axis=0, keepdims=True)
+    rows = [docs]
+    eight = jnp.broadcast_to(docs, (8, total))
+    for k in (1, 2, 3):
+        rows.append(jnp.where(spot >= k, (pltpu.roll(eight, k, 1)[0:1] == docs).astype(F32), 0.0))
+    blocks = [docs[:, i : i + CHUNK] for i in range(0, total, CHUNK)]
+    before = [jnp.full((1, 1), -1.0, F32)] + [v[:, CHUNK - 1 :] for v in blocks[:-1]]
+    rows.append(jnp.concatenate([(v == w).astype(F32) for v, w in zip(blocks, before)], axis=1))
+    rows.append(jnp.concatenate([(v == v[:, CHUNK - 1 :]).astype(F32) for v in blocks], axis=1))
+    for k in (1, 2, 3):
+        rows.append(jnp.where(spot < total - k, (pltpu.roll(eight, total - k, 1)[0:1] == docs).astype(F32), 0.0))
+    rows.append(spot.astype(F32) - begin)
+    rows.append(jnp.zeros((LANES - len(rows), total), F32))
+    feats = jnp.concatenate(rows, axis=0).T
+    feats_ref[...] = feats
+    lane = iota2((1, LANES), 1)
+    rates = jnp.exp((lane % (HEAD_SIZE // 2)).astype(F32) * (-2.0 * math.log(THETA) / HEAD_SIZE))
+    angles = feats[:, 9:10] * rates
+    cos_ref[...] = jnp.cos(angles)
+    sin_ref[...] = jnp.sin(angles) * jnp.where(lane % HEAD_SIZE < HEAD_SIZE // 2, -1.0, 1.0)
+    width, heads = conv_ref.shape[1], skip_ref.shape[1]
+    taps_ref[...] = jnp.zeros_like(taps_ref)
+    taps_ref[0:4, :width] = conv_ref[...]
+    taps_ref[4:5, :width] = conv_bias_ref[...]
+    spread = (iota2((heads, width), 0) == iota2((heads, width), 1) // (width // heads)).astype(F32)
+    taps_ref[5:6, :width] = exact_mm(jnp.broadcast_to(skip_ref[...], (8, heads)), spread)[0:1]
+    state_taps_ref[...] = jnp.zeros_like(state_taps_ref)
+    state_taps_ref[0:4, :] = state_conv_ref[...]
+    state_taps_ref[4:5, :] = state_bias_ref[...]
+    heads_ref[...] = jnp.zeros_like(heads_ref)
+    heads_ref[0:1, :heads] = step_bias_ref[...]
+    heads_ref[1:2, :heads] = -jnp.exp(decay_ref[...])
+
+
+def make_tables(docs, wide, conv, conv_bias, state_conv, state_bias, step_bias, decay, skip):
+    total = docs.shape[1]
+    shape = lambda r, c: jax.ShapeDtypeStruct((r, c), F32)
+    return pl.pallas_call(
+        table_kernel,
+        out_shape=[shape(total, LANES), shape(total, LANES), shape(total, LANES), shape(8, wide), shape(8, state_conv.shape[1]), shape(8, LANES)],
+        compiler_params=pltpu.CompilerParams(vmem_limit_bytes=32 * 2**20),
+        name="make_tables",
+    )(docs, conv, conv_bias[None], state_conv, state_bias[None], step_bias[None], decay[None], skip[None])
 
 
 def body(
@@ -635,68 +867,44 @@
     own_keyval = own_keyval.reshape(unit, 2, kv_heads, HEAD_SIZE).transpose(0, 2, 1, 3).reshape(unit, 2 * kv_heads * HEAD_SIZE)
     kv_wide = 2 * kv_heads * HEAD_SIZE
     low = lambda v: v.astype(BF)
-    pack = lambda parts: jnp.concatenate([low(v) for v in parts], axis=1)
-    ssm_wide, qkv_wide = wide + states2 + LANES, query_wide + kv_wide
-    first = gather_rows(
-        pack([
-            pad_to(mixer_weight[:, 1, :], wide), state_weight, pad_to(step_weight, LANES),
-            pad_to(query_weight, query_wide), own_keyval,
-        ]),
-        0,
+    first, rest = pack_weights(
+        mixer_weight, state_weight, step_weight, query_weight, own_keyval, mixer_proj, attention_proj, gate_up, down_proj
     )
-    full_ssm, full_qkv = first[:, :ssm_wide], first[:, ssm_wide:]
-    after = gather_rows(
-        pack([pad_to(mixer_weight[:, 0, :], wide), pad_to(mixer_proj.T, wide), pad_to(attention_proj.T, query_wide)]), 1
+    rest = lax.all_gather(rest, "fsdp", axis=0, tiled=True)
+    first = gather_weights(first, fsdp_count, 0)
+    ssm_wide = 2 * wide + states2 + LANES
+    cuts = np.cumsum([0, ssm_wide, query_wide + kv_wide, wide, query_wide])
+    full_ssm, full_qkv, full_proj, full_attention = (first[:, cuts[i] : cuts[i + 1]] for i in range(4))
+    full_gate_up, full_down = rest[:, : 2 * ffn], rest[:, 2 * ffn :]
+
+    tokens = tensor_gather(layer_input).astype(F32)
+    upstream = tensor_gather(cotangent)
+    docs = (doc_ids + jnp.arange(seq_count, dtype=jnp.int32)[:, None] * seq_length).reshape(1, total)
+    doc_row = docs.astype(F32)
+    feats, cos, sin, taps, state_taps, head_rows = make_tables(
+        doc_row, wide, conv_weight, conv_bias, state_conv, state_conv_bias, step_bias, decay_log, skip_gain
     )
-    full_z, full_proj, full_attention = after[:, :wide], after[:, wide : 2 * wide], after[:, 2 * wide :]
-    full_gate_up = gather_rows(low(gate_up).reshape(unit, 2 * ffn), 0)
-    full_down = gather_rows(low(down_proj).T, 1)
-
-    masks = block_masks(fsdp_count)
-    features = jnp.arange(hidden, dtype=jnp.int32)
-    source = (masks[features // unit] ^ fsdp_index) * unit + features % unit
-    turn = (features[:, None] == source[None, :]).astype(BF)
-    turn_back = (source[:, None] == features[None, :]).astype(BF)
-    tokens = tensor_gather(low(plain_dot(layer_input, turn))).astype(F32)
-    upstream = tensor_gather(low(plain_dot(cotangent, turn)))
-    gains = jnp.dot(
-        jnp.stack([input_gain, second_gain]), turn.astype(F32), precision=lax.Precision.HIGHEST, preferred_element_type=F32
-    )
-    first_gain, second_gain_turned = gains[0:1], gains[1:2]
-
-    docs = (doc_ids + jnp.arange(seq_count, dtype=jnp.int32)[:, None] * seq_length).reshape(total)
-    place = (jnp.arange(total, dtype=jnp.int32) - jnp.sum((docs[None, :] < docs[:, None]).astype(jnp.int32), axis=1)).astype(F32)
-    cos, sin = rotation_tables(place)
-    feats = token_features(docs, CHUNK)
-    doc_col, doc_row = docs.astype(F32)[:, None], docs.astype(F32)[None, :]
-    taps = jnp.concatenate(
-        [conv_weight, conv_bias[None], jnp.repeat(skip_gain, width // heads)[None], jnp.zeros((2, width), F32)], axis=0
-    )
-    taps = pad_to(taps, wide)
-    state_taps = jnp.concatenate([state_conv, state_conv_bias[None], jnp.zeros((3, states2), F32)], axis=0)
-    head_rows = pad_to(pad_to(jnp.stack([step_bias, -jnp.exp(decay_log)]), 8, 0), LANES)
     gain_row = pad_to(mixer_gain[None], wide)
 
     first_scale = norm_scale(tokens)
-    normed = low(tokens * first_scale * first_gain)
+    normed = low(tokens * first_scale * input_gain)
     ssm_in = plain_dot(normed, full_ssm)
     qkv_in = plain_dot(normed, full_qkv)
-    gate_z = plain_dot(normed, full_z)
-    scan, gated_low, squares, states = mamba_forward(feats, doc_row, ssm_in, gate_z, taps, state_taps, head_rows, gain_row, wide, states2)
-    attended, log_sums, query_rot, keys, values = attention_forward(kv_heads, doc_col, doc_row, qkv_in, cos, sin, query_wide)
+    scan, gated_low, squares, states = mamba_forward(feats, doc_row, ssm_in, taps, state_taps, head_rows, gain_row, wide, states2)
+    attended, log_sums, query_rot, keys, values = attention_forward(kv_heads, feats, doc_row, qkv_in, cos, sin, query_wide)
     squares = tensor_sum(squares.reshape(-1, LANES)).reshape(total, 1)
     gated_scale = lax.rsqrt(squares / DSSM + EPS)
     branch = gated_scale * right_dot(gated_low, full_proj) + right_dot(attended, full_attention)
     middle = tokens + tensor_sum_low(branch)
     second_scale = norm_scale(middle)
-    second = low(middle * second_scale * second_gain_turned)
+    second = low(middle * second_scale * second_gain)
     gate_vals = plain_dot(second, full_gate_up)
     gate_part, up_part = gate_vals[:, :ffn], gate_vals[:, ffn:]
     gate_sigmoid = jax.nn.sigmoid(gate_part)
     active = low(gate_part * gate_sigmoid * up_part)
     ffn_out = tensor_scatter(low(right_dot(active, full_down)))
     own = lambda v: lax.dynamic_slice_in_dim(v, tensor_index * own_rows, own_rows, 0)
-    layer_output = low(plain_dot(low(own(middle) + ffn_out), turn_back))
+    layer_output = low(own(middle) + ffn_out)
 
     grad_down = low(left_dot(upstream, active))
     active_grad = plain_dot(upstream, full_down)
@@ -705,7 +913,7 @@
     gu_grad = jnp.concatenate([low(gate_grad), low(up_grad)], axis=-1)
     grad_gate_up = low(left_dot(second, gu_grad))
     second_grad = tensor_sum_low(right_dot(gu_grad, full_gate_up))
-    weighted = second_grad * second_gain_turned
+    weighted = second_grad * second_gain
     inner = jnp.mean(weighted * middle, axis=-1, keepdims=True)
     middle_grad = upstream.astype(F32) + second_scale * weighted - middle * second_scale**3 * inner
     second_gain_part = jnp.sum(second_grad * middle * second_scale, axis=0) * (1.0 / tensor_count)
@@ -714,56 +922,48 @@
     norm_grad = low(plain_dot(branch_low, full_proj))
     attended_grad = low(plain_dot(branch_low, full_attention))
     inner_sums = tensor_sum(jnp.sum(norm_grad.astype(F32) * gated_low.astype(F32), axis=-1).reshape(-1, LANES)).reshape(total, 1)
-    back_feats = jnp.concatenate([feats, gated_scale, gated_scale**3 * (inner_sums / DSSM)], axis=1)
     grad_proj = low(left_dot(low(gated_scale * branch_low), gated_low))
     grad_attention = low(left_dot(branch_low, attended))
-    gate_z_grad, ssm_grad, sums, state_sums, head_sums = mamba_backward(
-        back_feats, doc_col, doc_row, ssm_in, gate_z, scan, states, norm_grad, taps, state_taps, head_rows, gain_row, wide, states2
+    ssm_grad, sums, state_sums, head_sums = mamba_backward(
+        feats, doc_row, gated_scale, gated_scale**3 * (inner_sums / DSSM), ssm_in, scan, states, norm_grad, taps, state_taps,
+        head_rows, gain_row, wide, states2,
     )
-    qkv_grad = attention_backward(kv_heads, doc_col, doc_row, query_rot, keys, values, log_sums, attended_grad, cos, sin)
-    grad_z = low(left_dot(normed, gate_z_grad))
+    qkv_grad = attention_backward(kv_heads, feats, doc_row, query_rot, keys, values, log_sums, attended_grad, cos, sin)
     grad_ssm = low(left_dot(normed, ssm_grad))
     grad_qkv = low(left_dot(normed, qkv_grad))
-    normed_part = right_dot(gate_z_grad, full_z) + right_dot(ssm_grad, full_ssm) + right_dot(qkv_grad, full_qkv)
+    normed_part = right_dot(ssm_grad, full_ssm) + right_dot(qkv_grad, full_qkv)
     input_gain_part = jnp.sum(normed_part * tokens * first_scale, axis=0)
     normed_grad = tensor_scatter(low(normed_part))
     own_tokens, own_scale = own(tokens), own(first_scale)
-    weighted = normed_grad * first_gain
+    weighted = normed_grad * input_gain
     inner = jnp.mean(weighted * own_tokens, axis=-1, keepdims=True)
     input_grad = own(middle_grad) + own_scale * weighted - own_tokens * own_scale**3 * inner
-    turned = plain_dot(split_lanes(input_grad, 0), turn_back)
-    input_grad = turned[:own_rows] + turned[own_rows:]
-
-    sum_gate_up = scatter_rows(grad_gate_up, 0).reshape(unit, 2, ffn)
-    sum_down = scatter_rows(grad_down, 1).T
-    sum_out = scatter_rows(jnp.concatenate([grad_proj, grad_attention], axis=1), 0)
-    sum_z = scatter_rows(grad_z, 1)[:, :width]
-    sum_ssm = scatter_rows(grad_ssm, 0)
-    sum_qkv = scatter_rows(grad_qkv, 1)
+
+    rest_sum = lax.psum_scatter(jnp.concatenate([grad_gate_up, grad_down], axis=1), "fsdp", scatter_dimension=0, tiled=True).astype(F32)
+    split_small = jnp.concatenate([sums, head_sums], axis=1).reshape(-1, LANES)
+    shared_small = jnp.concatenate([state_sums.reshape(-1, LANES), second_gain_part.reshape(-1, LANES), input_gain_part.reshape(-1, LANES)], axis=0)
+    split_rows = split_small.shape[0]
+    sum_ssm, sum_qkv, sum_proj, sum_attention, small = scatter_grads(
+        (grad_ssm, grad_qkv, grad_proj, grad_attention), (0, 1, 1, 1), jnp.concatenate([split_small, shared_small], axis=0),
+        split_rows, fsdp_count, tensor_count, 1,
+    )
     keyval_sum = sum_qkv[:, query_wide:].reshape(unit, kv_heads, 2, HEAD_SIZE).transpose(0, 2, 1, 3).reshape(unit, 2, kv_heads * HEAD_SIZE)
     keyval_sum = lax.dynamic_update_slice_in_dim(
         jnp.zeros((unit, 2, KEYVAL_HEADS * HEAD_SIZE), F32), keyval_sum, kv_leading * HEAD_SIZE, 2
     ).reshape(unit, 2 * KEYVAL_HEADS * HEAD_SIZE)
-    shared = tensor_sum(jnp.concatenate([sum_ssm[:, wide : wide + states2], keyval_sum], axis=1))
-
-    def turn_row(row):
-        blocks = (jnp.arange(fsdp_count, dtype=jnp.int32)[:, None] == (masks ^ fsdp_index)[None, :]).astype(F32)
-        return exact_mm(blocks, row.reshape(fsdp_count, unit)).reshape(1, hidden)
-
-    split_sums = sum_everywhere(jnp.concatenate([sums, head_sums], axis=1), ("fsdp",))
+    shared = tensor_sum(jnp.concatenate([sum_ssm[:, 2 * wide : 2 * wide + states2], keyval_sum], axis=1))
+    split_sums = small[:split_rows].reshape(8, wide + LANES)
     sums, head_sums = split_sums[:, :wide], split_sums[:, wide:]
-    state_sums = sum_everywhere(
-        jnp.concatenate([state_sums, pad_to(turn_row(second_gain_part).reshape(-1, states2), 8, 0)], axis=0), ("fsdp", "tensor")
-    )
-    second_gain_sum = state_sums[8 : 8 + hidden // states2].reshape(hidden)
-    input_gain_sum = sum_everywhere(turn_row(input_gain_part).reshape(-1, LANES), ("fsdp", "tensor")).reshape(hidden)
+    gain_rows = hidden // LANES
+    state_sums = small[split_rows : small.shape[0] - 2 * gain_rows].reshape(8, states2)
+    second_gain_sum, input_gain_sum = small[-2 * gain_rows : -gain_rows].reshape(hidden), small[-gain_rows:].reshape(hidden)
     return (
         layer_output,
         input_grad,
         input_gain_sum,
-        jnp.stack([sum_z, sum_ssm[:, :width]], axis=1),
+        jnp.stack([sum_ssm[:, :width], sum_ssm[:, wide : wide + width]], axis=1),
         shared[:, :states2],
-        sum_ssm[:, wide + states2 : wide + states2 + heads],
+        sum_ssm[:, 2 * wide + states2 : 2 * wide + states2 + heads],
         sums[0:4, :width],
         sums[4, :width],
         state_sums[0:4],
@@ -772,13 +972,13 @@
         head_sums[1, :heads],
         jnp.sum(sums[5, :width].reshape(heads, -1), axis=1),
         sums[6, :width],
-        sum_out[:, :width].T,
+        sum_proj[:, :width].T,
         sum_qkv[:, :query_width],
         shared[:, states2:].reshape(unit, 2, KEYVAL_HEADS * HEAD_SIZE),
-        sum_out[:, wide : wide + query_width].T,
+        sum_attention[:, :query_width].T,
         second_gain_sum,
-        sum_gate_up,
-        sum_down,
+        rest_sum[:, : 2 * ffn].reshape(unit, 2, ffn),
+        rest_sum[:, 2 * ffn :].T,
     )
 
 

time: 656 us -> 462 us (0.70)
  waiting for transfers between devices: 267 us -> 0.07 us
  Pallas kernels: 56.2 us -> 255 us
  starting transfers between devices: 59.2 us -> 10.3 us
  other arithmetic: 90.9 us -> 46.3 us
  local copies, waits for them, and re-layouts: 82.5 us -> 49.7 us
  between operations: 3.25 us -> 15.4 us
  matrix products: 87.9 us -> 81.2 us
    ppermute x52 -> x0, waiting for transfers between devices: 266 us -> none  [swap(): return lax.ppermute(values, 'fsdp', [(i, i ^ mask) for i in range(count)])]
    pallas_call x2 -> x6, Pallas kernels: 39.7 us -> 239 us  [the longest x1 99.8 us: scatter_grads(): pl.pallas_call(functools.partial(scatter_kernel, count, tensors, tuple(pa...]
    ppermute x52 -> x0, starting transfers between devices: 57.2 us -> none  [swap(): return lax.ppermute(values, 'fsdp', [(i, i ^ mask) for i in range(count)])]
    concatenate x26 -> x4, other arithmetic: 27.8 us -> 4.78 us  [the longest x1 4.76 us: body(): jnp.concatenate([grad_gate_up, grad_down], axis=1)]
    add x37 -> x0, other arithmetic: 22.9 us -> none  [the longest x6 10.3 us: scatter_rows(): total = kept.astype(F32) + swap(sent, 1 if order else 2).astype(F32)]
    another operation x12 -> x3, local copies, waits for them, and re-layouts: 9.82 us -> 0.21 us  [the longest x1 0.1 us: body(): own_keyval.reshape(unit, 2, kv_heads, HEAD_SIZE).transpose(0, 2, 1, 3)]
    slice x29 -> x5, local copies, waits for them, and re-layouts: 11.1 us -> 1.6 us  [the longest x1 0.99 us: body(): rest_sum[:, :2 * ffn].reshape(unit, 2, ffn)]
    ppermute x11 -> x9, starting transfers between devices: 1.99 us -> 10.1 us  [tensor_swap(): return lax.ppermute(values, 'tensor', [(0, 1), (1, 0)])]
  transfers between devices with their start and end apart: 63 -> 11, of which waited for: 30 -> 0; matrix products, arithmetic and copies ran while one was open for 29% -> 28% of each run, Pallas kernels for 9% -> 55%
where the time goes in v2:
time: 462 us; the launch traced here: 458 us
  Pallas kernels  255 us (55%)
  matrix products  81.2 us (18%)
  local copies, waits for them, and re-layouts  49.7 us (11%)
  other arithmetic  46.3 us (10%)
  between operations  15.4 us (3%)
  starting transfers between devices  10.3 us (2%)
    pallas_call x1, Pallas kernels, scatter_grads(): pl.pallas_call(functools.partial(scatter_kernel, count, tensors, tuple(pa...  99.8 us
    pallas_call x1, Pallas kernels, gather_weights(): pl.pallas_call(functools.partial(gather_kernel, count), in_specs=[pl.Bloc...  93.2 us
    unnamed x165, local copies, waits for them, and re-layouts  38.2 us
    dot_general x6, matrix products, plain_dot(): return jnp.dot(left_side, right_side, preferred_element_type=F32)  30.8 us
    pallas_call x1, Pallas kernels, mamba_backward(): pl.pallas_call(mamba_bwd_kernel, grid=(count,), in_specs=[block(LANES), b...  29.4 us
    dot_general x6, matrix products, right_dot(): lax.dot_general(left_side, right_side, (((1,), (1,)), ((), ())), preferre...  27.9 us
    dot_general x6, matrix products, left_dot(): lax.dot_general(left_side, right_side, (((0,), (0,)), ((), ())), preferre...  22.6 us
    pallas_call x1, Pallas kernels, mamba_forward(): pl.pallas_call(mamba_fwd_kernel, grid=(count,), in_specs=[block(LANES), s...  11.1 us
  transfers between devices with their start and end apart: 11, of which 0 were waited for; matrix products, arithmetic and copies ran while one was open for 28% of the time, Pallas kernels for 55%

profile of v2, /device:TPU:0, one launch (start us, length us, event | category | flops | bytes accessed | tf_op | source)
XLA Modules:
  0.0 458.4 jit_solution(16918895156914891627)
XLA Ops:
  20.1 93.2 %gather_weights.1 = bf16[1024,3328]{1,0:T(8,128)(2,1)} custom-call(bf16[64,3328]{1,0:T(8,128)(2,1)} %copy-done.4), custom_call_target="tpu_custom_call" | custom-call | bytes 13631488 | tf_op jit(solution)/shard_map/gather_weights/pallas_call | solution.py:572
  113.4 2.8 make_tables.1
  116.9 7.5 %fusion.6.x_ref.bc_ref.step_ref.z_ref.x_before_ref.bc_before_ref = f32[1024,1920]{1,0:T(8,128)S(1)} fusion(bf16[1024,3328]{1,0:T(8,128)(2,1)} %gather_weights.1, f32[1024]{0:T(1024)S(1)} %copy-done.65, f32[1024]{0:T(1024)S(1)} %add_rsqrt_fusion.2, bf16[512,1024]{0,1:T(8,128)(2,1)S(1)} %get-tuple-element.153, bf16[512,1024]{0,1:T(8,128)(2,1)S(1)} %get-tuple-element.152), kind=kOutput, calls=%fused_computation.26 | convolution fusion | flops 4033871872 | bytes 13901824 | tf_op jit(solution)/shard_map/dot_general | solution.py:35
  124.4 11.1 %mamba_fwd.1 = (f32[1024,768]{1,0:T(8,128)S(1)}, bf16[1024,768]{1,0:T(8,128)(2,1)S(1)}, f32[1024,1]{1,0:T(8,128)S(1)}, bf16[8,128,768]{2,1,0:T(8,128)(2,1)S(1)}) custom-call(f32[1024,128]{1,0:T(8,128)S(1)} %get-tuple-element.47.feats_ref.docs_col_ref, f32[1,1024]{1,0:T(1,128)S(1)} %convert_element_type.100.docs_ref, ...), custom_call_target="tpu_custom_call" | custom-call | flops 20000000000 | bytes 15728640 | tf_op jit(solution)/shard_map/mamba_fwd/pallas_call | solution.py:297
  138.7 3.2 fusion.17.q_ref.kv_ref
  142.0 7.2 %attention_fwd.1 = (bf16[1024,256]{1,0:T(8,128)(2,1)S(1)}, f32[1024,128]{1,0:T(8,128)S(1)}, bf16[1024,256]{1,0:T(8,128)(2,1)S(1)}, bf16[1024,128]{1,0:T(8,128)(2,1)S(1)}, bf16[1024,128]{1,0:T(8,128)(2,1)S(1)}) custom-call(f32[1024,128]{1,0:T(8,128)S(1)} %get-tuple-element.47.feats_ref.docs_col_ref, f32[1,1024]{1,0:T(1,128)S(1)} %convert_element_type.100.docs_ref, ...), custom_call_target="tpu_custom_call" | custom-call | flops 12000000000 | bytes 2621440 | tf_op jit(solution)/shard_map/attention_fwd/pallas_call | solution.py:461
  151.5 5.9 %fusion.30 = (bf16[1024,1024]{0,1:T(8,128)(2,1)}, f32[1024,1024]{0,1:T(8,128)}) fusion(f32[1024,1024]{0,1:T(8,128)S(1)} %fusion.20, bf16[1024,768]{1,0:T(8,128)(2,1)S(1)} %get-tuple-element.53, bf16[1024,3328]{1,0:T(8,128)(2,1)} %gather_weights.1, f32[1024]{0:T(1024)S(1)} %fusion.45), kind=kOutput, calls=%fused_computation.98 | convolution fusion | flops 1613758464 | bytes 13635584 | tf_op jit(solution)/shard_map/dot_general | solution.py:31
  160.3 4.2 fusion.27
  165.1 2.7 broadcast_select_fusion.3
  169.0 6.7 %multiply_reduce_fusion.3 = (f32[1024]{0:T(1024)S(1)}, f32[1024,1024]{0,1:T(8,128)}) fusion(f32[1024,1024]{0,1:T(8,128)} %get-tuple-element.166, bf16[1024,1024]{0,1:T(8,128)(2,1)} %collective-permute-done.2, bf16[512,1024]{0,1:T(8,128)(2,1)} %copy-done.51, bf16[512,1024]{0,1:T(8,128)(2,1)} %copy-done.48), kind=kLoop, calls=%fused_computation.13 | loop fusion | flops 9436160 | bytes 12587008 | tf_op jit(solution)/shard_map/reduce_sum | solution.py:740
  175.8 8.2 %fusion.2 = f32[1024,2048]{1,0:T(8,128)S(1)} fusion(bf16[1024,3072]{1,0:T(8,128)(2,1)} %all-gather.2.cloned.1.call-done, f32[1024,1024]{0,1:T(8,128)} %get-tuple-element.144, f32[1024]{0:T(1024)S(1)} %copy-done.66, f32[1024]{0:T(1024)S(1)} %get-tuple-element.164), kind=kOutput, calls=%fused_computation.22 | convolution fusion | flops 4298113024 | bytes 16785408 | tf_op jit(solution)/shard_map/dot_general | solution.py:35
  184.0 5.5 %multiply_convert_fusion.2 = (bf16[1024,1024]{1,0:T(8,128)(2,1)}, bf16[1024,1024]{1,0:T(8,128)(2,1)}, bf16[1024,1024]{1,0:T(8,128)(2,1)S(1)}) fusion(f32[1024,2048]{1,0:T(8,128)S(1)} %fusion.2, bf16[1024,3072]{1,0:T(8,128)(2,1)S(1)} %copy-done.71, bf16[512,1024]{0,1:T(8,128)(2,1)S(1)} %copy-done.60, bf16[512,1024]{0,1:T(8,128)(2,1)S(1)} %copy-done.58), kind=kOutput, calls=%fused_computation.9 | convolution fusion | flops 2168455168 | bytes 18874368 | tf_op jit(solution)/shard_map/dot_general | solution.py:35
  193.6 6.4 %fusion.31 = (bf16[1024,1024]{0,1:T(8,128)(2,1)}, f32[1024,1024]{0,1:T(8,128)}) fusion(bf16[1024,3072]{1,0:T(8,128)(2,1)S(1)} %copy-done.71, bf16[1024,1024]{1,0:T(8,128)(2,1)S(1)} %copy-done.75, bf16[1024,1024]{1,0:T(8,128)(2,1)S(1)} %copy-done.74), kind=kOutput, calls=%fused_computation.99 | convolution fusion | flops 4304404480 | bytes 14680064 | tf_op jit(solution)/shard_map/dot_general | solution.py:31
  200.4 4.9 %convolution_convert_fusion = bf16[1024,2048]{1,0:T(8,128)(2,1)S(1)} fusion(bf16[1024,1024]{1,0:T(8,128)(2,1)S(1)} %copy-done.75, bf16[1024,1024]{1,0:T(8,128)(2,1)S(1)} %copy-done.74, f32[1024,1024]{0,1:T(8,128)S(1)} %copy-done.44, f32[1024]{0:T(1024)S(1)} %copy-done.66, f32[1024]{0:T(1024)S(1)} %get-tuple-element.164), kind=kOutput, calls=%fused_computation.18 | convolution fusion | flops 4308598784 | bytes 12591104 | tf_op jit(solution)/shard_map/dot_general | solution.py:27
  205.3 3.7 convolution_convert_fusion.2
  209.0 4.8 %pad_maximum_fusion = bf16[1024,3072]{1,0:T(8,128)(2,1)} fusion(bf16[1024,1024]{1,0:T(8,128)(2,1)} %convolution_convert_fusion.2, bf16[1024,2048]{1,0:T(8,128)(2,1)S(1)} %convolution_convert_fusion), kind=kLoop, calls=%fused_computation | loop fusion | flops 12582912 | bytes 12582912 | tf_op jit(solution)/shard_map/concatenate | solution.py:942
  213.8 4.0 add_convert_fusion
  220.2 5.5 %multiply_reduce_fusion.1 = (f32[1024]{0:T(1024)S(1)}, f32[1024]{0:T(1024)S(1)}) fusion(f32[1024,1024]{0,1:T(8,128)} %get-tuple-element.144, f32[1024]{0:T(1024)S(1)} %get-tuple-element.164, f32[1024,1024]{0,1:T(8,128)} %get-tuple-element.168, bf16[1024,1024]{0,1:T(8,128)(2,1)} %collective-permute-done.5, f32[1024]{0:T(1024)S(1)} %copy-done.66), kind=kLoop, calls=%fused_computation.3 | loop fusion | flops 8386560 | bytes 10502144 | tf_op jit(solution)/shard_map/reduce_sum | solution.py:919
  227.2 5.2 %fusion.28 = (bf16[1024,1024]{0,1:T(8,128)(2,1)S(1)}, f32[1024,1024]{0,1:T(8,128)}) fusion(f32[1024]{0:T(1024)S(1)} %broadcast_multiply_fusion, f32[1024,1024]{0,1:T(8,128)S(1)} %copy-done.45, f32[1024]{0:T(1024)S(1)} %get-tuple-element.163, f32[1024]{0:T(1024)S(1)} %copy-done.66, f32[1024,1024]{0,1:T(8,128)S(1)} %copy-done.54, ...), kind=kLoop, calls=%fused_computation.96 | loop fusion | flops 13631488 | bytes 18890752 | tf_op jit(solution)/shard_map/convert_element_type | solution.py:869
  232.4 4.5 multiply_reduce_fusion.5
  240.8 9.3 %attention_bwd.1 = bf16[1024,384]{1,0:T(8,128)(2,1)S(1)} custom-call(f32[1024,128]{1,0:T(8,128)S(1)} %copy-done.15, f32[1,1024]{1,0:T(1,128)S(1)} %convert_element_type.100.docs_ref, bf16[1024,256]{1,0:T(8,128)(2,1)S(1)} %copy-done.39, bf16[1024,128]{1,0:T(8,128)(2,1)S(1)} %copy-done.41, bf16[1024,128]{1,0:T(8,128)(2,1)S(1)} %copy-done.43, ...), custom_call_target="tpu_custom_call" | custom-call | flops 16000000000 | bytes 2621440 | tf_op jit(solution)/shard_map/attention_bwd/pallas_call | solution.py:479
  251.4 3.0 fusion.13.refs_2_
  258.8 3.3 copy-done.29
  266.9 29.4 %mamba_bwd.1 = (bf16[1024,1920]{1,0:T(8,128)(2,1)S(1)}, f32[8,768]{1,0:T(8,128)S(1)}, f32[8,256]{1,0:T(8,128)S(1)}, f32[8,128]{1,0:T(8,128)S(1)}) custom-call(f32[1024,128]{1,0:T(8,128)S(1)} %copy-done.16, f32[1024,1]{1,0:T(8,128)S(1)} %copy.116.scale_ref, f32[1024,1]{1,0:T(8,128)S(1)} %multiply_multiply_fusion.coefficient_ref, ...), custom_call_target="tpu_custom_call" | custom-call | flops 35000000512 | bytes 18874368 | tf_op jit(solution)/shard_map/mamba_bwd/pallas_call | solution.py:331
  296.3 8.1 %fusion.4 = f32[1024,1024]{0,1:T(8,128)S(1)} fusion(bf16[1024,1920]{1,0:T(8,128)(2,1)S(1)} %get-tuple-element.60, bf16[1024,3328]{1,0:T(8,128)(2,1)} %gather_weights.1), kind=kOutput, calls=%fused_computation.24 | convolution fusion | flops 4026531840 | bytes 12058624 | tf_op jit(solution)/shard_map/dot_general | solution.py:31
  304.5 2.8 multiply_reduce_fusion
  310.1 9.0 %convolution_convert_fusion.1.refs_0_ = bf16[1024,1920]{1,0:T(8,128)(2,1)} fusion(bf16[1024,1920]{1,0:T(8,128)(2,1)} %copy-done.31, f32[1024]{0:T(1024)S(1)} %copy-done.65, f32[1024]{0:T(1024)S(1)} %add_rsqrt_fusion.2, bf16[512,1024]{0,1:T(8,128)(2,1)} %copy-done.51, bf16[512,1024]{0,1:T(8,128)(2,1)S(1)} %copy-done.50), kind=kOutput, calls=%fused_computation.19 | convolution fusion | flops 4035837952 | bytes 9969664 | tf_op jit(solution)/shard_map/dot_general | solution.py:27
  319.2 99.8 %scatter_grads.1 = (f32[64,1920]{1,0:T(8,128)S(1)}, f32[64,384]{1,0:T(8,128)S(1)}, f32[64,768]{1,0:T(8,128)S(1)}, f32[64,256]{1,0:T(8,128)S(1)}, f32[88,128]{1,0:T(8,128)S(1)}) custom-call(bf16[1024,1920]{1,0:T(8,128)(2,1)} %convolution_convert_fusion.1.refs_0_, bf16[1024,384]{1,0:T(8,128)(2,1)S(1)} %convolution_convert_fusion.5.refs_1_, ...), custom_call_target="tpu_custom_call" | custom-call | bytes 13631488 | tf_op jit(solution)/shard_map/scatter_grads/pallas_call | solution.py:687
  422.7 7.6 %collective-permute-start.8 = (f32[64,512]{1,0:T(8,128)S(1)}, f32[64,512]{1,0:T(8,128)S(1)}, u32[]{:S(2)}, u32[]{:S(2)}) collective-permute-start(f32[64,512]{1,0:T(8,128)S(1)} %pad_maximum_fusion.9), channel_id=1, source_target_pairs={{0,1},{1,0},{2,3},{3,2},{4,5},{5,4},{6,7},{7,6},{8,9},{9,8},{10,11... | collective-permute-start | bytes 393224 | tf_op jit(solution)/shard_map/ppermute | solution.py:700
  436.0 2.6 multiply_reduce_fusion.6
  439.1 4.0 multiply_subtract_fusion.1
  443.1 2.9 copy.121
  (248 shorter events, 64.0 us)
Async XLA Ops:
  7.2 11.8 %copy-start.62 = (bf16[512,1024]{1,0:T(8,128)(2,1)S(1)}, bf16[512,1024]{1,0:T(8,128)(2,1)}, u32[]{:S(2)}) copy-start(bf16[512,1024]{1,0:T(8,128)(2,1)} %param.25) | copy-start | bytes 3145732
  7.2 12.9 %copy-start.70 = (s32[1,1024]{1,0:T(1,128)S(1)}, s32[1,1024]{1,0:T(1,128)}, u32[]{:S(2)}) copy-start(s32[1,1024]{1,0:T(1,128)} %param.26) | copy-start | bytes 12292
  7.2 12.9 %copy-start.68 = (f32[768]{0:T(1024)S(1)}, f32[768]{0:T(1024)}, u32[]{:S(2)}) copy-start(f32[768]{0:T(1024)} %param.32) | copy-start | bytes 9220
  7.2 168.5 %all-gather.2.cloned.1.call-start = ((), (), s32[]{:S(2)}) async-start(), calls=%async_computation.1 | async-start | bytes 6684672 | tf_op jit(solution)/shard_map/all_gather | solution.py:873
  18.7 94.6 %copy-start.69 = (f32[768]{0:T(1024)S(1)}, f32[768]{0:T(1024)}, u32[]{:S(2)}) copy-start(f32[768]{0:T(1024)} %param.38) | copy-start | bytes 9220
  18.7 94.6 %copy-start.8 = (f32[4,768]{1,0:T(4,128)S(1)}, f32[4,768]{1,0:T(4,128)}, u32[]{:S(2)}) copy-start(f32[4,768]{1,0:T(4,128)} %conv_ref.1) | copy-start | bytes 36868
  18.7 94.6 %copy-start.9 = (f32[4,256]{1,0:T(4,128)S(1)}, f32[4,256]{1,0:T(4,128)}, u32[]{:S(2)}) copy-start(f32[4,256]{1,0:T(4,128)} %state_conv_ref.1) | copy-start | bytes 12292
  18.8 94.6 %copy-start.10 = (f32[256]{0:T(256)S(1)}, f32[256]{0:T(256)}, u32[]{:S(2)}) copy-start(f32[256]{0:T(256)} %param.34) | copy-start | bytes 3076
  18.8 94.6 %copy-start.11 = (f32[12]{0:T(128)S(1)}, f32[12]{0:T(128)}, u32[]{:S(2)}) copy-start(f32[12]{0:T(128)} %param.35) | copy-start | bytes 148
  18.8 94.6 %copy-start.12 = (f32[12]{0:T(128)S(1)}, f32[12]{0:T(128)}, u32[]{:S(2)}) copy-start(f32[12]{0:T(128)} %param.36) | copy-start | bytes 148
  18.8 94.6 %copy-start.13 = (f32[12]{0:T(128)S(1)}, f32[12]{0:T(128)}, u32[]{:S(2)}) copy-start(f32[12]{0:T(128)} %param.37) | copy-start | bytes 148
  18.8 427.2 %reduce-scatter.2.cloned.1.call-start = ((), (), s32[]{:S(2)}) async-start(), calls=%async_computation.2 | async-start | bytes 6684672 | tf_op jit(solution)/shard_map/reduce_scatter | solution.py:942
  19.6 96.6 %collective-permute-start = (bf16[512,1024]{0,1:T(8,128)(2,1)S(1)}, bf16[512,1024]{0,1:T(8,128)(2,1)S(1)}, u32[]{:S(2)}, u32[]{:S(2)}) collective-permute-start(bf16[512,1024]{0,1:T(8,128)(2,1)S(1)} %copy.98), channel_id=1, source_target_pairs={{0,1},{1,0},{2,3},{3,2},{4,5},{5,4},{6,7},{7,6},{8,9},{9,8},{10,11... | collective-permute-start | bytes 3145736 | tf_op jit(solution)/shard_map/ppermute | solution.py:700
  116.2 25.8 %copy-start.14 = (f32[1024,128]{1,0:T(8,128)}, f32[1024,128]{1,0:T(8,128)S(1)}, u32[]{:S(2)}) copy-start(f32[1024,128]{1,0:T(8,128)S(1)} %get-tuple-element.47.feats_ref.docs_col_ref) | copy-start | bytes 1572868
  124.4 11.1 %copy-start.28 = (f32[1024,1920]{1,0:T(8,128)}, f32[1024,1920]{1,0:T(8,128)S(1)}, u32[]{:S(2)}) copy-start(f32[1024,1920]{1,0:T(8,128)S(1)} %fusion.6.x_ref.bc_ref.step_ref.z_ref.x_before_ref.bc_before_ref) | copy-start | bytes 23592964
  138.6 12.9 %collective-permute-start.1 = (f32[8,128]{1,0:T(8,128)S(1)}, f32[8,128]{1,0:T(8,128)S(1)}, u32[]{:S(2)}, u32[]{:S(2)}) collective-permute-start(f32[8,128]{1,0:T(8,128)S(1)} %bitcast.66), channel_id=1, source_target_pairs={{0,1},{1,0},{2,3},{3,2},{4,5},{5,4},{6,7},{7,6},{8,9},{9,8},{10,11... | collective-permute-start | bytes 12296 | tf_op jit(solution)/shard_map/ppermute | solution.py:700
  157.4 11.6 %collective-permute-start.2 = (bf16[1024,1024]{0,1:T(8,128)(2,1)}, bf16[1024,1024]{0,1:T(8,128)(2,1)}, u32[]{:S(2)}, u32[]{:S(2)}) collective-permute-start(bf16[1024,1024]{0,1:T(8,128)(2,1)} %get-tuple-element.165), channel_id=1, source_target_pairs={{0,1},{1,0},{2,3},{3,2},{4,5},{5,4},{6,7},{7,6},{8,9},{9,8},{10,11... | collective-permute-start | bytes 6291464 | tf_op jit(solution)/shard_map/ppermute | solution.py:700
  160.1 5.0 %collective-permute-start.4 = (bf16[512,1024]{0,1:T(8,128)(2,1)}, bf16[512,1024]{0,1:T(8,128)(2,1)}, u32[]{:S(2)}, u32[]{:S(2)}) collective-permute-start(bf16[512,1024]{0,1:T(8,128)(2,1)} %copy.106), channel_id=1, source_target_pairs={{0,1},{1,0},{2,3},{3,2},{4,5},{5,4},{6,7},{7,6},{8,9},{9,8},{10,11... | collective-permute-start | bytes 3145736 | tf_op jit(solution)/shard_map/ppermute | solution.py:700
  175.8 8.2 %copy-start.58 = (bf16[512,1024]{0,1:T(8,128)(2,1)S(1)}, bf16[512,1024]{0,1:T(8,128)(2,1)}, u32[]{:S(2)}) copy-start(bf16[512,1024]{0,1:T(8,128)(2,1)} %get-tuple-element.150) | copy-start | bytes 3145732
  175.8 8.2 %copy-start.60 = (bf16[512,1024]{0,1:T(8,128)(2,1)S(1)}, bf16[512,1024]{0,1:T(8,128)(2,1)}, u32[]{:S(2)}) copy-start(bf16[512,1024]{0,1:T(8,128)(2,1)} %get-tuple-element.151) | copy-start | bytes 3145732
  193.2 20.7 %collective-permute-start.3 = (bf16[512,1024]{0,1:T(8,128)(2,1)}, bf16[512,1024]{0,1:T(8,128)(2,1)}, u32[]{:S(2)}, u32[]{:S(2)}) collective-permute-start(bf16[512,1024]{0,1:T(8,128)(2,1)} %broadcast_select_fusion.4), channel_id=1, source_target_pairs={{0,1},{1,0},{2,3},{3,2},{4,5},{5,4},{6,7},{7,6},{8,9},{9,8},{10,11... | collective-permute-start | bytes 3145736 | tf_op jit(solution)/shard_map/ppermute | solution.py:700
  200.0 20.1 %collective-permute-start.5 = (bf16[1024,1024]{0,1:T(8,128)(2,1)}, bf16[1024,1024]{0,1:T(8,128)(2,1)}, u32[]{:S(2)}, u32[]{:S(2)}) collective-permute-start(bf16[1024,1024]{0,1:T(8,128)(2,1)} %get-tuple-element.167), channel_id=1, source_target_pairs={{0,1},{1,0},{2,3},{3,2},{4,5},{5,4},{6,7},{7,6},{8,9},{9,8},{10,11... | collective-permute-start | bytes 6291464 | tf_op jit(solution)/shard_map/ppermute | solution.py:700
  236.9 17.5 %collective-permute-start.6 = (f32[8,128]{1,0:T(8,128)S(1)}, f32[8,128]{1,0:T(8,128)S(1)}, u32[]{:S(2)}, u32[]{:S(2)}) collective-permute-start(f32[8,128]{1,0:T(8,128)S(1)} %bitcast.70), channel_id=1, source_target_pairs={{0,1},{1,0},{2,3},{3,2},{4,5},{5,4},{6,7},{7,6},{8,9},{9,8},{10,11... | collective-permute-start | bytes 12296 | tf_op jit(solution)/shard_map/ppermute | solution.py:700
  240.8 9.3 %copy-start.49 = (bf16[512,1024]{0,1:T(8,128)(2,1)S(1)}, bf16[512,1024]{0,1:T(8,128)(2,1)}, u32[]{:S(2)}) copy-start(bf16[512,1024]{0,1:T(8,128)(2,1)} %copy-done.48) | copy-start | bytes 3145732
  240.8 9.3 %copy-start.52 = (bf16[512,1024]{0,1:T(8,128)(2,1)S(1)}, bf16[512,1024]{0,1:T(8,128)(2,1)}, u32[]{:S(2)}) copy-start(bf16[512,1024]{0,1:T(8,128)(2,1)} %copy-done.51) | copy-start | bytes 3145732
  309.7 126.2 %collective-permute-start.7 = (bf16[512,1024]{0,1:T(8,128)(2,1)}, bf16[512,1024]{0,1:T(8,128)(2,1)}, u32[]{:S(2)}, u32[]{:S(2)}) collective-permute-start(bf16[512,1024]{0,1:T(8,128)(2,1)} %broadcast_select_fusion), channel_id=1, source_target_pairs={{0,1},{1,0},{2,3},{3,2},{4,5},{5,4},{6,7},{7,6},{8,9},{9,8},{10,11... | collective-permute-start | bytes 3145736 | tf_op jit(solution)/shard_map/ppermute | solution.py:700
  310.1 9.1 %copy-start.2 = (bf16[1024,768]{1,0:T(8,128)(2,1)S(1)}, bf16[1024,768]{1,0:T(8,128)(2,1)}, u32[]{:S(2)}) copy-start(bf16[1024,768]{1,0:T(8,128)(2,1)} %fusion.13.refs_2_) | copy-start | bytes 4718596
  419.0 17.0 %copy-start.47 = (bf16[1024,1024]{0,1:T(8,128)(2,1)S(1)}, bf16[1024,1024]{0,1:T(8,128)(2,1)}, u32[]{:S(2)}) copy-start(bf16[1024,1024]{0,1:T(8,128)(2,1)} %copy-done.46) | copy-start | bytes 6291460
  420.4 18.3 %copy-start.64 = (f32[512]{0:T(512)S(1)}, f32[512]{0:T(512)}, u32[]{:S(2)}) copy-start(f32[512]{0:T(512)} %copy-done.63) | copy-start | bytes 6148
  420.4 18.2 %copy-start.67 = (f32[512,1]{0,1:T(1,128)S(1)}, f32[512,1]{0,1:T(1,128)}, u32[]{:S(2)}) copy-start(f32[512,1]{0,1:T(1,128)} %multiply_multiply_fusion.2) | copy-start | bytes 6148
  422.7 11.9 %collective-permute-start.8 = (f32[64,512]{1,0:T(8,128)S(1)}, f32[64,512]{1,0:T(8,128)S(1)}, u32[]{:S(2)}, u32[]{:S(2)}) collective-permute-start(f32[64,512]{1,0:T(8,128)S(1)} %pad_maximum_fusion.9), channel_id=1, source_target_pairs={{0,1},{1,0},{2,3},{3,2},{4,5},{5,4},{6,7},{7,6},{8,9},{9,8},{10,11... | collective-permute-start | bytes 393224 | tf_op jit(solution)/shard_map/ppermute | solution.py:700
  439.1 12.2 %copy-start.1 = (f32[64,2,128]{2,1,0:T(2,128)S(1)}, f32[64,2,128]{2,1,0:T(2,128)}, u32[]{:S(2)}) copy-start(f32[64,2,128]{2,1,0:T(2,128)} %param.41) | copy-start | bytes 196612
  (55 other events, 205.2 us)
Sparse Core Ops, SparseCore 0:
  18.8 130.2 all-gather.1
  213.9 148.6 reduce-scatter.1
